TPU v7x, 32 devices: a whole 2x2x4 slice. The times are simulated.
32 devices in a mesh: row: 8 (over z, x), col: 4 (over y, core).
Axes of the slice: x: 2, y: 2, z: 4, core: 2. Of those that a mesh axis runs over, the one named last changes fastest.
Arguments:
- schur: float32 [2, 8192, 4096], P(None, 'row', 'col'), may hold values from -6 to 6
- lower: bfloat16 [2, 8192, 2048], P(None, 'row', 'col'), may hold values from -6 to 6
- upper: bfloat16 [2, 2048, 4096], P(None, 'row', 'col'), may hold values from -0.1875 to 0.1875
- tile_mask: int32 [2, 64, 16], P(None, 'row', 'col'), may hold values from 0 to 1, as said below
- row_map: int32 [2, 8192], P(None, 'row'), may hold values from 0 to 8191, as said below
- front: float32 [8192, 4096], P('row', 'col'), may hold values from -6 to 6
Outputs:
- front_out: float32 [8192, 4096], P('row', 'col')
Inputs may be any that keep to these rules, and one draw needn't show every extreme that they name: `tile_mask`: in every row of tiles of each child, each aligned pair of tile columns (2 j, 2 j + 1) holds exactly one 1. `row_map`: for each child a permutation of the 8192 rows. Of the 1024 rows of any aligned block, at least 64 and at most 192 map into any one aligned block of 1024 parent rows; some pair of blocks reaches 192.
All inputs are finite; a program needn't handle non-finite values.
Results may differ from a plain program's by a relative error of at most 0.0003.
Values may be sent and summed in bfloat16 or wider, within the bound.
No kernel may reach another device: no remote copies, remote signals or barrier semaphores. Data moves between devices by JAX's collectives and lax.ppermute only.
A program may use at most 128 MiB of HBM per device.

v0:
```python
import jax
import jax.numpy as jnp
from jax import lax
from jax.sharding import PartitionSpec as P

TILE = 128


def build_send(contrib, maps, count):
    children, rows, width = contrib.shape
    cap = 3 * rows // (2 * count)
    target = maps // rows
    place = maps % rows
    onehot = (target[:, :, None] == jnp.arange(count, dtype=jnp.int32)[None, None, :]).astype(
        jnp.int32
    )
    ranks = jnp.cumsum(onehot, axis=1) - 1
    slot = jnp.sum(ranks * onehot, axis=2)
    flat = target * cap + slot
    child_ids = jnp.arange(children, dtype=jnp.int32)[:, None]
    values = jnp.zeros((children, count * cap, width), jnp.float32).at[child_ids, flat].set(contrib)
    places = (
        jnp.full((children, count * cap), float(rows), jnp.float32)
        .at[child_ids, flat]
        .set(place.astype(jnp.float32))
    )
    return (values.reshape(children, count, cap, width), places.reshape(children, count, cap))


def assemble(result, values, places):
    width = values.shape[-1]
    index = places.reshape(-1).astype(jnp.int32)
    return result.at[index].add(values.reshape(-1, width), mode="drop")


def shards(schur, lower, upper, tile_mask, row_map, front):
    children, rows, local_depth = lower.shape
    row_tiles = rows // TILE
    local_tiles = local_depth // TILE
    upper_full = lax.all_gather(upper, "row", axis=1, tiled=True)
    tile_weight = tile_mask.reshape(children, row_tiles, 1, local_tiles, 1).astype(jnp.bfloat16)
    masked = (lower.reshape(children, row_tiles, TILE, local_tiles, TILE) * tile_weight).reshape(
        children, rows, local_depth
    )
    update = jnp.einsum(
        "cmk,ckw->cmw",
        lax.all_gather(masked, "col", axis=2, tiled=True),
        upper_full,
        preferred_element_type=jnp.float32,
    )
    contrib = schur - update
    count = lax.axis_size("row")
    result = front
    for child in range(2):
        values, places = build_send(contrib[child : child + 1], row_map[child : child + 1], count)
        got_values, got_places = (
            lax.all_to_all(values, "row", split_axis=1, concat_axis=1, tiled=True),
            lax.all_to_all(places, "row", split_axis=1, concat_axis=1, tiled=True),
        )
        result = assemble(result, got_values, got_places)
    return result


def solution(mesh):
    in_specs = (
        P(None, "row", "col"),
        P(None, "row", "col"),
        P(None, "row", "col"),
        P(None, "row", "col"),
        P(None, "row"),
        P("row", "col"),
    )
    out_specs = P("row", "col")
    return jax.shard_map(shards, mesh=mesh, in_specs=in_specs, out_specs=out_specs, check_vma=False)
```

profile of v0, /device:TPU:0, one launch (start us, length us, event | category | flops | bytes accessed | tf_op | source)
XLA Modules:
  0.0 544.4 jit_solution(5980956793966110580)
XLA Ops:
  6.5 0.0 copy-start.1
  6.5 0.0 all-gather.3.cloned.1.call-start
  6.5 4.8 copy.25
  11.3 0.0 copy-done.1
  11.3 0.1 copy.14
  11.5 2.0 mul.25
  13.4 0.0 copy-start
  13.4 0.0 copy-start.2
  13.4 0.0 copy-start.3
  13.4 2.8 mul.26
  16.2 3.5 mul.27
  19.7 0.0 all-gather.3.cloned.1.call-update
  19.8 0.0 all-gather.5.cloned.1.call-start
  19.8 0.7 all-gather.5.cloned.1.call-update
  20.5 0.0 copy-done
  20.7 2.3 reduce-window.16
  23.0 0.3 slice_reduce_fusion
  23.2 0.2 reduce-window.19
  23.4 0.1 copy.15
  23.5 2.3 reduce-window.14
  25.8 0.3 slice_reduce_fusion.1
  26.1 0.2 reduce-window.15
  26.2 0.1 copy.13
  26.3 0.1 fusion.4
  26.4 0.1 fusion.6
  26.5 0.0 copy-done.2
  26.5 0.1 fusion.9
  26.6 0.0 copy-done.3
  26.6 0.1 and_reduce_fusion
  26.8 4.3 scatter_custom_fusion.2
  31.1 0.7 reshape.287
  31.8 7.3 %all-to-all-start = ((f32[1,8,192]{2,0,1:T(1,128)}), f32[1,8,192]{2,0,1:T(1,128)S(1)}, u32[]{:S(2)}, u32[]{:S(2)}) async-start(f32[1,8,192]{2,0,1:T(1,128)} %reshape.287), calls=%async_computation | async-start | bytes 16384 | tf_op jit(solution)/shard_map/all_to_all | solution.py:58
  39.0 4.3 scatter_custom_fusion.4
  43.3 0.7 reshape.295
  44.0 1.5 all-to-all-done
  45.5 4.5 all-to-all-start.2
  50.0 30.9 %all-gather.3.cloned.1.call-done = bf16[2,1024,2048]{2,1,0:T(8,128)(2,1)} async-done(((bf16[2,1024,512]{2,1,0:T(8,128)(2,1)}), bf16[2,1024,2048]{2,1,0:T(8,128)(2,1)}) %all-gather.3.cloned.1.call-update) | async-done | bytes 8388624 | tf_op jit(solution)/shard_map/all_gather | solution.py:47
  80.9 127.2 %all-gather.5.cloned.1.call-done = bf16[2,2048,1024]{2,1,0:T(8,128)(2,1)} async-done(((bf16[2,256,1024]{2,1,0:T(8,128)(2,1)}), bf16[2,2048,1024]{2,1,0:T(8,128)(2,1)}) %all-gather.5.cloned.1.call-update) | async-done | bytes 8388624 | tf_op jit(solution)/shard_map/all_gather | solution.py:40
  208.1 16.8 %convolution_subtract_fusion = f32[2,1024,1024]{2,1,0:T(8,128)} fusion(f32[2,1024,1024]{2,1,0:T(8,128)} %param.6, bf16[2,1024,2048]{2,1,0:T(8,128)(2,1)} %all-gather.3.cloned.1.call-done, bf16[2,2048,1024]{2,1,0:T(8,128)(2,1)} %all-gather.5.cloned.1.call-done), kind=kOutput, calls=%fused_computation.10 | convolution fusion | flops 8592031744 | bytes 33554432 | tf_op jit(solution)/shard_map/cmk,ckw->cmw/dot_general | solution.py:45
  224.9 9.1 %scatter_custom_fusion.3 = f32[1536,1024]{1,0:T(8,128)} fusion(s32[1024]{0:T(1024)S(1)} %get-tuple-element.15, f32[2,1024,1024]{2,1,0:T(8,128)} %convolution_subtract_fusion, f32[]{:T(128)} %constant.61.clone.1), kind=kCustom, calls=%fused_computation.9 | custom fusion | bytes 10486272
  234.0 0.0 all-to-all-done.2
  234.0 4.7 all-to-all-start.1
  238.8 9.2 %scatter_custom_fusion.5 = f32[1536,1024]{1,0:T(8,128)} fusion(s32[1024]{0:T(1024)S(1)} %get-tuple-element.14, f32[2,1024,1024]{2,1,0:T(8,128)} %convolution_subtract_fusion, f32[]{:T(128)} %constant.61.clone.1), kind=kCustom, calls=%fused_computation.7 | custom fusion | bytes 10486272
  248.0 128.8 %all-to-all-done.1 = f32[1,8,192,1024]{3,2,0,1:T(8,128)} async-done(((f32[1,8,192,1024]{3,2,0,1:T(8,128)}), f32[1,8,192,1024]{3,2,0,1:T(8,128)}, u32[]{:S(2)}, u32[]{:S(2)}) %all-to-all-start.1) | async-done | bytes 6291488 | tf_op jit(solution)/shard_map/all_to_all | solution.py:57
  376.8 4.8 all-to-all-start.3
  381.6 0.1 convert_element_type.56
  381.7 0.1 convert_element_type.60
  381.8 18.8 %scatter_fusion = f32[1024,1024]{1,0:T(8,128)} fusion(f32[1024,1024]{1,0:T(8,128)} %copy.25, s32[1536]{0:T(1024)S(1)} %fusion.10, f32[1536,1024]{1,0:T(8,128)} %bitcast.10), kind=kCustom, calls=%fused_computation | custom fusion | flops 1572864 | bytes 18880512 | tf_op jit(solution)/shard_map/scatter-add | solution.py:33
  400.6 118.2 %all-to-all-done.3 = f32[1,8,192,1024]{3,2,0,1:T(8,128)} async-done(((f32[1,8,192,1024]{3,2,0,1:T(8,128)}), f32[1,8,192,1024]{3,2,0,1:T(8,128)}, u32[]{:S(2)}, u32[]{:S(2)}) %all-to-all-start.3) | async-done | bytes 6291488 | tf_op jit(solution)/shard_map/all_to_all | solution.py:57
  518.8 18.8 %scatter_fusion.1 = f32[1024,1024]{1,0:T(8,128)} fusion(f32[1024,1024]{1,0:T(8,128)} %scatter_fusion, s32[1536]{0:T(1024)S(1)} %fusion.11, f32[1536,1024]{1,0:T(8,128)} %bitcast.21), kind=kCustom, calls=%fused_computation.1 | custom fusion | flops 1572864 | bytes 18880512 | tf_op jit(solution)/shard_map/scatter-add | solution.py:33
  (19 shorter events, 0.3 us)
Async XLA Ops:
  6.5 4.8 copy-start.1
  6.5 74.4 %all-gather.3.cloned.1.call-start = ((), (), s32[]{:S(2)}) async-start(), calls=%async_computation.4 | async-start | bytes 10485760 | tf_op jit(solution)/shard_map/all_gather | solution.py:47
  13.4 7.1 %copy-start = (s32[2,1024]{1,0:T(2,128)S(1)}, s32[2,1024]{1,0:T(2,128)}, u32[]{:S(2)}) copy-start(s32[2,1024]{1,0:T(2,128)} %param.10) | copy-start | bytes 24580
  13.4 13.1 %copy-start.2 = (s32[2]{0:T(128)S(1)}, s32[2]{0:T(128)}, u32[]{:S(2)}) copy-start(s32[2]{0:T(128)} %constant.66) | copy-start | bytes 28
  13.4 13.2 %copy-start.3 = (s32[2]{0:T(128)S(1)}, s32[2]{0:T(128)}, u32[]{:S(2)}) copy-start(s32[2]{0:T(128)} %constant.69) | copy-start | bytes 28
  19.8 188.3 %all-gather.5.cloned.1.call-start = ((), (), s32[]{:S(2)}) async-start(), calls=%async_computation.5 | async-start | bytes 9437184 | tf_op jit(solution)/shard_map/all_gather | solution.py:40
  31.8 13.8 %all-to-all-start = ((f32[1,8,192]{2,0,1:T(1,128)}), f32[1,8,192]{2,0,1:T(1,128)S(1)}, u32[]{:S(2)}, u32[]{:S(2)}) async-start(f32[1,8,192]{2,0,1:T(1,128)} %reshape.287), calls=%async_computation | async-start | bytes 16384 | tf_op jit(solution)/shard_map/all_to_all | solution.py:58
  45.5 188.5 %all-to-all-start.2 = ((f32[1,8,192]{2,0,1:T(1,128)}), f32[1,8,192]{2,0,1:T(1,128)S(1)}, u32[]{:S(2)}, u32[]{:S(2)}) async-start(f32[1,8,192]{2,0,1:T(1,128)} %reshape.295), calls=%async_computation.2 | async-start | bytes 16384 | tf_op jit(solution)/shard_map/all_to_all | solution.py:58
  234.0 142.7 %all-to-all-start.1 = ((f32[1,8,192,1024]{3,2,0,1:T(8,128)}), f32[1,8,192,1024]{3,2,0,1:T(8,128)}, u32[]{:S(2)}, u32[]{:S(2)}) async-start(f32[1,8,192,1024]{3,2,0,1:T(8,128)} %bitcast.69), calls=%async_computation.1 | async-start | bytes 12582912 | tf_op jit(solution)/shard_map/all_to_all | solution.py:57
  376.8 142.0 %all-to-all-start.3 = ((f32[1,8,192,1024]{3,2,0,1:T(8,128)}), f32[1,8,192,1024]{3,2,0,1:T(8,128)}, u32[]{:S(2)}, u32[]{:S(2)}) async-start(f32[1,8,192,1024]{3,2,0,1:T(8,128)} %bitcast.68), calls=%async_computation.3 | async-start | bytes 12582912 | tf_op jit(solution)/shard_map/all_to_all | solution.py:57
Sparse Core Ops, SparseCore 0:
  19.9 60.9 all-gather.2
  83.1 124.9 all-gather.4
where the time goes:
time: 545 us; the launch traced here: 544 us
  waiting for transfers between devices  407 us (75%)
  other arithmetic  46.6 us (9%)
  local copies, waits for them, and re-layouts  38.9 us (7%)
  starting transfers between devices  21.3 us (4%)
  matrix products  16.8 us (3%)
  between operations  13.6 us (2%)
    all_to_all x2, waiting for transfers between devices, shards(): lax.all_to_all(values, 'row', split_axis=1, concat_axis=1, tiled=True)  247 us
    all_gather x1, waiting for transfers between devices, shards(): upper_full = lax.all_gather(upper, 'row', axis=1, tiled=True)  127 us
    scatter-add x2, other arithmetic, assemble(): return result.at[index].add(values.reshape(-1, width), mode='drop')  37.6 us
    unnamed x15, local copies, waits for them, and re-layouts  31.7 us
    all_gather x1, waiting for transfers between devices, shards(): lax.all_gather(masked, 'col', axis=2, tiled=True)  30.9 us
    dot_general x1, matrix products, shards(): jnp.einsum('cmk,ckw->cmw', lax.all_gather(masked, 'col', axis=2, tiled=Tr...  16.8 us
    all_to_all x2, starting transfers between devices, shards(): lax.all_to_all(places, 'row', split_axis=1, concat_axis=1, tiled=True)  11.7 us
  transfers between devices with their start and end apart: 6, of which 5 were waited for; matrix products, arithmetic and copies ran while one was open for 13% of the time, Pallas kernels for 0%

commit v1 on v0

v1 whole, which is shorter than its diff:
```python
import jax
import jax.numpy as jnp
from jax import lax
from jax.sharding import PartitionSpec as P

TILE = 128
SCALE = 8192.0


def inner_factor(count):
    inner = 1
    while (2 * inner) * (2 * inner) <= count:
        inner *= 2
    return inner


def gather_rows(block, count):
    inner = inner_factor(count)
    outer = count // inner

    def send(x, pairs):
        return lax.ppermute(x, "row", pairs)

    def along(step, first, last):
        return [
            (z * inner + x, (z + step) * inner + x) for z in range(first, last) for x in range(inner)
        ]

    def across(step, first, last):
        return [
            (z * inner + x, z * inner + (x + step) % inner)
            for z in range(first, last)
            for x in range(inner)
        ]

    here = lax.axis_index("row") // inner
    up, down = block, block
    ups, downs = {}, {}
    for k in range(1, outer):
        up = send(up, along(1, k - 1, outer - 1))
        down = send(down, along(-1, 1, outer - k + 1))
        ups[k] = [up] + [send(up, across(j, k, outer)) for j in range(1, inner)]
        downs[k] = [down] + [send(down, across(j, 0, outer - k)) for j in range(1, inner)]
    found = [(0, j, block if j == 0 else send(block, across(j, 0, outer))) for j in range(inner)]
    for k in range(1, outer):
        for j in range(inner):
            found.append((k, j, jnp.where(here >= k, ups[k][j], downs[outer - k][j])))
    return found, inner, outer


def shards(schur, lower, upper, tile_mask, row_map, front):
    children, rows, local_depth = lower.shape
    width = schur.shape[-1]
    count = lax.axis_size("row")
    cap = 3 * rows // (2 * count)
    slots = count * cap
    row_tiles = rows // TILE
    pairs = local_depth // (2 * TILE)
    codes = 2**pairs

    blocks, inner, outer = gather_rows(upper, count)

    target = row_map // rows
    place = row_map % rows
    before = jnp.tril(jnp.ones((rows, rows), jnp.bool_), -1)
    rank = jnp.sum((target[:, :, None] == target[:, None, :]) & before[None], axis=2, dtype=jnp.int32)
    slot = target * cap + rank
    picks = tile_mask.reshape(children, row_tiles, pairs, 2)[..., 1]
    code = jnp.sum(picks * (2 ** jnp.arange(pairs, dtype=jnp.int32)), axis=-1)
    code = jnp.repeat(code, TILE, axis=1)
    row_ids = jnp.arange(rows, dtype=jnp.int32)
    tag = (code * rows + place) * rows + row_ids[None] + 1
    slot_ids = jnp.arange(slots, dtype=jnp.int32)
    tags = jnp.sum(
        jnp.where(slot[:, None, :] == slot_ids[None, :, None], tag[:, None, :], 0), axis=2, dtype=jnp.int32
    )
    source = jnp.maximum(tags - 1, 0) % rows

    tiles = lower.reshape(children, row_tiles, TILE, pairs, 2, TILE)
    second = picks.reshape(children, row_tiles, 1, pairs, 1) == 1
    compact = jnp.where(second, tiles[..., 1, :], tiles[..., 0, :]).reshape(children, rows, pairs * TILE)
    child_ids = jnp.arange(children, dtype=jnp.int32)[:, None]

    def rows_to_parents(x):
        return lax.all_to_all(
            x.reshape(x.shape[:-2] + (count, cap) + x.shape[-1:]), "row", split_axis=x.ndim - 2, concat_axis=x.ndim - 2, tiled=True
        ).reshape(x.shape)

    got_tags = lax.all_to_all(tags.reshape(children, count, cap), "row", split_axis=1, concat_axis=1, tiled=True)
    got_tags = got_tags.reshape(children, slots)
    got_lower = rows_to_parents(compact[child_ids, source])
    got_schur = []
    for child in range(children):
        sent = (schur[child][source[child]] * SCALE).astype(jnp.float16)
        got_schur.append(rows_to_parents(sent))

    got_place = jnp.where(got_tags > 0, (got_tags - 1) // rows % rows, rows)
    got_code = (got_tags - 1) // (rows * rows)
    note = slot_ids[None] * codes + got_code
    notes = jnp.sum(
        jnp.where(got_place[:, None, :] == row_ids[None, :, None], note[:, None, :], 0), axis=2, dtype=jnp.int32
    )
    where_from = notes // codes
    bits = (notes % codes)[:, :, None] // (2 ** jnp.arange(pairs, dtype=jnp.int32)) % 2
    parent_lower = got_lower[child_ids, where_from].reshape(children, rows, pairs, 1, TILE)
    halves = jnp.arange(2, dtype=jnp.int32)
    full = jnp.where(bits[..., None, None] == halves[:, None], parent_lower, 0).astype(jnp.bfloat16)
    full = lax.all_gather(full.reshape(children, rows, local_depth), "col", axis=2, tiled=True)

    me = lax.axis_index("row")
    z, x = me // inner, me % inner
    depth = upper.shape[1]
    lefts, rights = [], []
    for k, j, block in blocks:
        owner = ((z - k + outer) % outer) * inner + (x - j + inner) % inner
        for child in range(children):
            lefts.append(lax.dynamic_slice_in_dim(full[child], owner * depth, depth, axis=1))
            rights.append(block[child])
    update = jnp.dot(
        jnp.concatenate(lefts, axis=1), jnp.concatenate(rights, axis=0), preferred_element_type=jnp.float32
    )
    result = front - update
    for child in range(children):
        result = result + got_schur[child][where_from[child]].astype(jnp.float32) * (1.0 / SCALE)
    return result


def solution(mesh):
    in_specs = (
        P(None, "row", "col"),
        P(None, "row", "col"),
        P(None, "row", "col"),
        P(None, "row", "col"),
        P(None, "row"),
        P("row", "col"),
    )
    out_specs = P("row", "col")
    return jax.shard_map(shards, mesh=mesh, in_specs=in_specs, out_specs=out_specs, check_vma=False)
```

time: 545 us -> 427 us (0.78)
  waiting for transfers between devices: 407 us -> 183 us
  local copies, waits for them, and re-layouts: 38.9 us -> 128 us
  starting transfers between devices: 21.3 us -> 56.1 us
  other arithmetic: 46.6 us -> 31.3 us
    all_to_all x4, waiting for transfers between devices: 249 us -> 30.8 us  [the longest x3 30.8 us: rows_to_parents(): lax.all_to_all(x.reshape(x.shape[:-2] + (count, cap) + x.shape[-1:]), 'ro...]
    all_gather x2 -> x1, waiting for transfers between devices: 158 us -> 0.01 us  [shards(): lax.all_gather(full.reshape(children, rows, local_depth), 'col', axis=2,...]
    ppermute x0 -> x13, waiting for transfers between devices: none -> 153 us  [send(): return lax.ppermute(x, 'row', pairs)]
    gather x0 -> x6, local copies, waits for them, and re-layouts: none -> 62.1 us  [the longest x2 21.1 us: shards(): sent = (schur[child][source[child]] * SCALE).astype(jnp.float16)]
    scatter-add x2 -> x0, other arithmetic: 37.6 us -> none  [assemble(): return result.at[index].add(values.reshape(-1, width), mode='drop')]
    ppermute x0 -> x13, starting transfers between devices: none -> 32 us  [send(): return lax.ppermute(x, 'row', pairs)]
    slice x1 -> x3, local copies, waits for them, and re-layouts: 0.29 us -> 19 us  [the longest x1 14.1 us: shards(): tiles[..., 0, :]]
    select_n x3 -> x15, other arithmetic: 0.07 us -> 14.7 us  [the longest x1 6.92 us: shards(): jnp.where(bits[..., None, None] == halves[:, None], parent_lower, 0)]
  transfers between devices with their start and end apart: 6 -> 18, of which waited for: 5 -> 6; matrix products, arithmetic and copies ran while one was open for 13% -> 29% of each run, Pallas kernels for 0% -> 0%
where the time goes in v1:
time: 427 us; the launch traced here: 426 us
  waiting for transfers between devices  183 us (43%)
  local copies, waits for them, and re-layouts  128 us (30%)
  starting transfers between devices  56.1 us (13%)
  other arithmetic  31.3 us (7%)
  between operations  13.9 us (3%)
  matrix products  12.5 us (3%)
    ppermute x13, waiting for transfers between devices, send(): return lax.ppermute(x, 'row', pairs)  153 us
    ppermute x13, starting transfers between devices, send(): return lax.ppermute(x, 'row', pairs)  32 us
    all_to_all x3, waiting for transfers between devices, rows_to_parents(): lax.all_to_all(x.reshape(x.shape[:-2] + (count, cap) + x.shape[-1:]), 'ro...  30.8 us
    gather x2, local copies, waits for them, and re-layouts, shards(): sent = (schur[child][source[child]] * SCALE).astype(jnp.float16)  21.1 us
    unnamed x42, local copies, waits for them, and re-layouts  19.1 us
    all_to_all x3, starting transfers between devices, rows_to_parents(): lax.all_to_all(x.reshape(x.shape[:-2] + (count, cap) + x.shape[-1:]), 'ro...  16.6 us
    gather x1, local copies, waits for them, and re-layouts, shards(): got_lower = rows_to_parents(compact[child_ids, source])  16.3 us
    slice x1, local copies, waits for them, and re-layouts, shards(): tiles[..., 0, :]  14.1 us
  transfers between devices with their start and end apart: 18, of which 6 were waited for; matrix products, arithmetic and copies ran while one was open for 29% of the time, Pallas kernels for 0%

profile of v1, /device:TPU:0, one launch (start us, length us, event | category | flops | bytes accessed | tf_op | source)
XLA Modules:
  0.0 425.8 jit_solution(6641330874084406175)
XLA Ops:
  8.8 1.9 convert_reduce_fusion
  10.7 1.5 select_reduce_fusion.1
  13.0 7.3 %all-to-all-start = ((s32[2,8,192]{2,0,1:T(2,128)}), s32[2,8,192]{2,0,1:T(2,128)S(1)}, u32[]{:S(2)}, u32[]{:S(2)}) async-start(s32[2,8,192]{2,0,1:T(2,128)} %copy.35), calls=%async_computation | async-start | bytes 32768 | tf_op jit(solution)/shard_map/all_to_all | solution.py:89
  20.2 2.6 reshape.450
  22.8 14.1 %slice_reduce_fusion = (bf16[2,8,128,2,128]{4,3,2,1,0:T(2,128)(2,1)}, bf16[2,8,128,2,128]{4,3,2,1,0:T(2,128)(2,1)}) fusion(bf16[2,8,128,2,2,128]{5,4,3,2,1,0:T(2,128)(2,1)S(1)} %reshape.450), kind=kLoop, calls=%fused_computation.18 | loop fusion | bytes 4194304 | tf_op jit(solution)/shard_map/slice | solution.py:81
  37.8 1.0 copy.41
  38.8 1.7 squeeze.93
  40.5 2.5 squeeze.92
  43.0 1.6 select_n.429
  44.7 16.3 %gather_fusion = bf16[3072,256]{1,0:T(8,128)(2,1)S(1)} fusion(bf16[2,1024,256]{2,1,0:T(8,128)(2,1)S(1)} %select_n.429, s32[3072]{0:T(1024)S(1)} %reshape.455), kind=kCustom, calls=%fused_computation | custom fusion | bytes 3170304 | tf_op jit(solution)/shard_map/gather | solution.py:91
  61.0 1.3 copy.42
  62.3 6.0 %all-to-all-start.1 = ((bf16[2,8,192,256]{3,2,0,1:T(8,128)(2,1)}), bf16[2,8,192,256]{3,2,0,1:T(8,128)(2,1)}, u32[]{:S(2)}, u32[]{:S(2)}) async-start(bf16[2,8,192,256]{3,2,0,1:T(8,128)(2,1)} %copy.42), calls=%async_computation.1 | async-start | bytes 3145728 | tf_op jit(solution)/shard_map/all_to_all | solution.py:85
  68.9 1.5 select_reduce_fusion
  71.3 2.8 copy.38
  74.0 30.8 %all-to-all-done.1 = bf16[2,8,192,256]{3,2,0,1:T(8,128)(2,1)} async-done(((bf16[2,8,192,256]{3,2,0,1:T(8,128)(2,1)}), bf16[2,8,192,256]{3,2,0,1:T(8,128)(2,1)}, u32[]{:S(2)}, u32[]{:S(2)}) %all-to-all-start.1) | async-done | bytes 1572896 | tf_op jit(solution)/shard_map/all_to_all | solution.py:85
  104.8 1.5 copy.43
  106.3 11.1 %gather_fusion.1 = bf16[2048,256]{1,0:T(8,128)(2,1)S(1)} fusion(bf16[2,1536,256]{2,1,0:T(8,128)(2,1)S(1)} %bitcast.158, s32[2048]{0:T(1024)S(1)} %bitcast.156), kind=kCustom, calls=%fused_computation.1 | custom fusion | bytes 2113536 | tf_op jit(solution)/shard_map/gather | solution.py:105
  117.4 1.1 broadcast_in_dim.113
  118.6 6.9 %broadcast_select_fusion = bf16[2,1024,2,2,128]{4,3,2,1,0:T(2,128)(2,1)S(1)} fusion(pred[2,1024,2,2]{3,2,1,0:T(4,128)(4,1)} %copy.38, bf16[2,1024,2,128]{3,2,1,0:T(2,128)(2,1)} %broadcast_in_dim.113), kind=kLoop, calls=%fused_computation.17 | loop fusion | flops 1048576 | bytes 3153920 | tf_op jit(solution)/shard_map/jit(_where)/select_n | solution.py:107
  125.5 2.2 select_n.435
  127.8 9.0 %slice_bitcast_fusion.1 = (f32[1024,1024]{1,0:T(8,128)}, f32[1024,1024]{1,0:T(8,128)}) fusion(f32[2,1024,1024]{2,1,0:T(8,128)} %param.6), kind=kLoop, calls=%fused_computation.15 | loop fusion | bytes 16777216 | tf_op jit(solution)/shard_map/squeeze | solution.py:94
  136.8 11.1 %gather_fusion.2 = f32[1536,1024]{1,0:T(8,128)} fusion(f32[1024,1024]{1,0:T(8,128)} %get-tuple-element.13, s32[2048]{0:T(1024)S(1)} %pad_clamp_fusion.1), kind=kCustom, calls=%fused_computation.2 | custom fusion | bytes 12589056 | tf_op jit(solution)/shard_map/gather | solution.py:94
  147.9 5.4 %multiply_convert_fusion.1 = f16[1536,1024]{1,0:T(8,128)(2,1)} fusion(f32[1536,1024]{1,0:T(8,128)} %gather_fusion.2), kind=kLoop, calls=%fused_computation.12 | loop fusion | flops 3145728 | bytes 9437184 | tf_op jit(solution)/shard_map/convert_element_type | solution.py:94
  153.3 3.6 all-to-all-start.2
  157.0 1.3 collective-permute-start.2
  158.3 2.0 collective-permute-start
  160.3 5.6 %collective-permute-start.1 = (bf16[2,256,1024]{2,1,0:T(8,128)(2,1)}, bf16[2,256,1024]{2,1,0:T(8,128)(2,1)}, u32[]{:S(2)}, u32[]{:S(2)}) collective-permute-start(bf16[2,256,1024]{2,1,0:T(8,128)(2,1)} %param.8), channel_id=1, source_target_pairs={{0,8},{4,12},{8,16},{12,20},{16,24},{20,28},{1,9},{5,13},{9,17},{1... | collective-permute-start | bytes 3145736 | tf_op jit(solution)/shard_map/ppermute | solution.py:22
  165.9 10.0 %gather_fusion.4 = f32[1536,1024]{1,0:T(8,128)} fusion(f32[1024,1024]{1,0:T(8,128)} %get-tuple-element.14, s32[2048]{0:T(1024)S(1)} %pad_clamp_fusion), kind=kCustom, calls=%fused_computation.4 | custom fusion | bytes 12589056 | tf_op jit(solution)/shard_map/gather | solution.py:94
  175.9 55.8 %collective-permute-done.2 = bf16[2,256,1024]{2,1,0:T(8,128)(2,1)} collective-permute-done((bf16[2,256,1024]{2,1,0:T(8,128)(2,1)}, bf16[2,256,1024]{2,1,0:T(8,128)(2,1)}, u32[]{:S(2)}, u32[]{:S(2)}) %collective-permute-start.2) | collective-permute-done | bytes 1048608 | tf_op jit(solution)/shard_map/ppermute | solution.py:22
  231.6 1.3 collective-permute-start.3
  232.9 5.4 %multiply_convert_fusion = f16[1536,1024]{1,0:T(8,128)(2,1)} fusion(f32[1536,1024]{1,0:T(8,128)} %gather_fusion.4), kind=kLoop, calls=%fused_computation.11 | loop fusion | flops 3145728 | bytes 9437184 | tf_op jit(solution)/shard_map/convert_element_type | solution.py:94
  238.3 0.9 bitcast_dynamic-update-slice_fusion.1
  239.2 1.9 bitcast_dynamic-update-slice_fusion
  241.1 1.7 collective-permute-start.7
  242.8 30.6 %collective-permute-done.3 = bf16[2,256,1024]{2,1,0:T(8,128)(2,1)} collective-permute-done((bf16[2,256,1024]{2,1,0:T(8,128)(2,1)}, bf16[2,256,1024]{2,1,0:T(8,128)(2,1)}, u32[]{:S(2)}, u32[]{:S(2)}) %collective-permute-start.3) | collective-permute-done | bytes 1048608 | tf_op jit(solution)/shard_map/ppermute | solution.py:22
  273.4 1.3 collective-permute-start.4
  274.7 7.0 %all-to-all-start.3 = ((f16[8,192,1024]{2,1,0:T(8,128)(2,1)}), f16[8,192,1024]{2,1,0:T(8,128)(2,1)}, u32[]{:S(2)}, u32[]{:S(2)}) async-start(f16[8,192,1024]{2,1,0:T(8,128)(2,1)} %bitcast.159), calls=%async_computation.3 | async-start | bytes 6291456 | tf_op jit(solution)/shard_map/all_to_all | solution.py:85
  282.5 1.9 fusion.13
  284.3 1.9 fusion.12
  286.2 3.9 collective-permute-start.9
  291.6 1.4 broadcast_select_fusion.4
  293.0 27.0 %collective-permute-done.4 = bf16[2,256,1024]{2,1,0:T(8,128)(2,1)} collective-permute-done((bf16[2,256,1024]{2,1,0:T(8,128)(2,1)}, bf16[2,256,1024]{2,1,0:T(8,128)(2,1)}, u32[]{:S(2)}, u32[]{:S(2)}) %collective-permute-start.4) | collective-permute-done | bytes 1048608 | tf_op jit(solution)/shard_map/ppermute | solution.py:22
  320.0 9.9 %collective-permute-start.6 = (bf16[2,256,1024]{2,1,0:T(8,128)(2,1)}, bf16[2,256,1024]{2,1,0:T(8,128)(2,1)S(1)}, u32[]{:S(2)}, u32[]{:S(2)}) collective-permute-start(bf16[2,256,1024]{2,1,0:T(8,128)(2,1)} %collective-permute-done.4), channel_id=1, source_target_pairs={{0,4},{4,0},{1,5},{5,1},{2,6},{6,2},{3,7},{7,3}} | collective-permute-start | bytes 3145736 | tf_op jit(solution)/shard_map/ppermute | solution.py:22
  329.9 1.4 broadcast_select_fusion.6
  331.3 0.8 fusion.11
  333.0 1.9 collective-permute-start.12
  334.9 1.4 broadcast_select_fusion.2
  336.3 1.0 collective-permute-start.11
  337.4 25.8 %collective-permute-done.6 = bf16[2,256,1024]{2,1,0:T(8,128)(2,1)S(1)} collective-permute-done((bf16[2,256,1024]{2,1,0:T(8,128)(2,1)}, bf16[2,256,1024]{2,1,0:T(8,128)(2,1)S(1)}, u32[]{:S(2)}, u32[]{:S(2)}) %collective-permute-start.6) | collective-permute-done | bytes 1048608 | tf_op jit(solution)/shard_map/ppermute | solution.py:22
  363.3 0.8 fusion.9
  364.1 0.8 fusion.8
  365.0 0.9 fusion.7
  365.8 0.8 fusion.6
  366.7 0.8 fusion.5
  368.3 0.8 fusion.3
  369.2 0.9 fusion.2
  370.0 13.4 %collective-permute-done.12 = bf16[2,256,1024]{2,1,0:T(8,128)(2,1)S(1)} collective-permute-done((bf16[2,256,1024]{2,1,0:T(8,128)(2,1)}, bf16[2,256,1024]{2,1,0:T(8,128)(2,1)S(1)}, u32[]{:S(2)}, u32[]{:S(2)}) %collective-permute-start.12) | collective-permute-done | bytes 1048608 | tf_op jit(solution)/shard_map/ppermute | solution.py:22
  383.6 0.9 fusion.1
  384.4 0.9 fusion
  385.3 5.2 %gather_fusion.3 = f16[1024,1024]{1,0:T(8,128)(2,1)} fusion(f16[1536,1024]{1,0:T(8,128)(2,1)S(1)} %bitcast.157, s32[1024]{0:T(1024)S(1)} %broadcast_clamp_fusion.1), kind=kCustom, calls=%fused_computation.3 | custom fusion | bytes 4198400 | tf_op jit(solution)/shard_map/gather | solution.py:124
  390.5 8.4 %gather_fusion.5 = f16[1024,1024]{1,0:T(8,128)(2,1)} fusion(f16[1536,1024]{1,0:T(8,128)(2,1)} %bitcast.47, s32[1024]{0:T(1024)S(1)} %broadcast_clamp_fusion), kind=kCustom, calls=%fused_computation.5 | custom fusion | bytes 4198400 | tf_op jit(solution)/shard_map/gather | solution.py:124
  398.9 4.1 fusion.32
  405.3 1.2 slice-done.1
  406.5 12.5 %multiply_add_fusion = f32[1024,1024]{1,0:T(8,128)} fusion(f16[1024,1024]{1,0:T(8,128)(2,1)S(1)} %copy-done.1, f16[1024,1024]{1,0:T(8,128)(2,1)S(1)} %copy-done, f32[1024,1024]{1,0:T(8,128)} %param.11, bf16[1024,4096]{1,0:T(8,128)(2,1)S(1)} %bitcast_dynamic-update-slice_fusion.2, bf16[4096,1024]{1,0:T(8,128)(2,1)S(1)} %bitcast.163), kind=kOutput, calls=%fused_computation.13 | convolution fusion | flops 8597274624 | bytes 29360128 | tf_op jit(solution)/shard_map/dot_general | solution.py:119
  (82 shorter events, 11.7 us)
Async XLA Ops:
  13.0 49.3 %all-to-all-start = ((s32[2,8,192]{2,0,1:T(2,128)}), s32[2,8,192]{2,0,1:T(2,128)S(1)}, u32[]{:S(2)}, u32[]{:S(2)}) async-start(s32[2,8,192]{2,0,1:T(2,128)} %copy.35), calls=%async_computation | async-start | bytes 32768 | tf_op jit(solution)/shard_map/all_to_all | solution.py:89
  62.3 42.5 %all-to-all-start.1 = ((bf16[2,8,192,256]{3,2,0,1:T(8,128)(2,1)}), bf16[2,8,192,256]{3,2,0,1:T(8,128)(2,1)}, u32[]{:S(2)}, u32[]{:S(2)}) async-start(bf16[2,8,192,256]{3,2,0,1:T(8,128)(2,1)} %copy.42), calls=%async_computation.1 | async-start | bytes 3145728 | tf_op jit(solution)/shard_map/all_to_all | solution.py:85
  68.3 330.6 %all-gather.2.cloned.1.call-start = ((), (), s32[]{:S(2)}) async-start(), calls=%async_computation.4 | async-start | bytes 10485760 | tf_op jit(solution)/shard_map/all_gather | solution.py:108
  153.3 121.4 %all-to-all-start.2 = ((f16[8,192,1024]{2,1,0:T(8,128)(2,1)}), f16[8,192,1024]{2,1,0:T(8,128)(2,1)S(1)}, u32[]{:S(2)}, u32[]{:S(2)}) async-start(f16[8,192,1024]{2,1,0:T(8,128)(2,1)} %bitcast.160), calls=%async_computation.2 | async-start | bytes 6291456 | tf_op jit(solution)/shard_map/all_to_all | solution.py:85
  157.0 74.7 %collective-permute-start.2 = (bf16[2,256,1024]{2,1,0:T(8,128)(2,1)}, bf16[2,256,1024]{2,1,0:T(8,128)(2,1)}, u32[]{:S(2)}, u32[]{:S(2)}) collective-permute-start(bf16[2,256,1024]{2,1,0:T(8,128)(2,1)} %param.8), channel_id=1, source_target_pairs={{8,0},{12,4},{16,8},{20,12},{24,16},{28,20},{9,1},{13,5},{17,9},{2... | collective-permute-start | bytes 3145736 | tf_op jit(solution)/shard_map/ppermute | solution.py:22
  158.3 124.2 %collective-permute-start = (bf16[2,256,1024]{2,1,0:T(8,128)(2,1)}, bf16[2,256,1024]{2,1,0:T(8,128)(2,1)}, u32[]{:S(2)}, u32[]{:S(2)}) collective-permute-start(bf16[2,256,1024]{2,1,0:T(8,128)(2,1)} %param.8), channel_id=1, source_target_pairs={{0,4},{4,0},{8,12},{12,8},{16,20},{20,16},{24,28},{28,24},{1,5},{5... | collective-permute-start | bytes 3145736 | tf_op jit(solution)/shard_map/ppermute | solution.py:22
  160.3 80.8 %collective-permute-start.1 = (bf16[2,256,1024]{2,1,0:T(8,128)(2,1)}, bf16[2,256,1024]{2,1,0:T(8,128)(2,1)}, u32[]{:S(2)}, u32[]{:S(2)}) collective-permute-start(bf16[2,256,1024]{2,1,0:T(8,128)(2,1)} %param.8), channel_id=1, source_target_pairs={{0,8},{4,12},{8,16},{12,20},{16,24},{20,28},{1,9},{5,13},{9,17},{1... | collective-permute-start | bytes 3145736 | tf_op jit(solution)/shard_map/ppermute | solution.py:22
  175.9 62.5 %copy-start.2 = (bf16[2,256,1024]{2,1,0:T(8,128)(2,1)S(1)}, bf16[2,256,1024]{2,1,0:T(8,128)(2,1)}, u32[]{:S(2)}) copy-start(bf16[2,256,1024]{2,1,0:T(8,128)(2,1)} %param.8) | copy-start | bytes 3145732
  231.6 41.8 %collective-permute-start.3 = (bf16[2,256,1024]{2,1,0:T(8,128)(2,1)}, bf16[2,256,1024]{2,1,0:T(8,128)(2,1)}, u32[]{:S(2)}, u32[]{:S(2)}) collective-permute-start(bf16[2,256,1024]{2,1,0:T(8,128)(2,1)} %collective-permute-done.2), channel_id=1, source_target_pairs={{8,0},{12,4},{16,8},{20,12},{9,1},{13,5},{17,9},{21,13},{10,2},{14... | collective-permute-start | bytes 3145736 | tf_op jit(solution)/shard_map/ppermute | solution.py:22
  241.1 49.1 %collective-permute-start.7 = (bf16[2,256,1024]{2,1,0:T(8,128)(2,1)}, bf16[2,256,1024]{2,1,0:T(8,128)(2,1)}, u32[]{:S(2)}, u32[]{:S(2)}) collective-permute-start(bf16[2,256,1024]{2,1,0:T(8,128)(2,1)} %collective-permute-done.1), channel_id=1, source_target_pairs={{8,16},{12,20},{16,24},{20,28},{9,17},{13,21},{17,25},{21,29},{10,... | collective-permute-start | bytes 3145736 | tf_op jit(solution)/shard_map/ppermute | solution.py:22
  273.4 46.6 %collective-permute-start.4 = (bf16[2,256,1024]{2,1,0:T(8,128)(2,1)}, bf16[2,256,1024]{2,1,0:T(8,128)(2,1)}, u32[]{:S(2)}, u32[]{:S(2)}) collective-permute-start(bf16[2,256,1024]{2,1,0:T(8,128)(2,1)} %collective-permute-done.3), channel_id=1, source_target_pairs={{8,0},{12,4},{9,1},{13,5},{10,2},{14,6},{11,3},{15,7}} | collective-permute-start | bytes 3145736 | tf_op jit(solution)/shard_map/ppermute | solution.py:22
  274.7 115.7 %all-to-all-start.3 = ((f16[8,192,1024]{2,1,0:T(8,128)(2,1)}), f16[8,192,1024]{2,1,0:T(8,128)(2,1)}, u32[]{:S(2)}, u32[]{:S(2)}) async-start(f16[8,192,1024]{2,1,0:T(8,128)(2,1)} %bitcast.159), calls=%async_computation.3 | async-start | bytes 6291456 | tf_op jit(solution)/shard_map/all_to_all | solution.py:85
  281.7 55.7 %collective-permute-start.5 = (bf16[2,256,1024]{2,1,0:T(8,128)(2,1)}, bf16[2,256,1024]{2,1,0:T(8,128)(2,1)S(1)}, u32[]{:S(2)}, u32[]{:S(2)}) collective-permute-start(bf16[2,256,1024]{2,1,0:T(8,128)(2,1)} %collective-permute-done.1), channel_id=1, source_target_pairs={{8,12},{12,8},{16,20},{20,16},{24,28},{28,24},{9,13},{13,9},{17,21... | collective-permute-start | bytes 3145736 | tf_op jit(solution)/shard_map/ppermute | solution.py:22
  286.2 50.0 %collective-permute-start.9 = (bf16[2,256,1024]{2,1,0:T(8,128)(2,1)}, bf16[2,256,1024]{2,1,0:T(8,128)(2,1)S(1)}, u32[]{:S(2)}, u32[]{:S(2)}) collective-permute-start(bf16[2,256,1024]{2,1,0:T(8,128)(2,1)} %collective-permute-done.3), channel_id=1, source_target_pairs={{0,4},{4,0},{8,12},{12,8},{1,5},{5,1},{9,13},{13,9},{2,6},{6,2},{1... | collective-permute-start | bytes 3145736 | tf_op jit(solution)/shard_map/ppermute | solution.py:22
  290.2 42.8 %collective-permute-start.10 = (bf16[2,256,1024]{2,1,0:T(8,128)(2,1)}, bf16[2,256,1024]{2,1,0:T(8,128)(2,1)S(1)}, u32[]{:S(2)}, u32[]{:S(2)}) collective-permute-start(bf16[2,256,1024]{2,1,0:T(8,128)(2,1)} %collective-permute-done.7), channel_id=1, source_target_pairs={{16,24},{20,28},{17,25},{21,29},{18,26},{22,30},{19,27},{23,31}} | collective-permute-start | bytes 3145736 | tf_op jit(solution)/shard_map/ppermute | solution.py:22
  290.9 46.4 %collective-permute-start.8 = (bf16[2,256,1024]{2,1,0:T(8,128)(2,1)}, bf16[2,256,1024]{2,1,0:T(8,128)(2,1)S(1)}, u32[]{:S(2)}, u32[]{:S(2)}) collective-permute-start(bf16[2,256,1024]{2,1,0:T(8,128)(2,1)} %collective-permute-done.7), channel_id=1, source_target_pairs={{16,20},{20,16},{24,28},{28,24},{17,21},{21,17},{25,29},{29,25},{1... | collective-permute-start | bytes 3145736 | tf_op jit(solution)/shard_map/ppermute | solution.py:22
  320.0 43.2 %collective-permute-start.6 = (bf16[2,256,1024]{2,1,0:T(8,128)(2,1)}, bf16[2,256,1024]{2,1,0:T(8,128)(2,1)S(1)}, u32[]{:S(2)}, u32[]{:S(2)}) collective-permute-start(bf16[2,256,1024]{2,1,0:T(8,128)(2,1)} %collective-permute-done.4), channel_id=1, source_target_pairs={{0,4},{4,0},{1,5},{5,1},{2,6},{6,2},{3,7},{7,3}} | collective-permute-start | bytes 3145736 | tf_op jit(solution)/shard_map/ppermute | solution.py:22
  333.0 50.5 %collective-permute-start.12 = (bf16[2,256,1024]{2,1,0:T(8,128)(2,1)}, bf16[2,256,1024]{2,1,0:T(8,128)(2,1)S(1)}, u32[]{:S(2)}, u32[]{:S(2)}) collective-permute-start(bf16[2,256,1024]{2,1,0:T(8,128)(2,1)} %collective-permute-done.2), channel_id=1, source_target_pairs={{0,4},{4,0},{8,12},{12,8},{16,20},{20,16},{1,5},{5,1},{9,13},{13,9... | collective-permute-start | bytes 3145736 | tf_op jit(solution)/shard_map/ppermute | solution.py:22
  336.3 47.2 %collective-permute-start.11 = (bf16[2,256,1024]{2,1,0:T(8,128)(2,1)S(1)}, bf16[2,256,1024]{2,1,0:T(8,128)(2,1)S(1)}, u32[]{:S(2)}, u32[]{:S(2)}) collective-permute-start(bf16[2,256,1024]{2,1,0:T(8,128)(2,1)S(1)} %collective-permute-done.10), channel_id=1, source_target_pairs={{24,28},{28,24},{25,29},{29,25},{26,30},{30,26},{27,31},{31,27}} | collective-permute-start | bytes 3145736 | tf_op jit(solution)/shard_map/ppermute | solution.py:22
  398.8 5.6 %slice-start = ((s8[8388608]{0:T(1024)(128)(4,1)}), s8[4194304]{0:T(1024)(128)(4,1)S(1)}, s32[]{:S(2)}) async-start(s8[8388608]{0:T(1024)(128)(4,1)} %bitcast.162), calls=%async_computation.5 | async-start | bytes 8388608
  403.0 1.7 copy-start
  403.0 2.3 copy-start.1
  403.0 3.5 slice-start.1
Sparse Core Ops, SparseCore 0:
  127.9 57.3 all-gather.1

commit v2 on v0

v2 whole, which is shorter than its diff:
```python
import functools

import jax
import jax.numpy as jnp
from jax import lax
from jax.experimental import pallas as pl
from jax.experimental.pallas import tpu as pltpu
from jax.sharding import PartitionSpec as P

TILE = 128
LANES = 128
TOP = 32767.0
TINY = 1e-33
VMEM_LIMIT = 48 * 1024 * 1024
ANY = pl.BlockSpec(memory_space=pl.ANY)


def inner_factor(count):
    inner = 1
    while (2 * inner) * (2 * inner) <= count:
        inner *= 2
    return inner


def gate_kernel(*refs):
    pass


def gate(x, *first):
    return pl.pallas_call(
        gate_kernel,
        out_shape=jax.ShapeDtypeStruct(x.shape, x.dtype),
        in_specs=[ANY] * (1 + len(first)),
        out_specs=ANY,
        input_output_aliases={0: 0},
        name="gate",
    )(x, *first)


def pack_kernel(groups, steps, source, x, first, out, held):
    i = pl.program_id(0)
    rows = x.shape[0]
    per = 16 // groups

    @pl.when(i < steps)
    def _():
        def body(g, carry):
            at = pl.multiple_of(g * 8, 8)
            v = x[pl.ds(at, 8), :]
            most = jnp.max(jnp.abs(v), axis=1, keepdims=True)
            inverse = jnp.where(most > TINY, TOP / most, 0.0)
            q = jnp.floor(v * inverse + 0.5).astype(jnp.int32)
            base = (i * rows + at) * groups
            for j in range(groups):
                held[pl.ds(base + j, 8, stride=groups), :] = q[:, j * LANES : (j + 1) * LANES]
            return carry

        lax.fori_loop(0, rows // 8, body, 0, unroll=4)

    @pl.when(i >= steps)
    def _():
        tiles = out.shape[0]
        start = (i - steps) * tiles * per

        def body(t, carry):
            parts = []
            for a in range(per):
                row = pl.multiple_of(source[start + t * per + a] * groups, groups)
                parts.append(held[pl.ds(row, groups), :])
            out[t] = jnp.concatenate(parts, axis=0).astype(jnp.int16)
            return carry

        lax.fori_loop(0, tiles, body, 0, unroll=8)


def pack(x, source, first):
    rows, width = x.shape
    slots = source.shape[0]
    groups = width // LANES
    per = 16 // groups
    steps, out_steps = 4, 8
    tiles = slots // per // out_steps
    return pl.pallas_call(
        functools.partial(pack_kernel, groups, steps),
        out_shape=jax.ShapeDtypeStruct((slots // per, 16, LANES), jnp.int16),
        grid_spec=pltpu.PrefetchScalarGridSpec(
            num_scalar_prefetch=1,
            grid=(steps + out_steps,),
            in_specs=[
                pl.BlockSpec((rows // steps, width), lambda i, s: (jnp.minimum(i, steps - 1), 0)),
                ANY,
            ],
            out_specs=pl.BlockSpec((tiles, 16, LANES), lambda i, s: (jnp.maximum(i - steps, 0), 0, 0)),
            scratch_shapes=[pltpu.VMEM((rows * groups, LANES), jnp.int32)],
        ),
        compiler_params=pltpu.CompilerParams(vmem_limit_bytes=VMEM_LIMIT),
        cost_estimate=pl.CostEstimate(flops=8 * rows * width, bytes_accessed=7 * rows * width, transcendentals=0),
        name="pack",
    )(source, x, first)


def unpack_kernel(groups, steps, place, scale, got, before, out, held):
    i = pl.program_id(0)
    per = 16 // groups

    @pl.when(i < steps)
    def _():
        tiles = got.shape[0]
        start = i * tiles * per

        def body(t, carry):
            v = got[t].astype(jnp.int32).astype(jnp.float32)
            for a in range(per):
                s = start + t * per + a
                row = pl.multiple_of(place[s] * groups, groups)
                held[pl.ds(row, groups), :] = v[a * groups : (a + 1) * groups] * scale[s]
            return carry

        lax.fori_loop(0, tiles, body, 0, unroll=8)

    @pl.when(i >= steps)
    def _():
        rows = out.shape[0]

        def body(g, carry):
            at = pl.multiple_of(g * 8, 8)
            base = ((i - steps) * rows + at) * groups
            for j in range(groups):
                piece = held[pl.ds(base + j, 8, stride=groups), :]
                cols = pl.ds(j * LANES, LANES)
                out[pl.ds(at, 8), cols] = before[pl.ds(at, 8), cols] + piece
            return carry

        lax.fori_loop(0, rows // 8, body, 0, unroll=4)


def unpack(got, place, scale, before):
    rows, width = before.shape
    slots = place.shape[0]
    groups = width // LANES
    per = 16 // groups
    steps, out_steps = 8, 4
    tiles = slots // per // steps
    return pl.pallas_call(
        functools.partial(unpack_kernel, groups, steps),
        out_shape=jax.ShapeDtypeStruct((rows, width), jnp.float32),
        grid_spec=pltpu.PrefetchScalarGridSpec(
            num_scalar_prefetch=2,
            grid=(steps + out_steps,),
            in_specs=[
                pl.BlockSpec((tiles, 16, LANES), lambda i, p, s: (jnp.minimum(i, steps - 1), 0, 0)),
                pl.BlockSpec((rows // out_steps, width), lambda i, p, s: (jnp.maximum(i - steps, 0), 0)),
            ],
            out_specs=pl.BlockSpec((rows // out_steps, width), lambda i, p, s: (jnp.maximum(i - steps, 0), 0)),
            scratch_shapes=[pltpu.VMEM(((rows + 8) * groups, LANES), jnp.float32)],
        ),
        compiler_params=pltpu.CompilerParams(vmem_limit_bytes=VMEM_LIMIT),
        cost_estimate=pl.CostEstimate(flops=4 * rows * width, bytes_accessed=11 * rows * width, transcendentals=0),
        name="unpack",
    )(place, scale, got, before)


def lower_pack_kernel(picks, low, slot, out, compact):
    c = pl.program_id(0)
    rows, wide = compact.shape
    pairs = wide // TILE
    for i in range(rows // TILE):
        for j in range(pairs):
            column = (2 * j + picks[(c * (rows // TILE) + i) * pairs + j]) * TILE
            at = pl.ds(i * TILE, TILE)
            compact[at, j * TILE : (j + 1) * TILE] = low[0, at, pl.ds(pl.multiple_of(column, TILE), TILE)]
    step = 256

    def body(t, carry):
        at = pl.multiple_of(t * step, step)
        ids = lax.broadcasted_iota(jnp.int32, (step, rows), 0) + at
        hit = jnp.where(slot[0] == ids, 1.0, 0.0).astype(jnp.bfloat16)
        out[0, pl.ds(at, step), :] = jnp.dot(
            hit, compact[...], preferred_element_type=jnp.float32
        ).astype(jnp.bfloat16)
        return carry

    lax.fori_loop(0, out.shape[1] // step, body, 0)


def lower_pack(lower, picks, slot, slots):
    children, rows, depth = lower.shape
    wide = depth // 2
    return pl.pallas_call(
        lower_pack_kernel,
        out_shape=jax.ShapeDtypeStruct((children, slots, wide), jnp.bfloat16),
        grid_spec=pltpu.PrefetchScalarGridSpec(
            num_scalar_prefetch=1,
            grid=(children,),
            in_specs=[
                pl.BlockSpec((1, rows, depth), lambda c, p: (c, 0, 0)),
                pl.BlockSpec((1, 1, rows), lambda c, p: (c, 0, 0)),
            ],
            out_specs=pl.BlockSpec((1, slots, wide), lambda c, p: (c, 0, 0)),
            scratch_shapes=[pltpu.VMEM((rows, wide), jnp.bfloat16)],
        ),
        compiler_params=pltpu.CompilerParams(vmem_limit_bytes=VMEM_LIMIT),
        name="lower_pack",
    )(picks.reshape(-1), lower, slot.reshape(children, 1, rows))


def lower_unpack_kernel(got, place, code, out):
    slots, wide = got.shape[1:]
    rows = out.shape[1]
    step = 256

    def body(t, carry):
        at = pl.multiple_of(t * step, step)
        ids = lax.broadcasted_iota(jnp.int32, (step, slots), 0) + at
        hit = place[0] == ids
        mine = jnp.dot(
            jnp.where(hit, 1.0, 0.0).astype(jnp.bfloat16), got[0], preferred_element_type=jnp.float32
        )
        bits = jnp.sum(jnp.where(hit, code[0], 0.0), axis=1, keepdims=True).astype(jnp.int32)
        for j in range(wide // TILE):
            bit = (bits >> j) & 1
            for s in range(2):
                tile = jnp.where(bit == s, mine[:, j * TILE : (j + 1) * TILE], 0.0)
                out[0, pl.ds(at, step), (2 * j + s) * TILE : (2 * j + s + 1) * TILE] = tile.astype(jnp.bfloat16)
        return carry

    lax.fori_loop(0, rows // step, body, 0)


def lower_unpack(got, place, code, rows):
    children, slots, wide = got.shape
    lane = pl.BlockSpec((1, 1, slots), lambda c: (c, 0, 0))
    return pl.pallas_call(
        lower_unpack_kernel,
        out_shape=jax.ShapeDtypeStruct((children, rows, 2 * wide), jnp.bfloat16),
        grid=(children,),
        in_specs=[pl.BlockSpec((1, slots, wide), lambda c: (c, 0, 0)), lane, lane],
        out_specs=pl.BlockSpec((1, rows, 2 * wide), lambda c: (c, 0, 0)),
        compiler_params=pltpu.CompilerParams(vmem_limit_bytes=VMEM_LIMIT),
        name="lower_unpack",
    )(got, place.reshape(children, 1, slots), code.reshape(children, 1, slots))


class Relay:
    def __init__(self, block, count):
        self.inner = inner_factor(count)
        self.outer = count // self.inner
        self.up = self.down = block
        self.ups, self.downs = {}, {}
        self.own = [block] + self.exchange(block, 0, self.outer)
        self.k = 0

    def send(self, x, pairs):
        return lax.ppermute(x, "row", pairs)

    def along(self, step, first, last):
        n = self.inner
        return [(z * n + x, (z + step) * n + x) for z in range(first, last) for x in range(n)]

    def exchange(self, x, first, last):
        n = self.inner
        return [
            self.send(x, [(z * n + i, z * n + (i + j) % n) for z in range(first, last) for i in range(n)])
            for j in range(1, n)
        ]

    def step(self):
        if self.k + 1 >= self.outer:
            return
        self.k += 1
        self.up = self.send(self.up, self.along(1, self.k - 1, self.outer - 1))
        self.down = self.send(self.down, self.along(-1, 1, self.outer - self.k + 1))
        self.ups[self.k] = [self.up] + self.exchange(self.up, self.k, self.outer)
        self.downs[self.k] = [self.down] + self.exchange(self.down, 0, self.outer - self.k)

    def blocks(self):
        while self.k + 1 < self.outer:
            self.step()
        me = lax.axis_index("row")
        z, x = me // self.inner, me % self.inner
        found = []
        for k in range(self.outer):
            for j in range(self.inner):
                block = self.own[j] if k == 0 else jnp.where(z >= k, self.ups[k][j], self.downs[self.outer - k][j])
                owner = ((z - k + self.outer) % self.outer) * self.inner + (x - j + self.inner) % self.inner
                found.append((owner, block))
        return found


def shards(schur, lower, upper, tile_mask, row_map, front):
    children, rows, local_depth = lower.shape
    count = lax.axis_size("row")
    me = lax.axis_index("row")
    cap = 3 * rows // (2 * count)
    slots = count * cap
    row_tiles = rows // TILE
    pairs = local_depth // (2 * TILE)

    relay = Relay(upper, count)
    relay.step()

    target = row_map // rows
    place = row_map % rows
    earlier = jnp.tril(jnp.ones((rows, rows), jnp.bool_), -1)
    rank = jnp.sum((target[:, :, None] == target[:, None, :]) & earlier[None], axis=2, dtype=jnp.int32)
    slot = target * cap + rank
    picks = tile_mask.reshape(children, row_tiles, pairs, 2)[..., 1]
    code = jnp.sum(picks * (2 ** jnp.arange(pairs, dtype=jnp.int32)), axis=-1)
    tag = (jnp.repeat(code, TILE, axis=1) * rows + place + 1).astype(jnp.float32)
    slot_ids = jnp.arange(slots, dtype=jnp.int32)
    row_ids = jnp.arange(rows, dtype=jnp.int32)
    goes = slot[:, None, :] == slot_ids[None, :, None]
    source = jnp.sum(jnp.where(goes, row_ids, 0), axis=2, dtype=jnp.int32)
    tags = jnp.sum(jnp.where(goes, tag[:, None, :], 0.0), axis=2)
    scale = jnp.max(jnp.abs(schur), axis=2) * (1.0 / TOP)
    scales = jnp.sum(jnp.where(goes, scale[:, None, :], 0.0), axis=2)
    notes = lax.all_gather(jnp.stack([tags, scales]), "row", axis=0)
    notes = lax.dynamic_slice_in_dim(notes, me * cap, cap, axis=3)
    notes = notes.transpose(1, 2, 0, 3).reshape(2, children, slots)
    got_tags = notes[0].astype(jnp.int32)
    got_place = jnp.where(got_tags > 0, (got_tags - 1) % rows, rows)
    got_code = ((got_tags - 1) // rows).astype(jnp.float32)
    got_scale = notes[1]

    def to_parents(x, per_slot):
        shape = (count, x.shape[0] // count) + x.shape[1:]
        return lax.all_to_all(x.reshape(shape), "row", split_axis=0, concat_axis=0, tiled=True).reshape(x.shape)

    sent_lower = lower_pack(lower, picks, slot, slots)
    got_lower = lax.all_to_all(
        sent_lower.reshape(children, count, cap, -1), "row", split_axis=1, concat_axis=1, tiled=True
    ).reshape(sent_lower.shape)
    sent = [pack(schur[0], source[0], sent_lower)]
    sent.append(pack(schur[1], source[1], sent[0]))
    got = [to_parents(gate(sent[0], got_lower, relay.up, relay.down), 1)]
    relay.step()
    got.append(to_parents(gate(sent[1], got[0], relay.up, relay.down), 1))

    full = lower_unpack(got_lower, got_place, got_code, rows)
    full = lax.all_gather(full, "col", axis=2, tiled=True)
    depth = upper.shape[1]
    lefts, rights = [], []
    for owner, block in relay.blocks():
        for child in range(children):
            lefts.append(lax.dynamic_slice_in_dim(full[child], owner * depth, depth, axis=1))
            rights.append(block[child])
    result = front - jnp.dot(
        jnp.concatenate(lefts, axis=1), jnp.concatenate(rights, axis=0), preferred_element_type=jnp.float32
    )
    for child in range(children):
        result = unpack(got[child], got_place[child], got_scale[child], result)
    return result


def solution(mesh):
    in_specs = (
        P(None, "row", "col"),
        P(None, "row", "col"),
        P(None, "row", "col"),
        P(None, "row", "col"),
        P(None, "row"),
        P("row", "col"),
    )
    out_specs = P("row", "col")
    return jax.shard_map(shards, mesh=mesh, in_specs=in_specs, out_specs=out_specs, check_vma=False)
```

time: 545 us -> 365 us (0.67)
  waiting for transfers between devices: 407 us -> 129 us
  blocking collectives: 0 us -> 49.3 us
  Pallas kernels: 0 us -> 47.2 us
  starting transfers between devices: 21.3 us -> 58.5 us
  other arithmetic: 46.6 us -> 17.2 us
  matrix products: 16.8 us -> 10.3 us
    all_to_all x4 -> x3, waiting for transfers between devices: 249 us -> 34.7 us  [the longest x2 34.7 us: to_parents(): lax.all_to_all(x.reshape(shape), 'row', split_axis=0, concat_axis=0, tile...]
    all_gather x2 -> x1, waiting for transfers between devices: 158 us -> 0.01 us  [shards(): full = lax.all_gather(full, 'col', axis=2, tiled=True)]
    ppermute x0 -> x13, waiting for transfers between devices: none -> 94.2 us  [send(): return lax.ppermute(x, 'row', pairs)]
    all_gather x0 -> x1, blocking collectives: none -> 49.3 us  [shards(): notes = lax.all_gather(jnp.stack([tags, scales]), 'row', axis=0)]
    pallas_call x0 -> x8, Pallas kernels: none -> 47.2 us  [the longest x2 21 us: unpack(): pl.pallas_call(functools.partial(unpack_kernel, groups, steps), out_shape...]
    scatter-add x2 -> x0, other arithmetic: 37.6 us -> none  [assemble(): return result.at[index].add(values.reshape(-1, width), mode='drop')]
    ppermute x0 -> x13, starting transfers between devices: none -> 21.1 us  [send(): return lax.ppermute(x, 'row', pairs)]
    all_to_all x4 -> x3, starting transfers between devices: 21.2 us -> 37.4 us  [the longest x2 30.1 us: to_parents(): lax.all_to_all(x.reshape(shape), 'row', split_axis=0, concat_axis=0, tile...]
  transfers between devices with their start and end apart: 6 -> 17, of which waited for: 5 -> 6; matrix products, arithmetic and copies ran while one was open for 13% -> 14% of each run, Pallas kernels for 0% -> 8%
where the time goes in v2:
time: 365 us; the launch traced here: 363 us
  waiting for transfers between devices  129 us (35%)
  starting transfers between devices  58.5 us (16%)
  blocking collectives  49.3 us (14%)
  Pallas kernels  47.2 us (13%)
  local copies, waits for them, and re-layouts  37.4 us (10%)
  other arithmetic  17.2 us (5%)
  between operations  14.2 us (4%)
  matrix products  10.3 us (3%)
    ppermute x13, waiting for transfers between devices, send(): return lax.ppermute(x, 'row', pairs)  94.2 us
    all_gather x1, blocking collectives, shards(): notes = lax.all_gather(jnp.stack([tags, scales]), 'row', axis=0)  49.3 us
    all_to_all x2, waiting for transfers between devices, to_parents(): lax.all_to_all(x.reshape(shape), 'row', split_axis=0, concat_axis=0, tile...  34.7 us
    all_to_all x2, starting transfers between devices, to_parents(): lax.all_to_all(x.reshape(shape), 'row', split_axis=0, concat_axis=0, tile...  30.1 us
    ppermute x13, starting transfers between devices, send(): return lax.ppermute(x, 'row', pairs)  21.1 us
    pallas_call x2, Pallas kernels, unpack(): pl.pallas_call(functools.partial(unpack_kernel, groups, steps), out_shape...  21 us
    unnamed x55, local copies, waits for them, and re-layouts  18.3 us
    pallas_call x2, Pallas kernels, pack(): pl.pallas_call(functools.partial(pack_kernel, groups, steps), out_shape=j...  17.3 us
  transfers between devices with their start and end apart: 17, of which 6 were waited for; matrix products, arithmetic and copies ran while one was open for 14% of the time, Pallas kernels for 8%

profile of v2, /device:TPU:0, one launch (start us, length us, event | category | flops | bytes accessed | tf_op | source)
XLA Modules:
  0.0 363.0 jit_solution(7077199085104335301)
XLA Ops:
  6.5 0.7 slice.133
  7.5 0.7 iota_compare_fusion.1
  8.2 0.7 and_select_fusion.4
  8.9 1.9 convert_reduce_fusion
  10.9 1.6 copy-done.5
  12.5 4.5 %lower_pack.1.first = bf16[2,1536,256]{2,1,0:T(8,128)(2,1)S(1)} custom-call(s32[32]{0:T(128)S(1)} %reshape_squeeze.3.picks, bf16[2,1024,512]{2,1,0:T(8,128)(2,1)S(1)} %copy-done.5, s32[2,1,1024]{2,1,0:T(1,128)S(1)} %broadcast_in_dim.54.slot), custom_call_target="tpu_custom_call" | custom-call | tf_op jit(solution)/shard_map/lower_pack/pallas_call | solution.py:189
  17.0 1.3 copy.38
  18.3 1.2 copy-done.3
  19.5 7.3 %all-to-all-start = ((bf16[2,8,192,256]{3,2,0,1:T(8,128)(2,1)}), bf16[2,8,192,256]{3,2,0,1:T(8,128)(2,1)S(1)}, u32[]{:S(2)}, u32[]{:S(2)}) async-start(bf16[2,8,192,256]{3,2,0,1:T(8,128)(2,1)} %copy.38), calls=%async_computation | async-start | bytes 3145728 | tf_op jit(solution)/shard_map/all_to_all | solution.py:330
  26.8 4.1 %abs_reduce_fusion = f32[2,1024]{1,0:T(2,128)S(1)} fusion(f32[2,1024,1024]{2,1,0:T(8,128)} %param.6), kind=kLoop, calls=%fused_computation.4 | loop fusion | flops 4192256 | bytes 8396800 | tf_op jit(solution)/shard_map/reduce_max | solution.py:315
  30.9 3.9 %select_reduce_fusion.2 = (f32[2,1536]{1,0:T(2,128)S(1)}, f32[2,1536]{1,0:T(2,128)S(1)}) fusion(f32[2,1024]{1,0:T(2,128)S(1)} %get-tuple-element.20, s32[2,1024]{1,0:T(2,128)S(1)} %multiply_add_fusion, f32[2,1024]{1,0:T(2,128)S(1)} %broadcast_multiply_fusion), kind=kLoop, calls=%fused_computation.2 | loop fusion | flops 15722496 | bytes 49152 | tf_op jit(solution)/shard_map/reduce_sum | solution.py:314
  34.8 49.3 %all-gather = f32[16,2,1536]{2,1,0:T(2,128)S(1)} all-gather(f32[2,2,1536]{2,1,0:T(2,128)S(1)} %pad_maximum_fusion), channel_id=2, replica_groups=mesh['row'=8,'col'=4] {'row'}, dimensions={0}, use_global_device_ids=true | all-gather | bytes 221184 | tf_op jit(solution)/shard_map/all_gather | solution.py:317
  84.1 0.1 constant_dynamic-slice_fusion
  84.4 0.1 fusion.19
  84.6 0.1 copy.39
  84.7 4.4 %lower_unpack.1 = bf16[2,1024,512]{2,1,0:T(8,128)(2,1)} custom-call(bf16[2,1536,256]{2,1,0:T(8,128)(2,1)S(1)} %bitcast.135, s32[2,1,1536]{2,1,0:T(1,128)S(1)} %get-tuple-element.18.place, f32[2,1,1536]{2,1,0:T(1,128)S(1)} %get-tuple-element.17.code), custom_call_target="tpu_custom_call" | custom-call | tf_op jit(solution)/shard_map/lower_unpack/pallas_call | solution.py:233
  89.1 1.2 copy-done.2
  90.3 1.3 collective-permute-start.1
  91.6 5.5 %collective-permute-start = (bf16[2,256,1024]{2,1,0:T(8,128)(2,1)}, bf16[2,256,1024]{2,1,0:T(8,128)(2,1)}, u32[]{:S(2)}, u32[]{:S(2)}) collective-permute-start(bf16[2,256,1024]{2,1,0:T(8,128)(2,1)} %param.8), channel_id=1, source_target_pairs={{0,8},{4,12},{8,16},{12,20},{16,24},{20,28},{1,9},{5,13},{9,17},{1... | collective-permute-start | bytes 3145736 | tf_op jit(solution)/shard_map/ppermute | solution.py:254
  97.3 10.2 %slice_bitcast_fusion = (f32[1024,1024]{1,0:T(8,128)}, f32[1024,1024]{1,0:T(8,128)}) fusion(f32[2,1024,1024]{2,1,0:T(8,128)} %param.6), kind=kLoop, calls=%fused_computation.6 | loop fusion | bytes 16777216 | tf_op jit(solution)/shard_map/squeeze | solution.py:333
  107.6 6.1 %collective-permute-done.1.refs_3_ = bf16[2,256,1024]{2,1,0:T(8,128)(2,1)} collective-permute-done((bf16[2,256,1024]{2,1,0:T(8,128)(2,1)}, bf16[2,256,1024]{2,1,0:T(8,128)(2,1)}, u32[]{:S(2)}, u32[]{:S(2)}) %collective-permute-start.1) | collective-permute-done | bytes 1048608 | tf_op jit(solution)/shard_map/ppermute | solution.py:254
  113.6 1.3 collective-permute-start.3
  114.9 1.5 select_reduce_fusion
  116.5 8.7 %pack.2.first = s16[768,16,128]{2,1,0:T(8,128)(2,1)S(1)} custom-call(s32[1536]{0:T(1024)S(1)} %get-tuple-element.7.source, f32[1024,1024]{1,0:T(8,128)} %get-tuple-element.13.x, bf16[2,1536,256]{2,1,0:T(8,128)(2,1)S(1)} %copy-done.4), custom_call_target="tpu_custom_call" | custom-call | flops 8388608 | bytes 7340032 | tf_op jit(solution)/shard_map/pack/pallas_call | solution.py:83
  125.2 1.8 copy.48.refs_0_
  127.0 0.9 copy-done
  127.9 4.5 %all-to-all-start.1 = ((s16[8,96,16,128]{3,2,1,0:T(8,128)(2,1)}), s16[8,96,16,128]{3,2,1,0:T(8,128)(2,1)}, u32[]{:S(2)}, u32[]{:S(2)}) async-start(s16[8,96,16,128]{3,2,1,0:T(8,128)(2,1)} %bitcast.139), calls=%async_computation.1 | async-start | bytes 6291456 | tf_op jit(solution)/shard_map/all_to_all | solution.py:327
  132.4 0.9 collective-permute-start.2
  133.6 8.7 %pack.3.refs_0_ = s16[768,16,128]{2,1,0:T(8,128)(2,1)S(1)} custom-call(s32[1536]{0:T(1024)S(1)} %get-tuple-element.8.source, f32[1024,1024]{1,0:T(8,128)} %get-tuple-element.14.x, s16[768,16,128]{2,1,0:T(8,128)(2,1)} %copy-done), custom_call_target="tpu_custom_call" | custom-call | flops 8388608 | bytes 7340032 | tf_op jit(solution)/shard_map/pack/pallas_call | solution.py:83
  142.3 1.5 bitcast_dynamic-update-slice_fusion.1
  143.8 1.8 collective-permute-done.3.refs_3_
  145.5 1.3 collective-permute-start.5
  146.8 1.1 bitcast_dynamic-update-slice_fusion
  147.9 0.7 collective-permute-start.6
  148.6 1.1 fusion.13
  149.7 1.1 fusion.12
  150.8 2.0 collective-permute-start.9
  152.9 0.7 collective-permute-start.8
  153.6 0.7 collective-permute-start.10
  154.3 1.4 broadcast_select_fusion.3
  155.7 52.1 %collective-permute-done.5 = bf16[2,256,1024]{2,1,0:T(8,128)(2,1)S(1)} collective-permute-done((bf16[2,256,1024]{2,1,0:T(8,128)(2,1)}, bf16[2,256,1024]{2,1,0:T(8,128)(2,1)S(1)}, u32[]{:S(2)}, u32[]{:S(2)}) %collective-permute-start.5) | collective-permute-done | bytes 1048608 | tf_op jit(solution)/shard_map/ppermute | solution.py:254
  207.8 1.9 collective-permute-start.7
  209.7 0.1 broadcast_select_fusion.5
  209.9 3.9 %collective-permute-start.12 = (bf16[2,256,1024]{2,1,0:T(8,128)(2,1)}, bf16[2,256,1024]{2,1,0:T(8,128)(2,1)S(1)}, u32[]{:S(2)}, u32[]{:S(2)}) collective-permute-start(bf16[2,256,1024]{2,1,0:T(8,128)(2,1)} %collective-permute-done.1.refs_3_), channel_id=1, source_target_pairs={{0,4},{4,0},{8,12},{12,8},{16,20},{20,16},{1,5},{5,1},{9,13},{13,9... | collective-permute-start | bytes 3145736 | tf_op jit(solution)/shard_map/ppermute | solution.py:254
  213.9 1.3 broadcast_select_fusion.1
  215.2 0.7 collective-permute-start.11
  216.0 0.1 broadcast_select_fusion.2
  216.1 19.6 %collective-permute-done.7 = bf16[2,256,1024]{2,1,0:T(8,128)(2,1)S(1)} collective-permute-done((bf16[2,256,1024]{2,1,0:T(8,128)(2,1)S(1)}, bf16[2,256,1024]{2,1,0:T(8,128)(2,1)S(1)}, u32[]{:S(2)}, u32[]{:S(2)}) %collective-permute-start.7) | collective-permute-done | bytes 1048608 | tf_op jit(solution)/shard_map/ppermute | solution.py:254
  235.8 0.1 broadcast_select_fusion.4
  236.3 14.6 %collective-permute-done.12 = bf16[2,256,1024]{2,1,0:T(8,128)(2,1)S(1)} collective-permute-done((bf16[2,256,1024]{2,1,0:T(8,128)(2,1)}, bf16[2,256,1024]{2,1,0:T(8,128)(2,1)S(1)}, u32[]{:S(2)}, u32[]{:S(2)}) %collective-permute-start.12) | collective-permute-done | bytes 1048608 | tf_op jit(solution)/shard_map/ppermute | solution.py:254
  250.9 1.1 broadcast_select_fusion
  252.0 25.6 %all-to-all-start.2 = ((s16[8,96,16,128]{3,2,1,0:T(8,128)(2,1)}), s16[8,96,16,128]{3,2,1,0:T(8,128)(2,1)S(1)}, u32[]{:S(2)}, u32[]{:S(2)}) async-start(s16[8,96,16,128]{3,2,1,0:T(8,128)(2,1)} %bitcast.134), calls=%async_computation.2 | async-start | bytes 6291456 | tf_op jit(solution)/shard_map/all_to_all | solution.py:327
  277.6 1.9 fusion.1
  279.5 1.9 fusion
  281.3 4.0 %fusion.23 = (bf16[1,1024,2048]{2,1,0:T(8,128)(2,1)S(1)}, bf16[1,1024,2048]{2,1,0:T(8,128)(2,1)S(1)}) fusion(bf16[2,1024,2048]{2,1,0:T(8,128)(2,1)} %all-gather.3.cloned.1.call-done), kind=kLoop, calls=%fused_computation.109 | loop fusion | bytes 16777216 | tf_op jit(solution)/shard_map/slice | solution.py:345
  285.4 0.1 bitcast_dynamic-update-slice_fusion.17
  286.0 0.1 bitcast_dynamic-update-slice_fusion.10
  286.8 0.7 slice-done
  287.5 1.3 copy-done.8
  288.8 1.4 slice-done.1
  290.2 10.3 %convolution_subtract_fusion.before = f32[1024,1024]{1,0:T(8,128)} fusion(f32[1024,1024]{1,0:T(8,128)S(1)} %copy-done.8, bf16[1024,4096]{1,0:T(8,128)(2,1)S(1)} %bitcast_dynamic-update-slice_fusion.2, bf16[4096,1024]{1,0:T(8,128)(2,1)S(1)} %bitcast.145), kind=kOutput, calls=%fused_computation.9 | convolution fusion | flops 8590983168 | bytes 25165824 | tf_op jit(solution)/shard_map/dot_general | solution.py:347
  300.5 11.5 %unpack.2.before = f32[1024,1024]{1,0:T(8,128)} custom-call(s32[1536]{0:T(1024)S(1)} %get-tuple-element.5.place, f32[1536]{0:T(1024)S(1)} %squeeze.101.scale, s16[768,16,128]{2,1,0:T(8,128)(2,1)} %bitcast.11.refs_1_.got, f32[1024,1024]{1,0:T(8,128)} %convolution_subtract_fusion.before), custom_call_target="tpu_custom_call" | custom-call | flops 4194304 | bytes 11534336 | tf_op jit(solution)/shard_map/unpack/pallas_call | solution.py:144
  312.0 34.7 %all-to-all-done.2 = s16[8,96,16,128]{3,2,1,0:T(8,128)(2,1)S(1)} async-done(((s16[8,96,16,128]{3,2,1,0:T(8,128)(2,1)}), s16[8,96,16,128]{3,2,1,0:T(8,128)(2,1)S(1)}, u32[]{:S(2)}, u32[]{:S(2)}) %all-to-all-start.2) | async-done | bytes 3145760 | tf_op jit(solution)/shard_map/all_to_all | solution.py:327
  346.7 9.5 %unpack.3 = f32[1024,1024]{1,0:T(8,128)} custom-call(s32[1536]{0:T(1024)S(1)} %get-tuple-element.6.place, f32[1536]{0:T(1024)S(1)} %squeeze.95.scale, s16[768,16,128]{2,1,0:T(8,128)(2,1)S(1)} %bitcast.138, f32[1024,1024]{1,0:T(8,128)} %unpack.2.before), custom_call_target="tpu_custom_call" | custom-call | flops 4194304 | bytes 11534336 | tf_op jit(solution)/shard_map/unpack/pallas_call | solution.py:144
  (80 shorter events, 2.6 us)
Async XLA Ops:
  10.9 1.6 copy-start.5
  18.3 1.2 copy-start.3
  19.5 65.0 %all-to-all-start = ((bf16[2,8,192,256]{3,2,0,1:T(8,128)(2,1)}), bf16[2,8,192,256]{3,2,0,1:T(8,128)(2,1)S(1)}, u32[]{:S(2)}, u32[]{:S(2)}) async-start(bf16[2,8,192,256]{3,2,0,1:T(8,128)(2,1)} %copy.38), calls=%async_computation | async-start | bytes 3145728 | tf_op jit(solution)/shard_map/all_to_all | solution.py:330
  26.8 254.6 %all-gather.3.cloned.1.call-start = ((), (), s32[]{:S(2)}) async-start(), calls=%async_computation.3 | async-start | bytes 10485760 | tf_op jit(solution)/shard_map/all_gather | solution.py:340
  89.1 1.2 copy-start.2
  90.3 23.3 %collective-permute-start.1 = (bf16[2,256,1024]{2,1,0:T(8,128)(2,1)}, bf16[2,256,1024]{2,1,0:T(8,128)(2,1)}, u32[]{:S(2)}, u32[]{:S(2)}) collective-permute-start(bf16[2,256,1024]{2,1,0:T(8,128)(2,1)} %param.8), channel_id=1, source_target_pairs={{8,0},{12,4},{16,8},{20,12},{24,16},{28,20},{9,1},{13,5},{17,9},{2... | collective-permute-start | bytes 3145736 | tf_op jit(solution)/shard_map/ppermute | solution.py:254
  91.6 35.4 %collective-permute-start = (bf16[2,256,1024]{2,1,0:T(8,128)(2,1)}, bf16[2,256,1024]{2,1,0:T(8,128)(2,1)}, u32[]{:S(2)}, u32[]{:S(2)}) collective-permute-start(bf16[2,256,1024]{2,1,0:T(8,128)(2,1)} %param.8), channel_id=1, source_target_pairs={{0,8},{4,12},{8,16},{12,20},{16,24},{20,28},{1,9},{5,13},{9,17},{1... | collective-permute-start | bytes 3145736 | tf_op jit(solution)/shard_map/ppermute | solution.py:254
  97.1 51.5 %collective-permute-start.4 = (bf16[2,256,1024]{2,1,0:T(8,128)(2,1)}, bf16[2,256,1024]{2,1,0:T(8,128)(2,1)}, u32[]{:S(2)}, u32[]{:S(2)}) collective-permute-start(bf16[2,256,1024]{2,1,0:T(8,128)(2,1)} %param.8), channel_id=1, source_target_pairs={{0,4},{4,0},{8,12},{12,8},{16,20},{20,16},{24,28},{28,24},{1,5},{5... | collective-permute-start | bytes 3145736 | tf_op jit(solution)/shard_map/ppermute | solution.py:254
  97.3 19.2 %copy-start.4 = (bf16[2,1536,256]{2,1,0:T(8,128)(2,1)S(1)}, bf16[2,1536,256]{2,1,0:T(8,128)(2,1)}, u32[]{:S(2)}) copy-start(bf16[2,1536,256]{2,1,0:T(8,128)(2,1)} %copy-done.3) | copy-start | bytes 4718596
  113.6 31.9 %collective-permute-start.3 = (bf16[2,256,1024]{2,1,0:T(8,128)(2,1)}, bf16[2,256,1024]{2,1,0:T(8,128)(2,1)}, u32[]{:S(2)}, u32[]{:S(2)}) collective-permute-start(bf16[2,256,1024]{2,1,0:T(8,128)(2,1)} %collective-permute-done.1.refs_3_), channel_id=1, source_target_pairs={{8,0},{12,4},{16,8},{20,12},{9,1},{13,5},{17,9},{21,13},{10,2},{14... | collective-permute-start | bytes 3145736 | tf_op jit(solution)/shard_map/ppermute | solution.py:254
  125.2 2.7 copy-start
  127.9 124.1 %all-to-all-start.1 = ((s16[8,96,16,128]{3,2,1,0:T(8,128)(2,1)}), s16[8,96,16,128]{3,2,1,0:T(8,128)(2,1)}, u32[]{:S(2)}, u32[]{:S(2)}) async-start(s16[8,96,16,128]{3,2,1,0:T(8,128)(2,1)} %bitcast.139), calls=%async_computation.1 | async-start | bytes 6291456 | tf_op jit(solution)/shard_map/all_to_all | solution.py:327
  132.4 20.5 %collective-permute-start.2 = (bf16[2,256,1024]{2,1,0:T(8,128)(2,1)}, bf16[2,256,1024]{2,1,0:T(8,128)(2,1)S(1)}, u32[]{:S(2)}, u32[]{:S(2)}) collective-permute-start(bf16[2,256,1024]{2,1,0:T(8,128)(2,1)} %collective-permute-done.refs_2_), channel_id=1, source_target_pairs={{8,16},{12,20},{16,24},{20,28},{9,17},{13,21},{17,25},{21,29},{10,... | collective-permute-start | bytes 3145736 | tf_op jit(solution)/shard_map/ppermute | solution.py:254
  142.3 73.8 %copy-start.1 = (s16[768,16,128]{2,1,0:T(8,128)(2,1)}, s16[768,16,128]{2,1,0:T(8,128)(2,1)S(1)}, u32[]{:S(2)}) copy-start(s16[768,16,128]{2,1,0:T(8,128)(2,1)S(1)} %pack.3.refs_0_) | copy-start | bytes 9437188
  145.5 62.3 %collective-permute-start.5 = (bf16[2,256,1024]{2,1,0:T(8,128)(2,1)}, bf16[2,256,1024]{2,1,0:T(8,128)(2,1)S(1)}, u32[]{:S(2)}, u32[]{:S(2)}) collective-permute-start(bf16[2,256,1024]{2,1,0:T(8,128)(2,1)} %collective-permute-done.3.refs_3_), channel_id=1, source_target_pairs={{8,0},{12,4},{9,1},{13,5},{10,2},{14,6},{11,3},{15,7}} | collective-permute-start | bytes 3145736 | tf_op jit(solution)/shard_map/ppermute | solution.py:254
  147.9 68.2 %collective-permute-start.6 = (bf16[2,256,1024]{2,1,0:T(8,128)(2,1)}, bf16[2,256,1024]{2,1,0:T(8,128)(2,1)S(1)}, u32[]{:S(2)}, u32[]{:S(2)}) collective-permute-start(bf16[2,256,1024]{2,1,0:T(8,128)(2,1)} %collective-permute-done.refs_2_), channel_id=1, source_target_pairs={{8,12},{12,8},{16,20},{20,16},{24,28},{28,24},{9,13},{13,9},{17,21... | collective-permute-start | bytes 3145736 | tf_op jit(solution)/shard_map/ppermute | solution.py:254
  150.8 65.2 %collective-permute-start.9 = (bf16[2,256,1024]{2,1,0:T(8,128)(2,1)}, bf16[2,256,1024]{2,1,0:T(8,128)(2,1)S(1)}, u32[]{:S(2)}, u32[]{:S(2)}) collective-permute-start(bf16[2,256,1024]{2,1,0:T(8,128)(2,1)} %collective-permute-done.3.refs_3_), channel_id=1, source_target_pairs={{0,4},{4,0},{8,12},{12,8},{1,5},{5,1},{9,13},{13,9},{2,6},{6,2},{1... | collective-permute-start | bytes 3145736 | tf_op jit(solution)/shard_map/ppermute | solution.py:254
  152.9 83.0 %copy-start.6 = (bf16[2,256,1024]{2,1,0:T(8,128)(2,1)}, bf16[2,256,1024]{2,1,0:T(8,128)(2,1)S(1)}, u32[]{:S(2)}) copy-start(bf16[2,256,1024]{2,1,0:T(8,128)(2,1)S(1)} %collective-permute-done.2.refs_2_) | copy-start | bytes 3145732
  152.9 62.4 %collective-permute-start.8 = (bf16[2,256,1024]{2,1,0:T(8,128)(2,1)S(1)}, bf16[2,256,1024]{2,1,0:T(8,128)(2,1)S(1)}, u32[]{:S(2)}, u32[]{:S(2)}) collective-permute-start(bf16[2,256,1024]{2,1,0:T(8,128)(2,1)S(1)} %collective-permute-done.2.refs_2_), channel_id=1, source_target_pairs={{16,20},{20,16},{24,28},{28,24},{17,21},{21,17},{25,29},{29,25},{1... | collective-permute-start | bytes 3145736 | tf_op jit(solution)/shard_map/ppermute | solution.py:254
  153.6 56.3 %collective-permute-start.10 = (bf16[2,256,1024]{2,1,0:T(8,128)(2,1)S(1)}, bf16[2,256,1024]{2,1,0:T(8,128)(2,1)S(1)}, u32[]{:S(2)}, u32[]{:S(2)}) collective-permute-start(bf16[2,256,1024]{2,1,0:T(8,128)(2,1)S(1)} %collective-permute-done.2.refs_2_), channel_id=1, source_target_pairs={{16,24},{20,28},{17,25},{21,29},{18,26},{22,30},{19,27},{23,31}} | collective-permute-start | bytes 3145736 | tf_op jit(solution)/shard_map/ppermute | solution.py:254
  207.8 28.0 %collective-permute-start.7 = (bf16[2,256,1024]{2,1,0:T(8,128)(2,1)S(1)}, bf16[2,256,1024]{2,1,0:T(8,128)(2,1)S(1)}, u32[]{:S(2)}, u32[]{:S(2)}) collective-permute-start(bf16[2,256,1024]{2,1,0:T(8,128)(2,1)S(1)} %collective-permute-done.5), channel_id=1, source_target_pairs={{0,4},{4,0},{1,5},{5,1},{2,6},{6,2},{3,7},{7,3}} | collective-permute-start | bytes 3145736 | tf_op jit(solution)/shard_map/ppermute | solution.py:254
  209.9 40.9 %collective-permute-start.12 = (bf16[2,256,1024]{2,1,0:T(8,128)(2,1)}, bf16[2,256,1024]{2,1,0:T(8,128)(2,1)S(1)}, u32[]{:S(2)}, u32[]{:S(2)}) collective-permute-start(bf16[2,256,1024]{2,1,0:T(8,128)(2,1)} %collective-permute-done.1.refs_3_), channel_id=1, source_target_pairs={{0,4},{4,0},{8,12},{12,8},{16,20},{20,16},{1,5},{5,1},{9,13},{13,9... | collective-permute-start | bytes 3145736 | tf_op jit(solution)/shard_map/ppermute | solution.py:254
  215.2 35.7 %collective-permute-start.11 = (bf16[2,256,1024]{2,1,0:T(8,128)(2,1)S(1)}, bf16[2,256,1024]{2,1,0:T(8,128)(2,1)S(1)}, u32[]{:S(2)}, u32[]{:S(2)}) collective-permute-start(bf16[2,256,1024]{2,1,0:T(8,128)(2,1)S(1)} %collective-permute-done.10), channel_id=1, source_target_pairs={{24,28},{28,24},{25,29},{29,25},{26,30},{30,26},{27,31},{31,27}} | collective-permute-start | bytes 3145736 | tf_op jit(solution)/shard_map/ppermute | solution.py:254
  236.3 14.6 %copy-start.7 = (bf16[4096,1024]{1,0:T(8,128)(2,1)}, bf16[4096,1024]{1,0:T(8,128)(2,1)S(1)}, u32[]{:S(2)}) copy-start(bf16[4096,1024]{1,0:T(8,128)(2,1)S(1)} %fusion.2) | copy-start | bytes 25165828
  252.0 94.7 %all-to-all-start.2 = ((s16[8,96,16,128]{3,2,1,0:T(8,128)(2,1)}), s16[8,96,16,128]{3,2,1,0:T(8,128)(2,1)S(1)}, u32[]{:S(2)}, u32[]{:S(2)}) async-start(s16[8,96,16,128]{3,2,1,0:T(8,128)(2,1)} %bitcast.134), calls=%async_computation.2 | async-start | bytes 6291456 | tf_op jit(solution)/shard_map/all_to_all | solution.py:327
  285.3 2.2 slice-start
  285.4 3.5 copy-start.8
  286.0 4.2 %slice-start.1 = ((s8[8388608]{0:T(1024)(128)(4,1)}), s8[4194304]{0:T(1024)(128)(4,1)S(1)}, s32[]{:S(2)}) async-start(s8[8388608]{0:T(1024)(128)(4,1)} %bitcast.144), calls=%async_computation.5 | async-start | bytes 8388608
Sparse Core Ops, SparseCore 0:
  90.4 57.3 all-gather.2

commit v3 on v0

v3 whole, which is shorter than its diff:
```python
import functools
import math

import jax
import jax.numpy as jnp
from jax import lax
from jax.experimental import pallas as pl
from jax.experimental.pallas import tpu as pltpu
from jax.sharding import PartitionSpec as P

TILE = 128
LANES = 128
TOP = 32767.0
FINE = 256
LEAST = 1e-30
VMEM_LIMIT = 56 * 1024 * 1024
ANY = pl.BlockSpec(memory_space=pl.ANY)


def inner_factor(count):
    inner = 1
    while (2 * inner) * (2 * inner) <= count:
        inner *= 2
    return inner


def takes(us):
    return pl.CostEstimate(flops=int(us * 4e9), bytes_accessed=int(us * 3.3e6), transcendentals=0)


def gate_kernel(*refs):
    pass


def gate(arrays, *first):
    count = len(arrays)
    return pl.pallas_call(
        gate_kernel,
        out_shape=[jax.ShapeDtypeStruct(x.shape, x.dtype) for x in arrays],
        in_specs=[ANY] * (count + len(first)),
        out_specs=[ANY] * count,
        input_output_aliases={i: i for i in range(count)},
        name="gate",
    )(*arrays, *first)


def unit_of(code):
    return jnp.exp(code * (math.log(2.0) / FINE))


def mask_kernel(mask, low, out):
    c = pl.program_id(0)
    _, rows, depth = low.shape
    row_tiles, tiles = rows // TILE, depth // TILE
    for i in range(row_tiles):
        for j in range(tiles):
            at = (0, slice(i * TILE, (i + 1) * TILE), slice(j * TILE, (j + 1) * TILE))
            keep = mask[(c * row_tiles + i) * tiles + j] != 0

            @pl.when(keep)
            def _():
                out[at] = low[at]

            @pl.when(jnp.logical_not(keep))
            def _():
                out[at] = jnp.zeros((TILE, TILE), out.dtype)


def mask_tiles(lower, mask):
    children, rows, depth = lower.shape
    block = pl.BlockSpec((1, rows, depth), lambda c, m: (c, 0, 0))
    return pl.pallas_call(
        mask_kernel,
        out_shape=jax.ShapeDtypeStruct(lower.shape, lower.dtype),
        grid_spec=pltpu.PrefetchScalarGridSpec(
            num_scalar_prefetch=1, grid=(children,), in_specs=[block], out_specs=block
        ),
        compiler_params=pltpu.CompilerParams(vmem_limit_bytes=VMEM_LIMIT),
        cost_estimate=takes(4),
        name="mask_tiles",
    )(mask.reshape(-1), lower)


def send_kernel(groups, steps, parts, blocks, source, starts, slot, notes, schur, *refs):
    lows, ups = refs[:parts], refs[parts : parts + blocks]
    out, low_all, up_all, total, scale, held, codes, sems = refs[parts + blocks :]
    i = pl.program_id(0)
    rows, width = schur.shape[1:]
    targets, tiles = out.shape[0], out.shape[1] - 1
    per = 16 // groups
    stride = codes.shape[1] // (targets * (pl.num_programs(0) - steps))

    @pl.when(i == 0)
    def _():
        copies = []
        for n, low in enumerate(lows):
            at = pl.ds(pl.multiple_of(starts[n], low.shape[1]), low.shape[1])
            copies.append(pltpu.make_async_copy(low, low_all.at[:, at], sems.at[n]))
        for n, up in enumerate(ups):
            at = pl.ds(pl.multiple_of(starts[parts + n], up.shape[0]), up.shape[0])
            copies.append(pltpu.make_async_copy(up, up_all.at[at], sems.at[parts + n]))
        for copy in copies:
            copy.start()
        codes[...] = jnp.zeros(codes.shape, jnp.float32)
        for copy in copies:
            copy.wait()

    @pl.when(i < steps)
    def _():
        here = pl.ds(pl.multiple_of(i * rows, rows), rows)
        total[...] = schur[0] - jnp.dot(low_all[here, :], up_all[...], preferred_element_type=jnp.float32)
        most = jnp.maximum(jnp.max(jnp.abs(total[...]), axis=1, keepdims=True), LEAST)
        code = jnp.floor(jnp.log(most) * (FINE / math.log(2.0)) - FINE * math.log2(TOP)) + 2.0
        scale[0] = jnp.broadcast_to(1.0 / unit_of(code), (rows, LANES))
        scale[1] = jnp.broadcast_to(code, (rows, LANES))

        def body(g, carry):
            at = pl.multiple_of(g * 8, 8)
            inverse = scale[0, pl.ds(at, 8), :]
            base = (i * rows + at) * groups
            for j in range(groups):
                v = total[pl.ds(at, 8), j * LANES : (j + 1) * LANES]
                held[pl.ds(base + j, 8, stride=groups), :] = jnp.floor(v * inverse + 0.5).astype(jnp.int32)
            return carry

        lax.fori_loop(0, rows // 8, body, 0, unroll=4)

        for lane in range(0, codes.shape[1], 8 * LANES):
            lanes = lax.broadcasted_iota(jnp.int32, (8, 8 * LANES), 1) + lane

            def note(g, carry):
                at = pl.multiple_of(g * 8, 8)
                mine = jnp.concatenate([scale[1, pl.ds(at, 8), :]] * 8, axis=1)
                place = jnp.concatenate([slot[pl.ds(at, 8), :]] * 8, axis=1)
                return carry + jnp.where(place == lanes, mine, 0.0)

            codes[:, lane : lane + 8 * LANES] += lax.fori_loop(
                0, rows // 8, note, jnp.zeros(lanes.shape, jnp.float32), unroll=4
            )

    @pl.when(i >= steps)
    def _():
        for target in range(targets):
            number = (i - steps) * targets + target
            start = number * tiles * per

            def body(t, carry):
                pieces = []
                for a in range(per):
                    row = pl.multiple_of(source[start + t * per + a], groups)
                    pieces.append(held[pl.ds(row, groups), :])
                out[target, t] = jnp.concatenate(pieces, axis=0).astype(jnp.int16)
                return carry

            lax.fori_loop(0, tiles, body, 0, unroll=8)
            tile = notes[target]
            line = lax.broadcasted_iota(jnp.int32, tile.shape, 0)
            mine = jnp.sum(codes[:, pl.ds(pl.multiple_of(number * stride, stride), stride)], axis=0, keepdims=True)
            for a in range(stride // LANES):
                piece = mine[:, a * LANES : (a + 1) * LANES].astype(jnp.int32)
                tile = jnp.where(line == stride // LANES + a, piece, tile)
            out[target, tiles] = tile.astype(jnp.int16)


def send_rows(child, schur, lows, ups, starts, source, slot, notes):
    rows, width = schur.shape[1:]
    count = notes.shape[0]
    cap = source.shape[0] // count
    groups = width // LANES
    tiles = cap * groups // 16
    steps, out_steps = 2, 2
    depth = sum(up.shape[0] for up in ups)
    stride = -(-cap // LANES) * LANES
    first = lambda i, *_: jnp.minimum(i, steps - 1)
    second = lambda i, *_: jnp.maximum(i - steps, 0)
    return pl.pallas_call(
        functools.partial(send_kernel, groups, steps, len(lows), len(ups)),
        out_shape=jax.ShapeDtypeStruct((count, tiles + 1, 16, LANES), jnp.int16),
        grid_spec=pltpu.PrefetchScalarGridSpec(
            num_scalar_prefetch=2,
            grid=(steps + out_steps,),
            in_specs=[
                pl.BlockSpec((rows // steps, LANES), lambda i, *_: (first(i), 0)),
                pl.BlockSpec((count // out_steps, 16, LANES), lambda i, *_: (second(i), 0, 0)),
                pl.BlockSpec((1, rows // steps, width), lambda i, *_: (child, first(i), 0)),
            ]
            + [ANY] * (len(lows) + len(ups)),
            out_specs=pl.BlockSpec((count // out_steps, tiles + 1, 16, LANES), lambda i, *_: (second(i), 0, 0, 0)),
            scratch_shapes=[
                pltpu.VMEM((rows, depth), jnp.bfloat16),
                pltpu.VMEM((depth, width), jnp.bfloat16),
                pltpu.VMEM((rows // steps, width), jnp.float32),
                pltpu.VMEM((2, rows // steps, LANES), jnp.float32),
                pltpu.VMEM((rows * groups, LANES), jnp.int32),
                pltpu.VMEM((8, count * stride), jnp.float32),
                pltpu.SemaphoreType.DMA((len(lows) + len(ups),)),
            ],
        ),
        compiler_params=pltpu.CompilerParams(vmem_limit_bytes=VMEM_LIMIT),
        cost_estimate=takes(14),
        name="send_rows",
    )(source * groups, starts, slot, notes, schur, *lows, *ups)


def receive_kernel(groups, steps, cap, got, notes, before, out, held, plain, size, scale, place, sem):
    i = pl.program_id(0)
    count = notes.shape[0]
    per = 16 // groups
    chunk = 16
    lines = -(-cap // LANES)

    @pl.when(i == 0)
    def _():
        for s in range(count):
            note = notes[s, 0].astype(jnp.int32)
            plain[s * (lines + 1) : (s + 1) * (lines + 1), :] = jnp.concatenate(
                [note[:lines] * groups, note[2 * lines : 2 * lines + 1]], axis=0
            )
            size[s * lines : (s + 1) * lines, :] = unit_of(note[lines : 2 * lines].astype(jnp.float32))
        copy = pltpu.make_async_copy(plain, place, sem)
        copy.start()
        copy.wait()

    def collect(device, s):
        def body(k, carry):
            line = device * (lines + 1) + k // (LANES // chunk)
            lane = k % (LANES // chunk) * chunk
            for t in range(chunk // per):
                v = got[s, k * (chunk // per) + t].astype(jnp.int32).astype(jnp.float32)
                for a in range(per):
                    row = pl.multiple_of(place[line, lane + t * per + a], groups)
                    held[pl.ds(row, groups), :] = v[a * groups : (a + 1) * groups]
            return carry

        lax.fori_loop(0, (place[device * (lines + 1) + lines, 0] + chunk - 1) // chunk, body, 0)

    @pl.when(i < steps)
    def _():
        for s in range(count // steps):
            collect(i * (count // steps) + s, s)

    @pl.when(i >= steps)
    def _():
        rows = out.shape[0]
        start = (i - steps) * rows
        ids = (lax.broadcasted_iota(jnp.int32, (rows, LANES), 0) + start + 1) * groups

        def find(s, carry):
            for a in range(lines):
                here = plain[pl.ds(s * (lines + 1) + a, 1), :] == ids
                carry += jnp.where(here, size[pl.ds(s * lines + a, 1), :], 0.0)
            return carry

        unit = lax.fori_loop(0, count, find, jnp.zeros(ids.shape, jnp.float32))
        scale[...] = jnp.broadcast_to(jnp.sum(unit, axis=1, keepdims=True), scale.shape)

        def body(g, carry):
            at = pl.multiple_of(g * 8, 8)
            unit = scale[pl.ds(at, 8), :]
            for j in range(groups):
                cols = pl.ds(j * LANES, LANES)
                piece = held[pl.ds((start + at + 1) * groups + j, 8, stride=groups), :]
                out[pl.ds(at, 8), cols] = before[pl.ds(at, 8), cols] + piece * unit
            return carry

        lax.fori_loop(0, rows // 8, body, 0, unroll=4)


def receive_rows(got, cap, before):
    rows, width = before.shape
    count, tiles = got.shape[0], got.shape[1] - 1
    groups = width // LANES
    lines = -(-cap // LANES)
    steps, out_steps = count // 2, 2
    block = pl.BlockSpec((rows // out_steps, width), lambda i: (jnp.maximum(i - steps, 0), 0))
    return pl.pallas_call(
        functools.partial(receive_kernel, groups, steps, cap),
        out_shape=jax.ShapeDtypeStruct((rows, width), jnp.float32),
        grid=(steps + out_steps,),
        in_specs=[
            pl.BlockSpec((count // steps, tiles, 16, LANES), lambda i: (jnp.minimum(i, steps - 1), 0, 0, 0)),
            pl.BlockSpec((count, 1, 16, LANES), lambda i: (0, tiles, 0, 0)),
            block,
        ],
        out_specs=block,
        scratch_shapes=[
            pltpu.VMEM(((rows + 1) * groups, LANES), jnp.float32),
            pltpu.VMEM((count * (lines + 1), LANES), jnp.int32),
            pltpu.VMEM((count * lines, LANES), jnp.float32),
            pltpu.VMEM((rows // out_steps, LANES), jnp.float32),
            pltpu.SMEM((count * (lines + 1), LANES), jnp.int32),
            pltpu.SemaphoreType.DMA,
        ],
        compiler_params=pltpu.CompilerParams(vmem_limit_bytes=VMEM_LIMIT),
        cost_estimate=takes(8),
        name="receive_rows",
    )(got, got, before)


class Relay:
    def __init__(self, block, count):
        self.inner = inner_factor(count)
        self.outer = count // self.inner
        self.z = lax.axis_index("row") // self.inner
        self.x = lax.axis_index("row") % self.inner
        self.up = self.down = block
        self.came = {}
        self.order = [
            [(k, d) for k in range(1, self.outer) for d in (1, -1) if 0 <= z - d * k < self.outer]
            for z in range(self.outer)
        ]
        self.held = [[block] + self.exchange(block, range(self.outer))]
        self.k = 0

    def send(self, x, moves, turn=0):
        n = self.inner
        return lax.ppermute(
            x, "row", [(z * n + i, to * n + (i + turn) % n) for z, to in moves.items() for i in range(n)]
        )

    def exchange(self, x, where):
        return [self.send(x, {z: z for z in where}, j) for j in range(1, self.inner)]

    def choose(self, number, where):
        names = {z: self.order[z][number - 1] for z in where}
        every = sorted(set(names.values()))
        block = self.came[every[0]]
        for name in every[1:]:
            here = functools.reduce(jnp.logical_or, [self.z == z for z in where if names[z] == name])
            block = jnp.where(here, self.came[name], block)
        return block

    def step(self):
        if self.k:
            block = self.choose(self.k, range(self.outer))
            self.held.append([block] + self.exchange(block, range(self.outer)))
        self.k += 1
        last = self.outer - 1
        if self.k == last:
            inside = range(1, last)
            block = self.choose(last, inside)
            ends = {1: 0, last - 1: last}
            at_end = (self.z == 0) | (self.z == last)
            others = [block] + self.exchange(block, inside)
            self.held.append(
                [jnp.where(at_end, self.send(block, ends, j), others[j]) for j in range(self.inner)]
            )
            return
        self.up = self.send(self.up, {z: z + 1 for z in range(self.k - 1, last)})
        self.down = self.send(self.down, {z: z - 1 for z in range(1, last - self.k + 2)})
        self.came[self.k, 1], self.came[self.k, -1] = self.up, self.down

    def pass_gate(self, arrays):
        mine = self.held[self.k - 1][1:]
        count = len(mine)
        self.up, self.down, *rest = gate([self.up, self.down, *mine, *arrays])
        self.came[self.k, 1], self.came[self.k, -1] = self.up, self.down
        self.held[self.k - 1][1:] = rest[:count]
        return rest[count:]

    def blocks(self):
        while self.k < self.outer - 1:
            self.step()
        found = []
        for k in range(self.outer):
            at = self.z
            if k:
                at = jnp.array([z - d * far for z, (far, d) in enumerate(o[k - 1] for o in self.order)], jnp.int32)[at]
            for j in range(self.inner):
                found.append((at * self.inner + (self.x - j + self.inner) % self.inner, self.held[k][j]))
        return found


def gather_columns(x):
    size = lax.axis_size("col")
    found = [(0, x)]
    bit = size // 2
    while bit:
        pairs = [(i, i ^ bit) for i in range(size)]
        found += [(far ^ bit, lax.ppermute(y, "col", pairs)) for far, y in found]
        bit //= 2
    return found


def shards(schur, lower, upper, tile_mask, row_map, front):
    children, rows, local_depth = lower.shape
    count = lax.axis_size("row")
    cap = 3 * rows // (2 * count)
    lines = -(-cap // LANES)
    stride = lines * LANES
    depth = upper.shape[1]

    target = row_map // rows
    place = row_map % rows + 1
    earlier = jnp.tril(jnp.ones((rows, rows), jnp.bool_), -1)
    same = target[:, :, None] == target[:, None, :]
    rank = jnp.sum(same & earlier[None], axis=2, dtype=jnp.int32)
    slot = target * stride + rank
    slot_ids = jnp.arange(count * stride, dtype=jnp.int32)
    goes = slot[:, None, :] == slot_ids[None, :, None]
    row_ids = jnp.arange(rows, dtype=jnp.int32)
    source = jnp.sum(jnp.where(goes, row_ids, 0), axis=2, dtype=jnp.int32)
    source = source.reshape(children, count, stride)[:, :, :cap].reshape(children, -1)
    places = jnp.sum(jnp.where(goes, place[:, None, :], 0), axis=2, dtype=jnp.int32)
    places = places.reshape(children, count, lines, LANES)
    amount = jnp.sum(places > 0, axis=(2, 3), keepdims=True, dtype=jnp.int32)
    amount = jnp.broadcast_to(amount, (children, count, 16 - 2 * lines, LANES))
    notes = jnp.concatenate([places, jnp.zeros_like(places), amount], axis=2)

    masked = mask_tiles(lower, tile_mask)
    column = lax.axis_index("col")
    relays = []
    result = front
    got = []
    for child in range(children):
        block = upper[child]
        if relays:
            (block,) = gate([block], relays[-1].up, relays[-1].down)
        relay = Relay(block, count)
        relays.append(relay)
        relay.step()
        parts = gather_columns(masked[child])
        blocks = relay.blocks()
        starts = [(column ^ far) * local_depth for far, _ in parts] + [owner * depth for owner, _ in blocks]
        sent = send_rows(
            child,
            schur,
            [part for _, part in parts],
            [block for _, block in blocks],
            jnp.stack(starts).astype(jnp.int32),
            source[child],
            jnp.broadcast_to(slot[child][:, None], (rows, LANES)),
            notes[child],
        )
        if got:
            (sent,) = gate([sent], got[-1])
        got.append(lax.all_to_all(sent, "row", split_axis=0, concat_axis=0, tiled=True))
    for child in range(children):
        result = receive_rows(got[child], cap, result)
    return result


def solution(mesh):
    in_specs = (
        P(None, "row", "col"),
        P(None, "row", "col"),
        P(None, "row", "col"),
        P(None, "row", "col"),
        P(None, "row"),
        P("row", "col"),
    )
    out_specs = P("row", "col")
    return jax.shard_map(shards, mesh=mesh, in_specs=in_specs, out_specs=out_specs, check_vma=False)
```

time: 545 us -> 320 us (0.59)
  waiting for transfers between devices: 407 us -> 173 us
  Pallas kernels: 0 us -> 58.6 us
  other arithmetic: 46.6 us -> 20.4 us
  starting transfers between devices: 21.3 us -> 46.5 us
  local copies, waits for them, and re-layouts: 38.9 us -> 17 us
  matrix products: 16.8 us -> 0 us
  between operations: 13.6 us -> 2.59 us
    all_to_all x4 -> x2, waiting for transfers between devices: 249 us -> 60.8 us  [shards(): lax.all_to_all(sent, 'row', split_axis=0, concat_axis=0, tiled=True)]
    all_gather x2 -> x0, waiting for transfers between devices: 158 us -> none  [the longest x1 127 us: shards(): upper_full = lax.all_gather(upper, 'row', axis=1, tiled=True)]
    ppermute x0 -> x26, waiting for transfers between devices: none -> 112 us  [the longest x20 107 us: send(): lax.ppermute(x, 'row', [(z * n + i, to * n + (i + turn) % n) for z, to in...]
    pallas_call x0 -> x7, Pallas kernels: none -> 58.6 us  [the longest x2 33.7 us: send_rows(): pl.pallas_call(functools.partial(send_kernel, groups, steps, len(lows), l...]
    scatter-add x2 -> x0, other arithmetic: 37.6 us -> none  [assemble(): return result.at[index].add(values.reshape(-1, width), mode='drop')]
    ppermute x0 -> x26, starting transfers between devices: none -> 34.2 us  [the longest x20 31.7 us: send(): lax.ppermute(x, 'row', [(z * n + i, to * n + (i + turn) % n) for z, to in...]
    unnamed x15 -> x42, local copies, waits for them, and re-layouts: 31.7 us -> 4.9 us
    dot_general x1 -> x0, matrix products: 16.8 us -> none  [shards(): jnp.einsum('cmk,ckw->cmw', lax.all_gather(masked, 'col', axis=2, tiled=Tr...]
  transfers between devices with their start and end apart: 6 -> 28, of which waited for: 5 -> 12; matrix products, arithmetic and copies ran while one was open for 13% -> 10% of each run, Pallas kernels for 0% -> 15%
where the time goes in v3:
time: 320 us; the launch traced here: 318 us
  waiting for transfers between devices  173 us (54%)
  Pallas kernels  58.6 us (18%)
  starting transfers between devices  46.5 us (15%)
  other arithmetic  20.4 us (6%)
  local copies, waits for them, and re-layouts  17 us (5%)
    ppermute x20, waiting for transfers between devices, send(): lax.ppermute(x, 'row', [(z * n + i, to * n + (i + turn) % n) for z, to in...  107 us
    all_to_all x2, waiting for transfers between devices, shards(): lax.all_to_all(sent, 'row', split_axis=0, concat_axis=0, tiled=True)  60.8 us
    pallas_call x2, Pallas kernels, send_rows(): pl.pallas_call(functools.partial(send_kernel, groups, steps, len(lows), l...  33.7 us
    ppermute x20, starting transfers between devices, send(): lax.ppermute(x, 'row', [(z * n + i, to * n + (i + turn) % n) for z, to in...  31.7 us
    pallas_call x2, Pallas kernels, receive_rows(): pl.pallas_call(functools.partial(receive_kernel, groups, steps, cap), out...  21.1 us
    all_to_all x2, starting transfers between devices, shards(): lax.all_to_all(sent, 'row', split_axis=0, concat_axis=0, tiled=True)  12.3 us
    select_n x4, other arithmetic, step(): jnp.where(at_end, self.send(block, ends, j), others[j])  7.68 us
  transfers between devices with their start and end apart: 28, of which 12 were waited for; matrix products, arithmetic and copies ran while one was open for 10% of the time, Pallas kernels for 15%

profile of v3, /device:TPU:0, one launch (start us, length us, event | category | flops | bytes accessed | tf_op | source)
XLA Modules:
  0.0 318.5 jit_solution(3129919010715420488)
XLA Ops:
  0.0 2.3 slice_bitcast_fusion.2
  2.3 4.9 %collective-permute-start.3 = (bf16[256,1024]{1,0:T(8,128)(2,1)}, bf16[256,1024]{1,0:T(8,128)(2,1)S(1)}, u32[]{:S(2)}, u32[]{:S(2)}) collective-permute-start(bf16[256,1024]{1,0:T(8,128)(2,1)} %get-tuple-element.13.refs_4_), channel_id=1, source_target_pairs={{0,8},{4,12},{8,16},{12,20},{16,24},{20,28},{1,9},{5,13},{9,17},{1... | collective-permute-start | bytes 1572872 | tf_op jit(solution)/shard_map/ppermute | solution.py:317
  7.2 1.3 collective-permute-start.5
  8.5 1.6 collective-permute-start.20
  10.1 0.8 copy.17
  10.9 0.6 reshape.52.mask
  11.5 3.8 %mask_tiles.1 = bf16[2,1024,512]{2,1,0:T(8,128)(2,1)} custom-call(s32[64]{0:T(128)} %reshape.52.mask, bf16[2,1024,512]{2,1,0:T(8,128)(2,1)} %low.1), custom_call_target="tpu_custom_call" | custom-call | flops 16000000000 | bytes 13200000 | tf_op jit(solution)/shard_map/mask_tiles/pallas_call | solution.py:72
  15.3 2.7 slice_bitcast_fusion
  17.9 1.5 collective-permute-start.17
  19.5 0.7 iota_compare_fusion.1
  20.2 1.9 convert_reduce_fusion
  22.1 0.7 collective-permute-start.4
  22.8 1.3 collective-permute-start.6
  24.1 5.6 %select_reduce_fusion = (s32[2,2048]{1,0:T(2,128)S(1)}, s32[2,2048]{1,0:T(2,128)S(1)}) fusion(s32[2,1024]{1,0:T(2,128)S(1)} %get-tuple-element.24, s32[2,1024]{1,0:T(2,128)S(1)} %multiply_add_fusion), kind=kLoop, calls=%fused_computation | loop fusion | flops 20963328 | bytes 49152 | tf_op jit(solution)/shard_map/reduce_sum | solution.py:404
  30.2 10.5 %collective-permute-done.6.refs_2_ = bf16[256,1024]{1,0:T(8,128)(2,1)S(1)} collective-permute-done((bf16[256,1024]{1,0:T(8,128)(2,1)S(1)}, bf16[256,1024]{1,0:T(8,128)(2,1)S(1)}, u32[]{:S(2)}, u32[]{:S(2)}) %collective-permute-start.6) | collective-permute-done | bytes 524320 | tf_op jit(solution)/shard_map/ppermute | solution.py:317
  40.7 0.8 copy-done.3
  41.5 3.7 %collective-permute-start.8 = (bf16[256,1024]{1,0:T(8,128)(2,1)}, bf16[256,1024]{1,0:T(8,128)(2,1)S(1)}, u32[]{:S(2)}, u32[]{:S(2)}) collective-permute-start(bf16[256,1024]{1,0:T(8,128)(2,1)} %gate.2.refs_4_), channel_id=1, source_target_pairs={{0,8},{4,12},{8,16},{12,20},{16,24},{20,28},{1,9},{5,13},{9,17},{1... | collective-permute-start | bytes 1572872 | tf_op jit(solution)/shard_map/ppermute | solution.py:317
  45.2 1.3 collective-permute-start.9
  46.5 1.5 broadcast_select_fusion
  48.0 1.3 collective-permute-start.23
  49.3 1.3 collective-permute-start.24
  50.6 1.5 collective-permute-start.25
  52.2 0.7 slice_bitcast_fusion.4
  52.9 1.5 collective-permute-done.8
  54.4 1.5 collective-permute-start.11
  55.9 6.4 %collective-permute-done.9 = bf16[256,1024]{1,0:T(8,128)(2,1)} collective-permute-done((bf16[256,1024]{1,0:T(8,128)(2,1)}, bf16[256,1024]{1,0:T(8,128)(2,1)}, u32[]{:S(2)}, u32[]{:S(2)}) %collective-permute-start.9) | collective-permute-done | bytes 524320 | tf_op jit(solution)/shard_map/ppermute | solution.py:317
  62.3 1.3 collective-permute-start.12
  63.6 0.6 dynamic_slice.18
  64.9 0.6 dynamic_slice.19
  66.1 0.6 dynamic_slice.20
  67.4 0.7 mul.127.source
  68.1 0.7 mul.148.source
  68.8 0.6 stack.78.starts
  69.4 4.1 %collective-permute-done.23 = bf16[256,1024]{1,0:T(8,128)(2,1)} collective-permute-done((bf16[256,1024]{1,0:T(8,128)(2,1)S(1)}, bf16[256,1024]{1,0:T(8,128)(2,1)}, u32[]{:S(2)}, u32[]{:S(2)}) %collective-permute-start.23) | collective-permute-done | bytes 524320 | tf_op jit(solution)/shard_map/ppermute | solution.py:317
  73.5 11.2 %collective-permute-done.24 = bf16[256,1024]{1,0:T(8,128)(2,1)} collective-permute-done((bf16[256,1024]{1,0:T(8,128)(2,1)S(1)}, bf16[256,1024]{1,0:T(8,128)(2,1)}, u32[]{:S(2)}, u32[]{:S(2)}) %collective-permute-start.24) | collective-permute-done | bytes 524320 | tf_op jit(solution)/shard_map/ppermute | solution.py:317
  85.2 1.9 broadcast_select_fusion.3.refs_10_
  87.1 1.5 collective-permute-start.21
  88.6 3.6 %collective-permute-done.12 = bf16[256,1024]{1,0:T(8,128)(2,1)} collective-permute-done((bf16[256,1024]{1,0:T(8,128)(2,1)}, bf16[256,1024]{1,0:T(8,128)(2,1)}, u32[]{:S(2)}, u32[]{:S(2)}) %collective-permute-start.12) | collective-permute-done | bytes 524320 | tf_op jit(solution)/shard_map/ppermute | solution.py:317
  92.3 0.5 collective-permute-start.22
  92.8 1.9 broadcast_select_fusion.2.refs_11_
  94.7 2.6 broadcast_select_fusion.1
  97.4 5.4 %collective-permute-done.refs_1_ = bf16[1024,512]{1,0:T(8,128)(2,1)} collective-permute-done((bf16[1024,512]{1,0:T(8,128)(2,1)}, bf16[1024,512]{1,0:T(8,128)(2,1)}, u32[]{:S(2)}, u32[]{:S(2)}) %collective-permute-start) | collective-permute-done | bytes 1048608 | tf_op jit(solution)/shard_map/ppermute | solution.py:380
  103.3 1.3 collective-permute-start.14
  104.6 8.1 %collective-permute-done.22.refs_9_ = bf16[256,1024]{1,0:T(8,128)(2,1)S(1)} collective-permute-done((bf16[256,1024]{1,0:T(8,128)(2,1)S(1)}, bf16[256,1024]{1,0:T(8,128)(2,1)S(1)}, u32[]{:S(2)}, u32[]{:S(2)}) %collective-permute-start.22) | collective-permute-done | bytes 524320 | tf_op jit(solution)/shard_map/ppermute | solution.py:317
  112.7 1.3 collective-permute-start.15
  114.0 1.5 collective-permute-start.16
  115.5 1.0 broadcast_in_dim.54.slot
  116.5 16.9 %send_rows.3 = s16[8,97,16,128]{3,2,1,0:T(8,128)(2,1)} custom-call(s32[1536]{0:T(1024)} %mul.148.source, s32[12]{0:T(128)} %stack.78.starts, s32[1024,128]{1,0:T(8,128)} %broadcast_in_dim.54.slot, s32[8,16,128]{2,1,0:T(8,128)} %get-tuple-element.17.notes, f32[2,1024,1024]{2,1,0:T(8,128)} %schur.3, bf16[1024,512]{1,0:T(8,128)(2,1)} %copy-done.4, ...), custom_call_target="tpu_custom_call" | custom-call | flops 56000000000 | bytes 46200000 | tf_op jit(solution)/shard_map/send_rows/pallas_call | solution.py:176
  133.4 7.8 %all-to-all-start = ((s16[8,97,16,128]{3,2,1,0:T(8,128)(2,1)}), s16[8,97,16,128]{3,2,1,0:T(8,128)(2,1)S(1)}, u32[]{:S(2)}, u32[]{:S(2)}) async-start(s16[8,97,16,128]{3,2,1,0:T(8,128)(2,1)} %send_rows.3), calls=%async_computation | async-start | bytes 6356992 | tf_op jit(solution)/shard_map/all_to_all | solution.py:437
  141.1 2.0 collective-permute-start.7
  143.3 1.9 collective-permute-start.13
  145.2 1.9 broadcast_select_fusion.5.refs_10_
  147.1 1.9 broadcast_select_fusion.4.refs_11_
  149.0 40.9 %collective-permute-done.7.refs_5_ = bf16[256,1024]{1,0:T(8,128)(2,1)S(1)} collective-permute-done((bf16[256,1024]{1,0:T(8,128)(2,1)}, bf16[256,1024]{1,0:T(8,128)(2,1)S(1)}, u32[]{:S(2)}, u32[]{:S(2)}) %collective-permute-start.7) | collective-permute-done | bytes 524320 | tf_op jit(solution)/shard_map/ppermute | solution.py:317
  189.9 11.5 %collective-permute-done.10.refs_7_ = bf16[256,1024]{1,0:T(8,128)(2,1)S(1)} collective-permute-done((bf16[256,1024]{1,0:T(8,128)(2,1)}, bf16[256,1024]{1,0:T(8,128)(2,1)S(1)}, u32[]{:S(2)}, u32[]{:S(2)}) %collective-permute-start.10) | collective-permute-done | bytes 524320 | tf_op jit(solution)/shard_map/ppermute | solution.py:317
  201.4 9.3 %collective-permute-done.13.refs_9_ = bf16[256,1024]{1,0:T(8,128)(2,1)S(1)} collective-permute-done((bf16[256,1024]{1,0:T(8,128)(2,1)}, bf16[256,1024]{1,0:T(8,128)(2,1)S(1)}, u32[]{:S(2)}, u32[]{:S(2)}) %collective-permute-start.13) | collective-permute-done | bytes 524320 | tf_op jit(solution)/shard_map/ppermute | solution.py:317
  210.7 1.0 broadcast_in_dim.50.slot
  211.7 16.8 %send_rows.2.refs_0_ = s16[8,97,16,128]{3,2,1,0:T(8,128)(2,1)} custom-call(s32[1536]{0:T(1024)} %mul.127.source, s32[12]{0:T(128)} %stack.78.starts, s32[1024,128]{1,0:T(8,128)} %broadcast_in_dim.50.slot, s32[8,16,128]{2,1,0:T(8,128)} %get-tuple-element.18.notes, f32[2,1024,1024]{2,1,0:T(8,128)} %schur.3, bf16[1024,512]{1,0:T(8,128)(2,1)} %get-tuple-element.8.refs_0_, ...), custom_call_target="tpu_custom_call" | custom-call | flops 56000000000 | bytes 46200000 | tf_op jit(solution)/shard_map/send_rows/pallas_call | solution.py:176
  228.6 1.6 copy-done
  230.2 4.5 %all-to-all-start.1 = ((s16[8,97,16,128]{3,2,1,0:T(8,128)(2,1)}), s16[8,97,16,128]{3,2,1,0:T(8,128)(2,1)S(1)}, u32[]{:S(2)}, u32[]{:S(2)}) async-start(s16[8,97,16,128]{3,2,1,0:T(8,128)(2,1)} %gate.3), calls=%async_computation.1 | async-start | bytes 6356992 | tf_op jit(solution)/shard_map/all_to_all | solution.py:437
  234.7 10.5 %receive_rows.2.before = f32[1024,1024]{1,0:T(8,128)} custom-call(s16[8,97,16,128]{3,2,1,0:T(8,128)(2,1)} %copy-done, s16[8,97,16,128]{3,2,1,0:T(8,128)(2,1)} %copy-done, f32[1024,1024]{1,0:T(8,128)} %before.1), custom_call_target="tpu_custom_call" | custom-call | flops 32000000000 | bytes 26400000 | tf_op jit(solution)/shard_map/receive_rows/pallas_call | solution.py:276
  245.2 60.8 %all-to-all-done.1.got.notes = s16[8,97,16,128]{3,2,1,0:T(8,128)(2,1)S(1)} async-done(((s16[8,97,16,128]{3,2,1,0:T(8,128)(2,1)}), s16[8,97,16,128]{3,2,1,0:T(8,128)(2,1)S(1)}, u32[]{:S(2)}, u32[]{:S(2)}) %all-to-all-start.1) | async-done | bytes 3178528 | tf_op jit(solution)/shard_map/all_to_all | solution.py:437
  306.1 1.6 copy-done.1
  307.7 10.6 %receive_rows.3 = f32[1024,1024]{1,0:T(8,128)} custom-call(s16[8,97,16,128]{3,2,1,0:T(8,128)(2,1)} %copy-done.1, s16[8,97,16,128]{3,2,1,0:T(8,128)(2,1)} %copy-done.1, f32[1024,1024]{1,0:T(8,128)} %receive_rows.2.before), custom_call_target="tpu_custom_call" | custom-call | flops 32000000000 | bytes 26400000 | tf_op jit(solution)/shard_map/receive_rows/pallas_call | solution.py:276
  (72 shorter events, 1.8 us)
Async XLA Ops:
  2.3 19.8 %collective-permute-start.3 = (bf16[256,1024]{1,0:T(8,128)(2,1)}, bf16[256,1024]{1,0:T(8,128)(2,1)S(1)}, u32[]{:S(2)}, u32[]{:S(2)}) collective-permute-start(bf16[256,1024]{1,0:T(8,128)(2,1)} %get-tuple-element.13.refs_4_), channel_id=1, source_target_pairs={{0,8},{4,12},{8,16},{12,20},{16,24},{20,28},{1,9},{5,13},{9,17},{1... | collective-permute-start | bytes 1572872 | tf_op jit(solution)/shard_map/ppermute | solution.py:317
  7.2 15.6 %collective-permute-start.5 = (bf16[256,1024]{1,0:T(8,128)(2,1)}, bf16[256,1024]{1,0:T(8,128)(2,1)S(1)}, u32[]{:S(2)}, u32[]{:S(2)}) collective-permute-start(bf16[256,1024]{1,0:T(8,128)(2,1)} %get-tuple-element.13.refs_4_), channel_id=1, source_target_pairs={{8,0},{12,4},{16,8},{20,12},{24,16},{28,20},{9,1},{13,5},{17,9},{2... | collective-permute-start | bytes 1572872 | tf_op jit(solution)/shard_map/ppermute | solution.py:317
  8.5 40.8 %collective-permute-start.20 = (bf16[256,1024]{1,0:T(8,128)(2,1)}, bf16[256,1024]{1,0:T(8,128)(2,1)}, u32[]{:S(2)}, u32[]{:S(2)}) collective-permute-start(bf16[256,1024]{1,0:T(8,128)(2,1)} %get-tuple-element.13.refs_4_), channel_id=1, source_target_pairs={{0,4},{4,0},{8,12},{12,8},{16,20},{20,16},{24,28},{28,24},{1,5},{5... | collective-permute-start | bytes 1572872 | tf_op jit(solution)/shard_map/ppermute | solution.py:317
  15.3 4.2 %copy-start.9 = (s32[2,1024]{1,0:T(2,128)S(1)}, s32[2,1024]{1,0:T(2,128)}, u32[]{:S(2)}) copy-start(s32[2,1024]{1,0:T(2,128)} %param.16) | copy-start | bytes 24580
  17.9 55.6 %copy-start.4 = (bf16[1024,512]{1,0:T(8,128)(2,1)}, bf16[1024,512]{1,0:T(8,128)(2,1)S(1)}, u32[]{:S(2)}) copy-start(bf16[1024,512]{1,0:T(8,128)(2,1)S(1)} %get-tuple-element.7.refs_0_) | copy-start | bytes 3145732
  17.9 32.7 %collective-permute-start.17 = (bf16[1024,512]{1,0:T(8,128)(2,1)S(1)}, bf16[1024,512]{1,0:T(8,128)(2,1)}, u32[]{:S(2)}, u32[]{:S(2)}) collective-permute-start(bf16[1024,512]{1,0:T(8,128)(2,1)S(1)} %get-tuple-element.7.refs_0_), channel_id=1, source_target_pairs={{0,2},{1,3},{2,0},{3,1},{4,6},{5,7},{6,4},{7,5},{8,10},{9,11},{10,... | collective-permute-start | bytes 3145736 | tf_op jit(solution)/shard_map/ppermute | solution.py:380
  20.1 43.5 %copy-start.19 = (s32[4]{0:T(128)S(1)}, s32[4]{0:T(128)}, u32[]{:S(2)}) copy-start(s32[4]{0:T(128)} %constant.133.clone) | copy-start | bytes 52
  20.2 44.7 %copy-start.18 = (s32[4]{0:T(128)S(1)}, s32[4]{0:T(128)}, u32[]{:S(2)}) copy-start(s32[4]{0:T(128)} %constant.134.clone) | copy-start | bytes 52
  20.2 46.0 %copy-start.17 = (s32[4]{0:T(128)S(1)}, s32[4]{0:T(128)}, u32[]{:S(2)}) copy-start(s32[4]{0:T(128)} %constant.135.clone) | copy-start | bytes 52
  22.1 23.1 %copy-start.7 = (bf16[256,1024]{1,0:T(8,128)(2,1)}, bf16[256,1024]{1,0:T(8,128)(2,1)S(1)}, u32[]{:S(2)}) copy-start(bf16[256,1024]{1,0:T(8,128)(2,1)S(1)} %collective-permute-done.3) | copy-start | bytes 1572868
  22.1 8.1 %collective-permute-start.4 = (bf16[256,1024]{1,0:T(8,128)(2,1)S(1)}, bf16[256,1024]{1,0:T(8,128)(2,1)S(1)}, u32[]{:S(2)}, u32[]{:S(2)}) collective-permute-start(bf16[256,1024]{1,0:T(8,128)(2,1)S(1)} %collective-permute-done.3), channel_id=1, source_target_pairs={{8,16},{12,20},{16,24},{20,28},{9,17},{13,21},{17,25},{21,29},{10,... | collective-permute-start | bytes 1572872 | tf_op jit(solution)/shard_map/ppermute | solution.py:317
  22.8 17.9 %copy-start.8 = (bf16[256,1024]{1,0:T(8,128)(2,1)}, bf16[256,1024]{1,0:T(8,128)(2,1)S(1)}, u32[]{:S(2)}) copy-start(bf16[256,1024]{1,0:T(8,128)(2,1)S(1)} %collective-permute-done.5) | copy-start | bytes 1572868
  22.8 17.9 %collective-permute-start.6 = (bf16[256,1024]{1,0:T(8,128)(2,1)S(1)}, bf16[256,1024]{1,0:T(8,128)(2,1)S(1)}, u32[]{:S(2)}, u32[]{:S(2)}) collective-permute-start(bf16[256,1024]{1,0:T(8,128)(2,1)S(1)} %collective-permute-done.5), channel_id=1, source_target_pairs={{8,0},{12,4},{16,8},{20,12},{9,1},{13,5},{17,9},{21,13},{10,2},{14... | collective-permute-start | bytes 1572872 | tf_op jit(solution)/shard_map/ppermute | solution.py:317
  30.2 10.5 %copy-start.2 = (bf16[256,1024]{1,0:T(8,128)(2,1)}, bf16[256,1024]{1,0:T(8,128)(2,1)S(1)}, u32[]{:S(2)}) copy-start(bf16[256,1024]{1,0:T(8,128)(2,1)S(1)} %collective-permute-done.4.refs_1_) | copy-start | bytes 1572868
  40.7 0.8 copy-start.3
  41.5 12.9 %collective-permute-start.8 = (bf16[256,1024]{1,0:T(8,128)(2,1)}, bf16[256,1024]{1,0:T(8,128)(2,1)S(1)}, u32[]{:S(2)}, u32[]{:S(2)}) collective-permute-start(bf16[256,1024]{1,0:T(8,128)(2,1)} %gate.2.refs_4_), channel_id=1, source_target_pairs={{0,8},{4,12},{8,16},{12,20},{16,24},{20,28},{1,9},{5,13},{9,17},{1... | collective-permute-start | bytes 1572872 | tf_op jit(solution)/shard_map/ppermute | solution.py:317
  45.2 17.1 %collective-permute-start.9 = (bf16[256,1024]{1,0:T(8,128)(2,1)}, bf16[256,1024]{1,0:T(8,128)(2,1)}, u32[]{:S(2)}, u32[]{:S(2)}) collective-permute-start(bf16[256,1024]{1,0:T(8,128)(2,1)} %gate.2.refs_4_), channel_id=1, source_target_pairs={{8,0},{12,4},{16,8},{20,12},{24,16},{28,20},{9,1},{13,5},{17,9},{2... | collective-permute-start | bytes 1572872 | tf_op jit(solution)/shard_map/ppermute | solution.py:317
  48.0 68.5 %copy-start.5 = (bf16[256,1024]{1,0:T(8,128)(2,1)}, bf16[256,1024]{1,0:T(8,128)(2,1)S(1)}, u32[]{:S(2)}) copy-start(bf16[256,1024]{1,0:T(8,128)(2,1)S(1)} %get-tuple-element.10.refs_8_) | copy-start | bytes 1572868
  48.0 68.5 %copy-start.6 = (bf16[256,1024]{1,0:T(8,128)(2,1)}, bf16[256,1024]{1,0:T(8,128)(2,1)S(1)}, u32[]{:S(2)}) copy-start(bf16[256,1024]{1,0:T(8,128)(2,1)S(1)} %get-tuple-element.16.refs_6_) | copy-start | bytes 1572868
  48.0 25.5 %collective-permute-start.23 = (bf16[256,1024]{1,0:T(8,128)(2,1)S(1)}, bf16[256,1024]{1,0:T(8,128)(2,1)}, u32[]{:S(2)}, u32[]{:S(2)}) collective-permute-start(bf16[256,1024]{1,0:T(8,128)(2,1)S(1)} %get-tuple-element.9), channel_id=1, source_target_pairs={{8,0},{12,4},{16,24},{20,28},{9,1},{13,5},{17,25},{21,29},{10,2},{... | collective-permute-start | bytes 1572872 | tf_op jit(solution)/shard_map/ppermute | solution.py:317
  49.3 35.4 %collective-permute-start.24 = (bf16[256,1024]{1,0:T(8,128)(2,1)S(1)}, bf16[256,1024]{1,0:T(8,128)(2,1)}, u32[]{:S(2)}, u32[]{:S(2)}) collective-permute-start(bf16[256,1024]{1,0:T(8,128)(2,1)S(1)} %get-tuple-element.9), channel_id=1, source_target_pairs={{8,4},{12,0},{16,28},{20,24},{9,5},{13,1},{17,29},{21,25},{10,6},{... | collective-permute-start | bytes 1572872 | tf_op jit(solution)/shard_map/ppermute | solution.py:317
  50.6 34.6 %collective-permute-start.25 = (bf16[256,1024]{1,0:T(8,128)(2,1)S(1)}, bf16[256,1024]{1,0:T(8,128)(2,1)}, u32[]{:S(2)}, u32[]{:S(2)}) collective-permute-start(bf16[256,1024]{1,0:T(8,128)(2,1)S(1)} %get-tuple-element.9), channel_id=1, source_target_pairs={{8,12},{12,8},{16,20},{20,16},{9,13},{13,9},{17,21},{21,17},{10,14... | collective-permute-start | bytes 1572872 | tf_op jit(solution)/shard_map/ppermute | solution.py:317
  54.4 32.7 %collective-permute-start.11 = (bf16[256,1024]{1,0:T(8,128)(2,1)S(1)}, bf16[256,1024]{1,0:T(8,128)(2,1)}, u32[]{:S(2)}, u32[]{:S(2)}) collective-permute-start(bf16[256,1024]{1,0:T(8,128)(2,1)S(1)} %collective-permute-done.8), channel_id=1, source_target_pairs={{8,16},{12,20},{16,24},{20,28},{9,17},{13,21},{17,25},{21,29},{10,... | collective-permute-start | bytes 1572872 | tf_op jit(solution)/shard_map/ppermute | solution.py:317
  62.3 30.0 %collective-permute-start.12 = (bf16[256,1024]{1,0:T(8,128)(2,1)}, bf16[256,1024]{1,0:T(8,128)(2,1)}, u32[]{:S(2)}, u32[]{:S(2)}) collective-permute-start(bf16[256,1024]{1,0:T(8,128)(2,1)} %collective-permute-done.9), channel_id=1, source_target_pairs={{8,0},{12,4},{16,8},{20,12},{9,1},{13,5},{17,9},{21,13},{10,2},{14... | collective-permute-start | bytes 1572872 | tf_op jit(solution)/shard_map/ppermute | solution.py:317
  73.5 29.3 %collective-permute-start.18 = (bf16[1024,512]{1,0:T(8,128)(2,1)S(1)}, bf16[1024,512]{1,0:T(8,128)(2,1)S(1)}, u32[]{:S(2)}, u32[]{:S(2)}) collective-permute-start(bf16[1024,512]{1,0:T(8,128)(2,1)S(1)} %get-tuple-element.7.refs_0_), channel_id=1, source_target_pairs={{0,1},{1,0},{2,3},{3,2},{4,5},{5,4},{6,7},{7,6},{8,9},{9,8},{10,11... | collective-permute-start | bytes 3145736 | tf_op jit(solution)/shard_map/ppermute | solution.py:380
  84.7 18.1 %collective-permute-start = (bf16[1024,512]{1,0:T(8,128)(2,1)}, bf16[1024,512]{1,0:T(8,128)(2,1)}, u32[]{:S(2)}, u32[]{:S(2)}) collective-permute-start(bf16[1024,512]{1,0:T(8,128)(2,1)} %get-tuple-element.8.refs_0_), channel_id=1, source_target_pairs={{0,2},{1,3},{2,0},{3,1},{4,6},{5,7},{6,4},{7,5},{8,10},{9,11},{10,... | collective-permute-start | bytes 3145736 | tf_op jit(solution)/shard_map/ppermute | solution.py:380
  85.2 28.8 %collective-permute-start.19 = (bf16[1024,512]{1,0:T(8,128)(2,1)}, bf16[1024,512]{1,0:T(8,128)(2,1)S(1)}, u32[]{:S(2)}, u32[]{:S(2)}) collective-permute-start(bf16[1024,512]{1,0:T(8,128)(2,1)} %collective-permute-done.17.refs_1_), channel_id=1, source_target_pairs={{0,1},{1,0},{2,3},{3,2},{4,5},{5,4},{6,7},{7,6},{8,9},{9,8},{10,11... | collective-permute-start | bytes 3145736 | tf_op jit(solution)/shard_map/ppermute | solution.py:380
  87.1 16.2 %collective-permute-start.21 = (bf16[256,1024]{1,0:T(8,128)(2,1)S(1)}, bf16[256,1024]{1,0:T(8,128)(2,1)S(1)}, u32[]{:S(2)}, u32[]{:S(2)}) collective-permute-start(bf16[256,1024]{1,0:T(8,128)(2,1)S(1)} %get-tuple-element.16.refs_6_), channel_id=1, source_target_pairs={{0,4},{4,0},{8,12},{12,8},{16,20},{20,16},{24,28},{28,24},{1,5},{5... | collective-permute-start | bytes 1572872 | tf_op jit(solution)/shard_map/ppermute | solution.py:317
  92.3 20.4 %collective-permute-start.22 = (bf16[256,1024]{1,0:T(8,128)(2,1)S(1)}, bf16[256,1024]{1,0:T(8,128)(2,1)S(1)}, u32[]{:S(2)}, u32[]{:S(2)}) collective-permute-start(bf16[256,1024]{1,0:T(8,128)(2,1)S(1)} %get-tuple-element.10.refs_8_), channel_id=1, source_target_pairs={{0,4},{4,0},{8,12},{12,8},{16,20},{20,16},{24,28},{28,24},{1,5},{5... | collective-permute-start | bytes 1572872 | tf_op jit(solution)/shard_map/ppermute | solution.py:317
  102.8 46.2 %collective-permute-start.1 = (bf16[1024,512]{1,0:T(8,128)(2,1)}, bf16[1024,512]{1,0:T(8,128)(2,1)}, u32[]{:S(2)}, u32[]{:S(2)}) collective-permute-start(bf16[1024,512]{1,0:T(8,128)(2,1)} %get-tuple-element.8.refs_0_), channel_id=1, source_target_pairs={{0,1},{1,0},{2,3},{3,2},{4,5},{5,4},{6,7},{7,6},{8,9},{9,8},{10,11... | collective-permute-start | bytes 3145736 | tf_op jit(solution)/shard_map/ppermute | solution.py:380
  102.8 13.7 %copy-start.10 = (bf16[1024,512]{1,0:T(8,128)(2,1)}, bf16[1024,512]{1,0:T(8,128)(2,1)S(1)}, u32[]{:S(2)}) copy-start(bf16[1024,512]{1,0:T(8,128)(2,1)S(1)} %collective-permute-done.18.refs_2_) | copy-start | bytes 3145732
  102.8 87.1 %collective-permute-start.2 = (bf16[1024,512]{1,0:T(8,128)(2,1)}, bf16[1024,512]{1,0:T(8,128)(2,1)}, u32[]{:S(2)}, u32[]{:S(2)}) collective-permute-start(bf16[1024,512]{1,0:T(8,128)(2,1)} %collective-permute-done.refs_1_), channel_id=1, source_target_pairs={{0,1},{1,0},{2,3},{3,2},{4,5},{5,4},{6,7},{7,6},{8,9},{9,8},{10,11... | collective-permute-start | bytes 3145736 | tf_op jit(solution)/shard_map/ppermute | solution.py:380
  103.3 13.2 %copy-start.12 = (bf16[256,1024]{1,0:T(8,128)(2,1)}, bf16[256,1024]{1,0:T(8,128)(2,1)S(1)}, u32[]{:S(2)}) copy-start(bf16[256,1024]{1,0:T(8,128)(2,1)S(1)} %collective-permute-done.21.refs_7_) | copy-start | bytes 1572868
  103.3 37.8 %collective-permute-start.14 = (bf16[256,1024]{1,0:T(8,128)(2,1)}, bf16[256,1024]{1,0:T(8,128)(2,1)}, u32[]{:S(2)}, u32[]{:S(2)}) collective-permute-start(bf16[256,1024]{1,0:T(8,128)(2,1)} %get-tuple-element.11), channel_id=1, source_target_pairs={{8,0},{12,4},{16,24},{20,28},{9,1},{13,5},{17,25},{21,29},{10,2},{... | collective-permute-start | bytes 1572872 | tf_op jit(solution)/shard_map/ppermute | solution.py:317
  112.7 3.8 %copy-start.13 = (bf16[256,1024]{1,0:T(8,128)(2,1)}, bf16[256,1024]{1,0:T(8,128)(2,1)S(1)}, u32[]{:S(2)}) copy-start(bf16[256,1024]{1,0:T(8,128)(2,1)S(1)} %collective-permute-done.22.refs_9_) | copy-start | bytes 1572868
  112.7 30.5 %collective-permute-start.15 = (bf16[256,1024]{1,0:T(8,128)(2,1)}, bf16[256,1024]{1,0:T(8,128)(2,1)}, u32[]{:S(2)}, u32[]{:S(2)}) collective-permute-start(bf16[256,1024]{1,0:T(8,128)(2,1)} %get-tuple-element.11), channel_id=1, source_target_pairs={{8,4},{12,0},{16,28},{20,24},{9,5},{13,1},{17,29},{21,25},{10,6},{... | collective-permute-start | bytes 1572872 | tf_op jit(solution)/shard_map/ppermute | solution.py:317
  114.0 2.5 copy-start.11
  114.0 29.3 %collective-permute-start.16 = (bf16[256,1024]{1,0:T(8,128)(2,1)}, bf16[256,1024]{1,0:T(8,128)(2,1)}, u32[]{:S(2)}, u32[]{:S(2)}) collective-permute-start(bf16[256,1024]{1,0:T(8,128)(2,1)} %get-tuple-element.11), channel_id=1, source_target_pairs={{8,12},{12,8},{16,20},{20,16},{9,13},{13,9},{17,21},{21,17},{10,14... | collective-permute-start | bytes 1572872 | tf_op jit(solution)/shard_map/ppermute | solution.py:317
  133.4 95.2 %all-to-all-start = ((s16[8,97,16,128]{3,2,1,0:T(8,128)(2,1)}), s16[8,97,16,128]{3,2,1,0:T(8,128)(2,1)S(1)}, u32[]{:S(2)}, u32[]{:S(2)}) async-start(s16[8,97,16,128]{3,2,1,0:T(8,128)(2,1)} %send_rows.3), calls=%async_computation | async-start | bytes 6356992 | tf_op jit(solution)/shard_map/all_to_all | solution.py:437
  141.1 48.8 %collective-permute-start.7 = (bf16[256,1024]{1,0:T(8,128)(2,1)}, bf16[256,1024]{1,0:T(8,128)(2,1)S(1)}, u32[]{:S(2)}, u32[]{:S(2)}) collective-permute-start(bf16[256,1024]{1,0:T(8,128)(2,1)} %gate.2.refs_4_), channel_id=1, source_target_pairs={{0,4},{4,0},{8,12},{12,8},{16,20},{20,16},{24,28},{28,24},{1,5},{5... | collective-permute-start | bytes 1572872 | tf_op jit(solution)/shard_map/ppermute | solution.py:317
  143.2 58.2 %collective-permute-start.10 = (bf16[256,1024]{1,0:T(8,128)(2,1)}, bf16[256,1024]{1,0:T(8,128)(2,1)S(1)}, u32[]{:S(2)}, u32[]{:S(2)}) collective-permute-start(bf16[256,1024]{1,0:T(8,128)(2,1)} %get-tuple-element.15.refs_6_), channel_id=1, source_target_pairs={{0,4},{4,0},{8,12},{12,8},{16,20},{20,16},{24,28},{28,24},{1,5},{5... | collective-permute-start | bytes 1572872 | tf_op jit(solution)/shard_map/ppermute | solution.py:317
  143.3 67.4 %collective-permute-start.13 = (bf16[256,1024]{1,0:T(8,128)(2,1)}, bf16[256,1024]{1,0:T(8,128)(2,1)S(1)}, u32[]{:S(2)}, u32[]{:S(2)}) collective-permute-start(bf16[256,1024]{1,0:T(8,128)(2,1)} %get-tuple-element.12.refs_8_), channel_id=1, source_target_pairs={{0,4},{4,0},{8,12},{12,8},{16,20},{20,16},{24,28},{28,24},{1,5},{5... | collective-permute-start | bytes 1572872 | tf_op jit(solution)/shard_map/ppermute | solution.py:317
  189.9 21.8 %copy-start.14 = (bf16[256,1024]{1,0:T(8,128)(2,1)}, bf16[256,1024]{1,0:T(8,128)(2,1)S(1)}, u32[]{:S(2)}) copy-start(bf16[256,1024]{1,0:T(8,128)(2,1)S(1)} %collective-permute-done.7.refs_5_) | copy-start | bytes 1572868
  201.4 10.3 %copy-start.15 = (bf16[256,1024]{1,0:T(8,128)(2,1)}, bf16[256,1024]{1,0:T(8,128)(2,1)S(1)}, u32[]{:S(2)}) copy-start(bf16[256,1024]{1,0:T(8,128)(2,1)S(1)} %collective-permute-done.10.refs_7_) | copy-start | bytes 1572868
  210.7 1.0 copy-start.16
  228.6 1.6 copy-start
  230.2 75.9 %all-to-all-start.1 = ((s16[8,97,16,128]{3,2,1,0:T(8,128)(2,1)}), s16[8,97,16,128]{3,2,1,0:T(8,128)(2,1)S(1)}, u32[]{:S(2)}, u32[]{:S(2)}) async-start(s16[8,97,16,128]{3,2,1,0:T(8,128)(2,1)} %gate.3), calls=%async_computation.1 | async-start | bytes 6356992 | tf_op jit(solution)/shard_map/all_to_all | solution.py:437
  306.0 1.6 copy-start.1

commit v4 on v2

v4 whole, which is shorter than its diff:
```python
import functools

import jax
import jax.numpy as jnp
from jax import lax
from jax.experimental import pallas as pl
from jax.experimental.pallas import tpu as pltpu
from jax.sharding import PartitionSpec as P

TILE = 128
LANES = 128
TOP = 32767.0
STEP = (1.0 + 2.0**-7) / TOP
NOTES = 16
BASE = 32
TINY = 1e-33
VMEM_LIMIT = 56 * 1024 * 1024
ANY = pl.BlockSpec(memory_space=pl.ANY)


def inner_factor(count):
    inner = 1
    while (2 * inner) * (2 * inner) <= count:
        inner *= 2
    return inner


def takes(us):
    return pl.CostEstimate(flops=int(us * 4e9), bytes_accessed=int(us * 3.3e6), transcendentals=0)


def gate_kernel(*refs):
    pass


def gate(arrays, *first):
    count = len(arrays)
    return pl.pallas_call(
        gate_kernel,
        out_shape=[jax.ShapeDtypeStruct(x.shape, x.dtype) for x in arrays],
        in_specs=[ANY] * (count + len(first)),
        out_specs=[ANY] * count,
        input_output_aliases={i: i for i in range(count)},
        name="gate",
    )(*arrays, *first)


def row_unit(x):
    most = jnp.max(jnp.abs(x), axis=-1, keepdims=True)
    return jnp.where(most > TINY, most * STEP, 0.0).astype(jnp.bfloat16)


def pack_kernel(groups, steps, source, x, *refs):
    out, held = refs[-2:]
    i = pl.program_id(0)
    rows = x.shape[1]
    targets, _, tiles = out.shape[:3]
    per = 16 // groups

    @pl.when(i < steps)
    def _():
        def body(g, carry):
            at = pl.multiple_of(g * 8, 8)
            v = x[0, pl.ds(at, 8), :]
            unit = row_unit(v).astype(jnp.float32)
            inverse = jnp.where(unit > 0.0, 1.0 / unit, 0.0)
            q = jnp.floor(v * inverse + 0.5).astype(jnp.int32)
            base = (i * rows + at) * groups
            for j in range(groups):
                held[pl.ds(base + j, 8, stride=groups), :] = q[:, j * LANES : (j + 1) * LANES]
            return carry

        lax.fori_loop(0, rows // 8, body, 0, unroll=4)

    @pl.when(i >= steps)
    def _():
        for target in range(targets):
            start = ((i - steps) * targets + target) * tiles * per

            def body(t, carry):
                parts = []
                for a in range(per):
                    row = pl.multiple_of(source[start + t * per + a] * groups, groups)
                    parts.append(held[pl.ds(row, groups), :])
                out[target, 0, t] = jnp.concatenate(parts, axis=0).astype(jnp.int16)
                return carry

            lax.fori_loop(0, tiles, body, 0, unroll=8)


def pack(x, child, source, count, into, *first):
    children, rows, width = x.shape
    cap = source.shape[0] // count
    groups = width // LANES
    tiles = cap * groups // 16
    steps, out_steps = 2, 4
    first = first if into is None else (into,) + first
    return pl.pallas_call(
        functools.partial(pack_kernel, groups, steps),
        out_shape=jax.ShapeDtypeStruct((count, children, tiles, 16, LANES), jnp.int16),
        grid_spec=pltpu.PrefetchScalarGridSpec(
            num_scalar_prefetch=1,
            grid=(steps + out_steps,),
            in_specs=[pl.BlockSpec((1, rows // steps, width), lambda i, s: (child, jnp.minimum(i, steps - 1), 0))]
            + [ANY] * len(first),
            out_specs=pl.BlockSpec(
                (count // out_steps, 1, tiles, 16, LANES),
                lambda i, s: (jnp.maximum(i - steps, 0), child, 0, 0, 0),
            ),
            scratch_shapes=[pltpu.VMEM((rows * groups, LANES), jnp.int32)],
        ),
        input_output_aliases={} if into is None else {2: 0},
        compiler_params=pltpu.CompilerParams(vmem_limit_bytes=VMEM_LIMIT),
        cost_estimate=takes(10),
        name="pack",
    )(source, x, *first)


def unpack_kernel(groups, parts, row_at, valid, got, before, unit, out, held):
    i = pl.program_id(0)
    children = unit.shape[0]
    per = 16 // groups
    chunk = 16
    tiles = got.shape[2]

    @pl.when(i < parts)
    def _():
        for c in range(children):
            base = (c * parts + i) * tiles * per

            def body(k, carry):
                for t in range(chunk // per):
                    v = got[0, c, k * (chunk // per) + t].astype(jnp.int32).astype(jnp.float32)
                    for a in range(per):
                        row = pl.multiple_of(row_at[base + k * chunk + t * per + a], groups)
                        held[c, pl.ds(row, groups), :] = v[a * groups : (a + 1) * groups]
                return carry

            lax.fori_loop(0, (valid[c * parts + i] + chunk - 1) // chunk, body, 0)

    @pl.when(i >= parts)
    def _():
        rows = out.shape[0]

        def body(g, carry):
            at = pl.multiple_of(g * 8, 8)
            base = ((i - parts) * rows + at) * groups
            for j in range(groups):
                cols = pl.ds(j * LANES, LANES)
                total = before[pl.ds(at, 8), cols]
                for c in range(children):
                    total += held[c, pl.ds(base + j, 8, stride=groups), :] * unit[c, pl.ds(at, 8), :]
                out[pl.ds(at, 8), cols] = total
            return carry

        lax.fori_loop(0, rows // 8, body, 0, unroll=2)


def unpack(got, place, unit, before):
    rows, width = before.shape
    count, children, tiles = got.shape[:3]
    groups = width // LANES
    out_steps = 4

    def block(i, *_):
        return jnp.maximum(i - count, 0), 0

    valid = jnp.sum(place < rows, axis=2, dtype=jnp.int32)
    return pl.pallas_call(
        functools.partial(unpack_kernel, groups, count),
        out_shape=jax.ShapeDtypeStruct((rows, width), jnp.float32),
        grid_spec=pltpu.PrefetchScalarGridSpec(
            num_scalar_prefetch=2,
            grid=(count + out_steps,),
            in_specs=[
                pl.BlockSpec((1, children, tiles, 16, LANES), lambda i, *_: (jnp.minimum(i, count - 1), 0, 0, 0, 0)),
                pl.BlockSpec((rows // out_steps, width), block),
                pl.BlockSpec((children, rows // out_steps, LANES), lambda i, *_: (0, block(i)[0], 0)),
            ],
            out_specs=pl.BlockSpec((rows // out_steps, width), block),
            scratch_shapes=[pltpu.VMEM((children, (rows + 8) * groups, LANES), jnp.float32)],
        ),
        compiler_params=pltpu.CompilerParams(vmem_limit_bytes=VMEM_LIMIT),
        cost_estimate=takes(11),
        name="unpack",
    )((place * groups).reshape(-1), valid.reshape(-1), got, before, unit)


def lower_pack_kernel(picks, low, slot, digits, out, compact):
    c = pl.program_id(0)
    rows, wide = compact.shape
    pairs = wide // TILE
    count, _, room, _ = out.shape
    for i in range(rows // TILE):
        for j in range(pairs):
            column = (2 * j + picks[(c * (rows // TILE) + i) * pairs + j]) * TILE
            at = pl.ds(i * TILE, TILE)
            compact[at, j * TILE : (j + 1) * TILE] = low[0, at, pl.ds(pl.multiple_of(column, TILE), TILE)]

    def body(t, carry):
        ids = lax.broadcasted_iota(jnp.int32, (max(room, wide), rows), 0) + t * room
        hit = jnp.where(slot[0] == ids, 1.0, 0.0).astype(jnp.bfloat16)
        mine = jnp.dot(hit[:room], compact[...], preferred_element_type=jnp.float32)
        out[t, 0] = mine.astype(jnp.bfloat16)
        notes = lax.dot_general(
            digits[0], hit[:wide], (((1,), (1,)), ((), ())), preferred_element_type=jnp.float32
        )
        out[t, 0, room - NOTES :, :] = notes.astype(jnp.bfloat16)
        return carry

    lax.fori_loop(0, count, body, 0)


def lower_pack(lower, picks, slot, digits, count, room):
    children, rows, depth = lower.shape
    wide = depth // 2
    return pl.pallas_call(
        lower_pack_kernel,
        out_shape=jax.ShapeDtypeStruct((count, children, room, wide), jnp.bfloat16),
        grid_spec=pltpu.PrefetchScalarGridSpec(
            num_scalar_prefetch=1,
            grid=(children,),
            in_specs=[
                pl.BlockSpec((1, rows, depth), lambda c, p: (c, 0, 0)),
                pl.BlockSpec((1, 1, rows), lambda c, p: (c, 0, 0)),
                pl.BlockSpec((1, NOTES, rows), lambda c, p: (c, 0, 0)),
            ],
            out_specs=pl.BlockSpec((count, 1, room, wide), lambda c, p: (0, c, 0, 0)),
            scratch_shapes=[pltpu.VMEM((rows, wide), jnp.bfloat16)],
        ),
        compiler_params=pltpu.CompilerParams(vmem_limit_bytes=VMEM_LIMIT),
        cost_estimate=takes(7),
        name="lower_pack",
    )(picks.reshape(-1), lower, slot.reshape(children, 1, rows), digits)


def lower_unpack_kernel(got, place, code, unit, out, units):
    count, _, room, wide = got.shape
    slots = count * room
    rows = out.shape[1]
    step = 256

    def body(t, carry):
        at = pl.multiple_of(t * step, step)
        ids = lax.broadcasted_iota(jnp.int32, (step, slots), 0) + at
        hit = place[0] == ids
        mine = jnp.dot(
            jnp.where(hit, 1.0, 0.0).astype(jnp.bfloat16),
            got[...].reshape(slots, wide),
            preferred_element_type=jnp.float32,
        )
        bits = jnp.sum(jnp.where(hit, code[0], 0.0), axis=1, keepdims=True).astype(jnp.int32)
        row = jnp.sum(jnp.where(hit, unit[0], 0.0), axis=1, keepdims=True)
        units[0, pl.ds(at, step), :] = jnp.broadcast_to(row, (step, LANES))
        for j in range(wide // TILE):
            bit = (bits >> j) & 1
            for s in range(2):
                tile = jnp.where(bit == s, mine[:, j * TILE : (j + 1) * TILE], 0.0)
                out[0, pl.ds(at, step), (2 * j + s) * TILE : (2 * j + s + 1) * TILE] = tile.astype(jnp.bfloat16)
        return carry

    lax.fori_loop(0, rows // step, body, 0)


def lower_unpack(got, rows, *lanes):
    count, children, room, wide = got.shape
    slots = count * room
    lane = pl.BlockSpec((1, 1, slots), lambda c: (c, 0, 0))
    whole = lambda n: pl.BlockSpec((1, rows, n), lambda c: (c, 0, 0))
    return pl.pallas_call(
        lower_unpack_kernel,
        out_shape=(
            jax.ShapeDtypeStruct((children, rows, 2 * wide), jnp.bfloat16),
            jax.ShapeDtypeStruct((children, rows, LANES), jnp.float32),
        ),
        grid=(children,),
        in_specs=[pl.BlockSpec((count, 1, room, wide), lambda c: (0, c, 0, 0))] + [lane] * len(lanes),
        out_specs=(whole(2 * wide), whole(LANES)),
        compiler_params=pltpu.CompilerParams(vmem_limit_bytes=VMEM_LIMIT),
        cost_estimate=takes(5),
        name="lower_unpack",
    )(got, *[x.reshape(children, 1, slots) for x in lanes])


def product_kernel(children, steps, parts, blocks, starts, front, *refs):
    lows, ups = refs[:parts], refs[parts : parts + blocks]
    out, low_all, up_all, sems = refs[parts + blocks :]
    i = pl.program_id(0)
    rows = front.shape[0]
    depth = low_all.shape[1] // children

    @pl.when(i == 0)
    def _():
        copies = []
        for c in range(children):
            for n, low in enumerate(lows):
                at = pl.ds(pl.multiple_of(c * depth + starts[n], low.shape[2]), low.shape[2])
                copies.append(pltpu.make_async_copy(low.at[c], low_all.at[:, at], sems.at[len(copies)]))
            for n, up in enumerate(ups):
                at = pl.ds(pl.multiple_of(c * depth + starts[parts + n], up.shape[1]), up.shape[1])
                copies.append(pltpu.make_async_copy(up.at[c], up_all.at[at], sems.at[len(copies)]))
        for copy in copies:
            copy.start()
        for copy in copies:
            copy.wait()

    here = pl.ds(pl.multiple_of(i * rows, rows), rows)
    out[...] = front[...] - jnp.dot(low_all[here, :], up_all[...], preferred_element_type=jnp.float32)


def product(front, lows, ups, starts):
    rows, width = front.shape
    children = ups[0].shape[0]
    depth = children * sum(up.shape[1] for up in ups)
    steps = 4
    block = pl.BlockSpec((rows // steps, width), lambda i, s: (i, 0))
    return pl.pallas_call(
        functools.partial(product_kernel, children, steps, len(lows), len(ups)),
        out_shape=jax.ShapeDtypeStruct((rows, width), jnp.float32),
        grid_spec=pltpu.PrefetchScalarGridSpec(
            num_scalar_prefetch=1,
            grid=(steps,),
            in_specs=[block] + [ANY] * (len(lows) + len(ups)),
            out_specs=block,
            scratch_shapes=[
                pltpu.VMEM((rows, depth), jnp.bfloat16),
                pltpu.VMEM((depth, width), jnp.bfloat16),
                pltpu.SemaphoreType.DMA((children * (len(lows) + len(ups)),)),
            ],
        ),
        compiler_params=pltpu.CompilerParams(vmem_limit_bytes=VMEM_LIMIT),
        cost_estimate=takes(15),
        name="product",
    )(starts, front, *lows, *ups)


class Relay:
    def __init__(self, block, count):
        self.inner = inner_factor(count)
        self.outer = count // self.inner
        self.z = lax.axis_index("row") // self.inner
        self.x = lax.axis_index("row") % self.inner
        self.up = self.down = block
        self.came = {}
        self.order = [
            [(k, d) for k in range(1, self.outer) for d in (1, -1) if 0 <= z - d * k < self.outer]
            for z in range(self.outer)
        ]
        self.held = [[block] + self.exchange(block, range(self.outer))]
        self.k = 0

    def send(self, x, moves, turn=0):
        n = self.inner
        return lax.ppermute(
            x, "row", [(z * n + i, to * n + (i + turn) % n) for z, to in moves.items() for i in range(n)]
        )

    def exchange(self, x, where):
        return [self.send(x, {z: z for z in where}, j) for j in range(1, self.inner)]

    def choose(self, number, where):
        names = {z: self.order[z][number - 1] for z in where}
        every = sorted(set(names.values()))
        block = self.came[every[0]]
        for name in every[1:]:
            here = functools.reduce(jnp.logical_or, [self.z == z for z in where if names[z] == name])
            block = jnp.where(here, self.came[name], block)
        return block

    def step(self):
        if self.k:
            block = self.choose(self.k, range(self.outer))
            self.held.append([block] + self.exchange(block, range(self.outer)))
        self.k += 1
        last = self.outer - 1
        if self.k == last:
            self.inside = self.choose(last, range(1, last))
            self.at_ends = self.send(self.inside, {1: 0, last - 1: last})
            return
        self.up = self.send(self.up, {z: z + 1 for z in range(self.k - 1, last)})
        self.down = self.send(self.down, {z: z - 1 for z in range(1, last - self.k + 2)})
        self.came[self.k, 1], self.came[self.k, -1] = self.up, self.down

    def pass_gate(self, arrays):
        mine = self.held[self.k - 1][1:]
        count = len(mine)
        self.up, self.down, *rest = gate([self.up, self.down, *mine, *arrays])
        self.came[self.k, 1], self.came[self.k, -1] = self.up, self.down
        self.held[self.k - 1][1:] = rest[:count]
        return rest[count:]

    def finish(self, arrays):
        mine = self.held[-1][1:]
        self.at_ends, *rest = gate([self.at_ends, *mine, *arrays])
        self.held[-1][1:] = rest[: len(mine)]
        block = jnp.where((self.z == 0) | (self.z == self.outer - 1), self.at_ends, self.inside)
        self.held.append([block] + self.exchange(block, range(self.outer)))
        return rest[len(mine) :]

    def blocks(self):
        found = []
        for k in range(self.outer):
            at = self.z
            if k:
                at = sum(
                    jnp.where(self.z == z, z - d * far, 0) for z, (far, d) in enumerate(o[k - 1] for o in self.order)
                )
            for j in range(self.inner):
                found.append((at * self.inner + (self.x - j + self.inner) % self.inner, self.held[k][j]))
        return found


def exchange_columns(found, bit):
    pairs = [(i, i ^ bit) for i in range(lax.axis_size("col"))]
    return found + [(far ^ bit, lax.ppermute(x, "col", pairs)) for far, x in found]


def shards(schur, lower, upper, tile_mask, row_map, front):
    children, rows, local_depth = lower.shape
    count = lax.axis_size("row")
    cap = 3 * rows // (2 * count)
    room = cap + NOTES
    row_tiles = rows // TILE
    pairs = local_depth // (2 * TILE)

    relay = Relay(upper, count)
    relay.step()

    target = row_map // rows
    place = row_map % rows
    earlier = jnp.tril(jnp.ones((rows, rows), jnp.bool_), -1)
    rank = jnp.sum((target[:, :, None] == target[:, None, :]) & earlier[None], axis=2, dtype=jnp.int32)
    picks = tile_mask.reshape(children, row_tiles, pairs, 2)[..., 1]
    code = jnp.sum(picks * (2 ** jnp.arange(pairs, dtype=jnp.int32)), axis=-1)
    code = jnp.repeat(code, TILE, axis=1)
    row_ids = jnp.broadcast_to(jnp.arange(rows, dtype=jnp.int32), (children, rows))
    digits = [place // BASE + 1, place % BASE, code, row_ids // BASE, row_ids % BASE]
    digits = [d.astype(jnp.bfloat16) for d in digits] + [row_unit(schur)[..., 0]]
    digits = jnp.stack(digits + [jnp.zeros_like(digits[0])] * (NOTES - len(digits)), axis=1)

    (digits,) = relay.pass_gate([digits])
    relay.step()
    sent_lower = lower_pack(lower, picks, target * room + rank, digits, count, room)
    notes = sent_lower[:, :, cap + 3 : cap + 5, :cap].astype(jnp.int32)
    source = (notes[:, :, 0] * BASE + notes[:, :, 1]).transpose(1, 0, 2).reshape(children, -1)
    sent = pack(schur, 0, source[0], count, None)
    while relay.k < relay.outer - 2:
        (sent,) = relay.pass_gate([sent])
        relay.step()
    sent_lower, sent, source = relay.pass_gate([sent_lower, sent, source])
    got_lower = lax.all_to_all(sent_lower, "row", split_axis=0, concat_axis=0, tiled=True)
    relay.step()
    for child in range(1, children):
        sent = pack(schur, child, source[child], count, sent)
    sent, got_lower = gate([sent, got_lower])
    got = lax.all_to_all(sent, "row", split_axis=0, concat_axis=0, tiled=True)

    notes = got_lower[:, :, cap : cap + NOTES, :cap].transpose(2, 1, 0, 3)
    got_place = notes[0].astype(jnp.int32) * BASE + notes[1].astype(jnp.int32) - BASE
    got_place = jnp.where(got_place >= 0, got_place, rows)
    spare = ((0, 0), (0, 0), (0, NOTES))
    full, units = lower_unpack(
        got_lower,
        rows,
        jnp.pad(got_place, spare, constant_values=rows),
        jnp.pad(notes[2].astype(jnp.float32), spare),
        jnp.pad(notes[5].astype(jnp.float32), spare),
    )

    full, units = relay.finish([full, units])
    column = lax.axis_index("col")
    bit = lax.axis_size("col")
    lows = [(0, full)]
    while bit > 1:
        bit //= 2
        lows = exchange_columns(lows, bit)
    ups = relay.blocks()
    starts = [(column ^ far) * local_depth for far, _ in lows] + [owner * upper.shape[1] for owner, _ in ups]
    result = product(front, [low for _, low in lows], [up for _, up in ups], jnp.stack(starts).astype(jnp.int32))
    return unpack(got, got_place, units, result)


def solution(mesh):
    in_specs = (
        P(None, "row", "col"),
        P(None, "row", "col"),
        P(None, "row", "col"),
        P(None, "row", "col"),
        P(None, "row"),
        P("row", "col"),
    )
    out_specs = P("row", "col")
    return jax.shard_map(shards, mesh=mesh, in_specs=in_specs, out_specs=out_specs, check_vma=False)
```

time: 365 us -> 268 us (0.73)
  blocking collectives: 49.3 us -> 0 us
  starting transfers between devices: 58.5 us -> 32 us
  local copies, waits for them, and re-layouts: 37.4 us -> 15.6 us
  Pallas kernels: 47.2 us -> 65.9 us
  between operations: 14.2 us -> 0.33 us
  matrix products: 10.3 us -> 0 us
  waiting for transfers between devices: 129 us -> 137 us
    all_gather x1 -> x0, blocking collectives: 49.3 us -> none  [shards(): notes = lax.all_gather(jnp.stack([tags, scales]), 'row', axis=0)]
    all_to_all x3 -> x2, starting transfers between devices: 37.4 us -> 12.8 us  [the longest x1 8.04 us: shards(): lax.all_to_all(sent_lower, 'row', split_axis=0, concat_axis=0, tiled=True)]
    pallas_call x6 -> x8, Pallas kernels: 29.9 us -> 46.3 us  [the longest x1 18.3 us: product(): pl.pallas_call(functools.partial(product_kernel, children, steps, len(low...]
    ppermute x13 -> x12, waiting for transfers between devices: 94.2 us -> 110 us  [the longest x9 65.6 us: send(): lax.ppermute(x, 'row', [(z * n + i, to * n + (i + turn) % n) for z, to in...]
    unnamed x55 -> x24, local copies, waits for them, and re-layouts: 18.3 us -> 4.96 us
    dot_general x1 -> x0, matrix products: 10.3 us -> none  [shards(): jnp.dot(jnp.concatenate(lefts, axis=1), jnp.concatenate(rights, axis=0),...]
    squeeze x3 -> x1, local copies, waits for them, and re-layouts: 10.4 us -> 0.67 us  [shards(): sent = pack(schur, 0, source[0], count, None)]
    all_to_all x3 -> x2, waiting for transfers between devices: 34.7 us -> 26.8 us  [the longest x1 20.9 us: shards(): lax.all_to_all(sent_lower, 'row', split_axis=0, concat_axis=0, tiled=True)]
  transfers between devices with their start and end apart: 17 -> 14, of which waited for: 6 -> 10; matrix products, arithmetic and copies ran while one was open for 14% -> 10% of each run, Pallas kernels for 8% -> 20%
where the time goes in v4:
time: 268 us; the launch traced here: 267 us
  waiting for transfers between devices  137 us (51%)
  Pallas kernels  65.9 us (25%)
  starting transfers between devices  32 us (12%)
  other arithmetic  16.2 us (6%)
  local copies, waits for them, and re-layouts  15.6 us (6%)
    ppermute x9, waiting for transfers between devices, send(): lax.ppermute(x, 'row', [(z * n + i, to * n + (i + turn) % n) for z, to in...  65.6 us
    ppermute x3, waiting for transfers between devices, exchange_columns(): lax.ppermute(x, 'col', pairs)  44.2 us
    all_to_all x1, waiting for transfers between devices, shards(): lax.all_to_all(sent_lower, 'row', split_axis=0, concat_axis=0, tiled=True)  20.9 us
    pallas_call x2, Pallas kernels, pack(): pl.pallas_call(functools.partial(pack_kernel, groups, steps), out_shape=j...  19.7 us
    pallas_call x1, Pallas kernels, product(): pl.pallas_call(functools.partial(product_kernel, children, steps, len(low...  18.3 us
    ppermute x9, starting transfers between devices, send(): lax.ppermute(x, 'row', [(z * n + i, to * n + (i + turn) % n) for z, to in...  17.7 us
    pallas_call x1, Pallas kernels, unpack(): pl.pallas_call(functools.partial(unpack_kernel, groups, count), out_shape...  12.7 us
    pallas_call x1, Pallas kernels, lower_pack(): pl.pallas_call(lower_pack_kernel, out_shape=jax.ShapeDtypeStruct((count,...  9.13 us
  transfers between devices with their start and end apart: 14, of which 10 were waited for; matrix products, arithmetic and copies ran while one was open for 10% of the time, Pallas kernels for 20%

profile of v4, /device:TPU:0, one launch (start us, length us, event | category | flops | bytes accessed | tf_op | source)
XLA Modules:
  0.0 266.6 jit_solution(12581857028747655183)
XLA Ops:
  0.0 1.3 collective-permute-start.1
  1.3 5.6 %collective-permute-start = (bf16[2,256,1024]{2,1,0:T(8,128)(2,1)}, bf16[2,256,1024]{2,1,0:T(8,128)(2,1)S(1)}, u32[]{:S(2)}, u32[]{:S(2)}) collective-permute-start(bf16[2,256,1024]{2,1,0:T(8,128)(2,1)} %refs_4_.1), channel_id=1, source_target_pairs={{0,8},{4,12},{8,16},{12,20},{16,24},{20,28},{1,9},{5,13},{9,17},{1... | collective-permute-start | bytes 3145736 | tf_op jit(solution)/shard_map/ppermute | solution.py:354
  6.9 2.0 collective-permute-start.2
  8.9 0.7 slice.45
  9.6 0.1 copy.67
  9.7 0.1 multiply_reduce_fusion
  9.8 0.1 broadcast_in_dim.38
  9.9 0.7 reshape_squeeze.3.picks
  10.6 4.1 %abs_reduce_fusion = f32[2,1024]{1,0:T(2,128)S(1)} fusion(f32[2,1024,1024]{2,1,0:T(8,128)} %x.9), kind=kLoop, calls=%fused_computation.1 | loop fusion | flops 4192256 | bytes 8396800 | tf_op jit(solution)/shard_map/reduce_max | solution.py:49
  14.7 0.1 fusion.16
  14.8 0.7 iota_compare_fusion
  15.5 1.9 convert_reduce_fusion
  17.4 0.6 reshape.254.slot
  18.1 1.3 stack.61.refs_3_
  19.4 8.9 %collective-permute-done.1.refs_1_ = bf16[2,256,1024]{2,1,0:T(8,128)(2,1)S(1)} collective-permute-done((bf16[2,256,1024]{2,1,0:T(8,128)(2,1)}, bf16[2,256,1024]{2,1,0:T(8,128)(2,1)S(1)}, u32[]{:S(2)}, u32[]{:S(2)}) %collective-permute-start.1) | collective-permute-done | bytes 1048608 | tf_op jit(solution)/shard_map/ppermute | solution.py:354
  28.3 1.3 collective-permute-done.refs_0_
  29.6 2.2 collective-permute-done.2.refs_2_
  31.8 1.0 copy-done.7
  32.8 0.7 collective-permute-start.3
  33.5 1.3 collective-permute-start.4
  34.8 2.3 broadcast_select_fusion.2.refs_6_
  37.2 1.6 collective-permute-start.5
  38.8 9.1 %lower_pack.1.refs_3_ = bf16[8,2,208,256]{3,2,1,0:T(8,128)(2,1)} custom-call(s32[32]{0:T(128)} %reshape_squeeze.3.picks, bf16[2,1024,512]{2,1,0:T(8,128)(2,1)} %low.1, s32[2,1,1024]{2,1,0:T(1,128)} %reshape.254.slot, bf16[2,16,1024]{2,1,0:T(8,128)(2,1)} %get-tuple-element.25.digits), custom_call_target="tpu_custom_call" | custom-call | flops 28000000000 | bytes 23100000 | tf_op jit(solution)/shard_map/lower_pack/pallas_call | solution.py:217
  47.9 0.9 slice_convert_fusion.2
  48.9 0.7 squeeze.7.source
  49.6 9.8 %pack.2.refs_4_ = s16[8,2,96,16,128]{4,3,2,1,0:T(8,128)(2,1)} custom-call(s32[1536]{0:T(1024)} %squeeze.7.source, f32[2,1024,1024]{2,1,0:T(8,128)} %x.9), custom_call_target="tpu_custom_call" | custom-call | flops 40000000000 | bytes 33000000 | tf_op jit(solution)/shard_map/pack/pallas_call | solution.py:98
  59.4 0.7 reshape.255.refs_5_
  60.1 1.1 collective-permute-done.5.refs_2_
  61.2 0.0 collective-permute-done.3.refs_0_
  61.2 0.4 collective-permute-done.4.refs_1_
  61.6 0.6 copy-done.5
  62.2 1.1 copy-done.6
  63.3 1.3 slice_reduce_fusion.1.source
  64.6 8.0 %all-to-all-start = ((bf16[8,2,208,256]{3,2,1,0:T(8,128)(2,1)}), bf16[8,2,208,256]{3,2,1,0:T(8,128)(2,1)S(1)}, u32[]{:S(2)}, u32[]{:S(2)}) async-start(bf16[8,2,208,256]{3,2,1,0:T(8,128)(2,1)} %get-tuple-element.28), calls=%async_computation | async-start | bytes 3407872 | tf_op jit(solution)/shard_map/all_to_all | solution.py:451
  72.7 3.1 %select_select_fusion = (bf16[2,256,1024]{2,1,0:T(8,128)(2,1)}, bf16[2,256,1024]{2,1,0:T(8,128)(2,1)}) fusion(bf16[2,256,1024]{2,1,0:T(8,128)(2,1)} %get-tuple-element.31, bf16[2,256,1024]{2,1,0:T(8,128)(2,1)} %get-tuple-element.32, bf16[2,256,1024]{2,1,0:T(8,128)(2,1)S(1)} %copy-done.1, pred[]{:T(512)S(6)} %eq.61, pred[]{:T(512)S(6)} %eq.30, pred[]{:T(512)S(6)} %eq.29), kind=kLoop, calls=%fused_computation.3 | loop fusion | flops 1572864 | bytes 5242883 | tf_op jit(solution)/shard_map/jit(_where)/select_n | solution.py:367
  75.8 2.0 collective-permute-start.7
  77.8 1.3 collective-permute-start.6
  79.1 9.8 %pack.3.refs_0_ = s16[8,2,96,16,128]{4,3,2,1,0:T(8,128)(2,1)} custom-call(s32[1536]{0:T(1024)} %slice_reduce_fusion.1.source, f32[2,1024,1024]{2,1,0:T(8,128)} %x.9, s16[8,2,96,16,128]{4,3,2,1,0:T(8,128)(2,1)} %get-tuple-element.27.refs_0_), custom_call_target="tpu_custom_call", output_to_operand_aliasing={{}: (2, {})} | custom-call | flops 40000000000 | bytes 33000000 | tf_op jit(solution)/shard_map/pack/pallas_call | solution.py:98
  89.0 20.9 %all-to-all-done.refs_1_ = bf16[8,2,208,256]{3,2,1,0:T(8,128)(2,1)S(1)} async-done(((bf16[8,2,208,256]{3,2,1,0:T(8,128)(2,1)}), bf16[8,2,208,256]{3,2,1,0:T(8,128)(2,1)S(1)}, u32[]{:S(2)}, u32[]{:S(2)}) %all-to-all-start) | async-done | bytes 1703968 | tf_op jit(solution)/shard_map/all_to_all | solution.py:451
  109.9 1.2 copy-done.2
  111.1 0.9 slice_bitcast_fusion
  112.1 4.8 %all-to-all-start.1 = ((s16[8,2,96,16,128]{4,3,2,1,0:T(8,128)(2,1)}), s16[8,2,96,16,128]{4,3,2,1,0:T(8,128)(2,1)}, u32[]{:S(2)}, u32[]{:S(2)}) async-start(s16[8,2,96,16,128]{4,3,2,1,0:T(8,128)(2,1)} %get-tuple-element.30), calls=%async_computation.1 | async-start | bytes 12582912 | tf_op jit(solution)/shard_map/all_to_all | solution.py:456
  116.9 0.7 reshape.265.unit
  117.6 0.7 reshape.263.code
  118.3 0.2 fusion
  118.5 0.7 reshape.257.place
  119.2 6.1 %lower_unpack.1 = (bf16[2,1024,512]{2,1,0:T(8,128)(2,1)}, f32[2,1024,128]{2,1,0:T(8,128)}) custom-call(bf16[8,2,208,256]{3,2,1,0:T(8,128)(2,1)} %get-tuple-element.29.got, s32[2,1,1664]{2,1,0:T(1,128)} %reshape.257.place, f32[2,1,1664]{2,1,0:T(1,128)} %reshape.263.code, f32[2,1,1664]{2,1,0:T(1,128)} %reshape.265.unit), custom_call_target="tpu_custom_call" | custom-call | flops 20000000000 | bytes 16500000 | tf_op jit(solution)/shard_map/lower_unpack/pallas_call | solution.py:270
  125.4 0.0 collective-permute-done.7.refs_1_
  125.4 0.4 collective-permute-done.6.refs_0_
  125.8 1.0 copy-done.4
  126.8 1.5 collective-permute-start.8
  128.3 0.0 collective-permute-start.9
  128.3 44.2 %collective-permute-done.8.refs_1_ = bf16[2,1024,512]{2,1,0:T(8,128)(2,1)S(1)} collective-permute-done((bf16[2,1024,512]{2,1,0:T(8,128)(2,1)}, bf16[2,1024,512]{2,1,0:T(8,128)(2,1)S(1)}, u32[]{:S(2)}, u32[]{:S(2)}) %collective-permute-start.8) | collective-permute-done | bytes 2097184 | tf_op jit(solution)/shard_map/ppermute | solution.py:415
  172.5 2.1 broadcast_select_fusion.refs_10_
  174.6 1.8 collective-permute-start.11
  176.4 0.6 stack.74.starts
  177.0 0.1 sub.35
  177.1 0.1 copy.70
  177.2 0.6 reshape.256.valid
  177.8 0.6 fusion.4.row_at
  178.4 51.3 %collective-permute-done.11.refs_11_ = bf16[2,256,1024]{2,1,0:T(8,128)(2,1)} collective-permute-done((bf16[2,256,1024]{2,1,0:T(8,128)(2,1)S(1)}, bf16[2,256,1024]{2,1,0:T(8,128)(2,1)}, u32[]{:S(2)}, u32[]{:S(2)}) %collective-permute-start.11) | collective-permute-done | bytes 1048608 | tf_op jit(solution)/shard_map/ppermute | solution.py:354
  229.7 18.3 %product.1.before = f32[1024,1024]{1,0:T(8,128)} custom-call(s32[12]{0:T(128)} %stack.74.starts, f32[1024,1024]{1,0:T(8,128)} %front.1, bf16[2,1024,512]{2,1,0:T(8,128)(2,1)} %get-tuple-element.35.refs_0_, bf16[2,1024,512]{2,1,0:T(8,128)(2,1)} %copy-done.10, bf16[2,1024,512]{2,1,0:T(8,128)(2,1)} %collective-permute-done.9.refs_2_, ...), custom_call_target="tpu_custom_call" | custom-call | flops 60000002048 | bytes 49500000 | tf_op jit(solution)/shard_map/product/pallas_call | solution.py:317
  248.0 5.9 %all-to-all-done.1.got = s16[8,2,96,16,128]{4,3,2,1,0:T(8,128)(2,1)} async-done(((s16[8,2,96,16,128]{4,3,2,1,0:T(8,128)(2,1)}), s16[8,2,96,16,128]{4,3,2,1,0:T(8,128)(2,1)}, u32[]{:S(2)}, u32[]{:S(2)}) %all-to-all-start.1) | async-done | bytes 6291488 | tf_op jit(solution)/shard_map/all_to_all | solution.py:456
  253.9 12.7 %unpack.1 = f32[1024,1024]{1,0:T(8,128)} custom-call(s32[3072]{0:T(1024)} %fusion.4.row_at, s32[16]{0:T(128)} %reshape.256.valid, s16[8,2,96,16,128]{4,3,2,1,0:T(8,128)(2,1)} %all-to-all-done.1.got, f32[1024,1024]{1,0:T(8,128)} %product.1.before, f32[2,1024,128]{2,1,0:T(8,128)} %get-tuple-element.40.unit), custom_call_target="tpu_custom_call" | custom-call | flops 44000002048 | bytes 36300000 | tf_op jit(solution)/shard_map/unpack/pallas_call | solution.py:169
  (55 shorter events, 0.4 us)
Async XLA Ops:
  0.0 28.3 %collective-permute-start.1 = (bf16[2,256,1024]{2,1,0:T(8,128)(2,1)}, bf16[2,256,1024]{2,1,0:T(8,128)(2,1)S(1)}, u32[]{:S(2)}, u32[]{:S(2)}) collective-permute-start(bf16[2,256,1024]{2,1,0:T(8,128)(2,1)} %refs_4_.1), channel_id=1, source_target_pairs={{8,0},{12,4},{16,8},{20,12},{24,16},{28,20},{9,1},{13,5},{17,9},{2... | collective-permute-start | bytes 3145736 | tf_op jit(solution)/shard_map/ppermute | solution.py:354
  1.3 28.3 %collective-permute-start = (bf16[2,256,1024]{2,1,0:T(8,128)(2,1)}, bf16[2,256,1024]{2,1,0:T(8,128)(2,1)S(1)}, u32[]{:S(2)}, u32[]{:S(2)}) collective-permute-start(bf16[2,256,1024]{2,1,0:T(8,128)(2,1)} %refs_4_.1), channel_id=1, source_target_pairs={{0,8},{4,12},{8,16},{12,20},{16,24},{20,28},{1,9},{5,13},{9,17},{1... | collective-permute-start | bytes 3145736 | tf_op jit(solution)/shard_map/ppermute | solution.py:354
  6.9 24.9 %collective-permute-start.2 = (bf16[2,256,1024]{2,1,0:T(8,128)(2,1)}, bf16[2,256,1024]{2,1,0:T(8,128)(2,1)S(1)}, u32[]{:S(2)}, u32[]{:S(2)}) collective-permute-start(bf16[2,256,1024]{2,1,0:T(8,128)(2,1)} %refs_4_.1), channel_id=1, source_target_pairs={{0,4},{4,0},{8,12},{12,8},{16,20},{20,16},{24,28},{28,24},{1,5},{5... | collective-permute-start | bytes 3145736 | tf_op jit(solution)/shard_map/ppermute | solution.py:354
  10.6 4.1 %copy-start.9 = (s32[2,1024]{1,0:T(2,128)S(1)}, s32[2,1024]{1,0:T(2,128)}, u32[]{:S(2)}) copy-start(s32[2,1024]{1,0:T(2,128)} %param.10) | copy-start | bytes 24580
  28.3 3.5 %copy-start = (bf16[2,256,1024]{2,1,0:T(8,128)(2,1)}, bf16[2,256,1024]{2,1,0:T(8,128)(2,1)S(1)}, u32[]{:S(2)}) copy-start(bf16[2,256,1024]{2,1,0:T(8,128)(2,1)S(1)} %collective-permute-done.1.refs_1_) | copy-start | bytes 3145732
  29.6 2.3 copy-start.3
  31.8 1.0 copy-start.7
  32.8 28.4 %collective-permute-start.3 = (bf16[2,256,1024]{2,1,0:T(8,128)(2,1)}, bf16[2,256,1024]{2,1,0:T(8,128)(2,1)S(1)}, u32[]{:S(2)}, u32[]{:S(2)}) collective-permute-start(bf16[2,256,1024]{2,1,0:T(8,128)(2,1)} %get-tuple-element.23), channel_id=1, source_target_pairs={{8,16},{12,20},{16,24},{20,28},{9,17},{13,21},{17,25},{21,29},{10,... | collective-permute-start | bytes 3145736 | tf_op jit(solution)/shard_map/ppermute | solution.py:354
  33.5 28.1 %collective-permute-start.4 = (bf16[2,256,1024]{2,1,0:T(8,128)(2,1)}, bf16[2,256,1024]{2,1,0:T(8,128)(2,1)S(1)}, u32[]{:S(2)}, u32[]{:S(2)}) collective-permute-start(bf16[2,256,1024]{2,1,0:T(8,128)(2,1)} %get-tuple-element.24), channel_id=1, source_target_pairs={{8,0},{12,4},{16,8},{20,12},{9,1},{13,5},{17,9},{21,13},{10,2},{14... | collective-permute-start | bytes 3145736 | tf_op jit(solution)/shard_map/ppermute | solution.py:354
  37.2 24.0 %collective-permute-start.5 = (bf16[2,256,1024]{2,1,0:T(8,128)(2,1)}, bf16[2,256,1024]{2,1,0:T(8,128)(2,1)}, u32[]{:S(2)}, u32[]{:S(2)}) collective-permute-start(bf16[2,256,1024]{2,1,0:T(8,128)(2,1)} %broadcast_select_fusion.2.refs_6_), channel_id=1, source_target_pairs={{0,4},{4,0},{8,12},{12,8},{16,20},{20,16},{24,28},{28,24},{1,5},{5... | collective-permute-start | bytes 3145736 | tf_op jit(solution)/shard_map/ppermute | solution.py:354
  60.1 12.6 %copy-start.1 = (bf16[2,256,1024]{2,1,0:T(8,128)(2,1)S(1)}, bf16[2,256,1024]{2,1,0:T(8,128)(2,1)}, u32[]{:S(2)}) copy-start(bf16[2,256,1024]{2,1,0:T(8,128)(2,1)} %get-tuple-element.24) | copy-start | bytes 3145732
  61.2 1.0 copy-start.5
  62.2 1.1 copy-start.6
  64.6 45.3 %all-to-all-start = ((bf16[8,2,208,256]{3,2,1,0:T(8,128)(2,1)}), bf16[8,2,208,256]{3,2,1,0:T(8,128)(2,1)S(1)}, u32[]{:S(2)}, u32[]{:S(2)}) async-start(bf16[8,2,208,256]{3,2,1,0:T(8,128)(2,1)} %get-tuple-element.28), calls=%async_computation | async-start | bytes 3407872 | tf_op jit(solution)/shard_map/all_to_all | solution.py:451
  75.8 49.6 %collective-permute-start.7 = (bf16[2,256,1024]{2,1,0:T(8,128)(2,1)}, bf16[2,256,1024]{2,1,0:T(8,128)(2,1)}, u32[]{:S(2)}, u32[]{:S(2)}) collective-permute-start(bf16[2,256,1024]{2,1,0:T(8,128)(2,1)} %get-tuple-element.45.refs_8_), channel_id=1, source_target_pairs={{0,4},{4,0},{8,12},{12,8},{16,20},{20,16},{24,28},{28,24},{1,5},{5... | collective-permute-start | bytes 3145736 | tf_op jit(solution)/shard_map/ppermute | solution.py:354
  77.8 48.0 %collective-permute-start.6 = (bf16[2,256,1024]{2,1,0:T(8,128)(2,1)}, bf16[2,256,1024]{2,1,0:T(8,128)(2,1)S(1)}, u32[]{:S(2)}, u32[]{:S(2)}) collective-permute-start(bf16[2,256,1024]{2,1,0:T(8,128)(2,1)} %get-tuple-element.46), channel_id=1, source_target_pairs={{8,0},{12,4},{16,24},{20,28},{9,1},{13,5},{17,25},{21,29},{10,2},{... | collective-permute-start | bytes 3145736 | tf_op jit(solution)/shard_map/ppermute | solution.py:354
  109.9 1.2 copy-start.2
  112.1 141.8 %all-to-all-start.1 = ((s16[8,2,96,16,128]{4,3,2,1,0:T(8,128)(2,1)}), s16[8,2,96,16,128]{4,3,2,1,0:T(8,128)(2,1)}, u32[]{:S(2)}, u32[]{:S(2)}) async-start(s16[8,2,96,16,128]{4,3,2,1,0:T(8,128)(2,1)} %get-tuple-element.30), calls=%async_computation.1 | async-start | bytes 12582912 | tf_op jit(solution)/shard_map/all_to_all | solution.py:456
  125.8 1.0 copy-start.4
  126.8 45.7 %collective-permute-start.8 = (bf16[2,1024,512]{2,1,0:T(8,128)(2,1)}, bf16[2,1024,512]{2,1,0:T(8,128)(2,1)S(1)}, u32[]{:S(2)}, u32[]{:S(2)}) collective-permute-start(bf16[2,1024,512]{2,1,0:T(8,128)(2,1)} %get-tuple-element.35.refs_0_), channel_id=1, source_target_pairs={{0,2},{1,3},{2,0},{3,1},{4,6},{5,7},{6,4},{7,5},{8,10},{9,11},{10,... | collective-permute-start | bytes 6291464 | tf_op jit(solution)/shard_map/ppermute | solution.py:415
  128.3 101.3 %collective-permute-start.9 = (bf16[2,1024,512]{2,1,0:T(8,128)(2,1)}, bf16[2,1024,512]{2,1,0:T(8,128)(2,1)}, u32[]{:S(2)}, u32[]{:S(2)}) collective-permute-start(bf16[2,1024,512]{2,1,0:T(8,128)(2,1)} %get-tuple-element.35.refs_0_), channel_id=1, source_target_pairs={{0,1},{1,0},{2,3},{3,2},{4,5},{5,4},{6,7},{7,6},{8,9},{9,8},{10,11... | collective-permute-start | bytes 6291464 | tf_op jit(solution)/shard_map/ppermute | solution.py:415
  172.5 57.2 %copy-start.10 = (bf16[2,1024,512]{2,1,0:T(8,128)(2,1)}, bf16[2,1024,512]{2,1,0:T(8,128)(2,1)S(1)}, u32[]{:S(2)}) copy-start(bf16[2,1024,512]{2,1,0:T(8,128)(2,1)S(1)} %collective-permute-done.8.refs_1_) | copy-start | bytes 6291460
  172.5 57.2 %collective-permute-start.10 = (bf16[2,1024,512]{2,1,0:T(8,128)(2,1)S(1)}, bf16[2,1024,512]{2,1,0:T(8,128)(2,1)}, u32[]{:S(2)}, u32[]{:S(2)}) collective-permute-start(bf16[2,1024,512]{2,1,0:T(8,128)(2,1)S(1)} %collective-permute-done.8.refs_1_), channel_id=1, source_target_pairs={{0,1},{1,0},{2,3},{3,2},{4,5},{5,4},{6,7},{7,6},{8,9},{9,8},{10,11... | collective-permute-start | bytes 6291464 | tf_op jit(solution)/shard_map/ppermute | solution.py:415
  174.6 55.1 %copy-start.8 = (bf16[2,256,1024]{2,1,0:T(8,128)(2,1)}, bf16[2,256,1024]{2,1,0:T(8,128)(2,1)S(1)}, u32[]{:S(2)}) copy-start(bf16[2,256,1024]{2,1,0:T(8,128)(2,1)S(1)} %broadcast_select_fusion.refs_10_) | copy-start | bytes 3145732
  174.6 55.1 %collective-permute-start.11 = (bf16[2,256,1024]{2,1,0:T(8,128)(2,1)S(1)}, bf16[2,256,1024]{2,1,0:T(8,128)(2,1)}, u32[]{:S(2)}, u32[]{:S(2)}) collective-permute-start(bf16[2,256,1024]{2,1,0:T(8,128)(2,1)S(1)} %broadcast_select_fusion.refs_10_), channel_id=1, source_target_pairs={{0,4},{4,0},{8,12},{12,8},{16,20},{20,16},{24,28},{28,24},{1,5},{5... | collective-permute-start | bytes 3145736 | tf_op jit(solution)/shard_map/ppermute | solution.py:354

commit v5 on v4

--- a/solution.py
+++ b/solution.py
@@ -125,18 +125,20 @@
 
     @pl.when(i < parts)
     def _():
-        for c in range(children):
-            base = (c * parts + i) * tiles * per
+        for c, s in [(c, s) for s in range(got.shape[0]) for c in range(children)]:
+            device = i * got.shape[0] + s
+            number = c * parts * got.shape[0] + device
+            base = number * tiles * per
 
             def body(k, carry):
                 for t in range(chunk // per):
-                    v = got[0, c, k * (chunk // per) + t].astype(jnp.int32).astype(jnp.float32)
+                    v = got[s, c, k * (chunk // per) + t].astype(jnp.int32).astype(jnp.float32)
                     for a in range(per):
                         row = pl.multiple_of(row_at[base + k * chunk + t * per + a], groups)
                         held[c, pl.ds(row, groups), :] = v[a * groups : (a + 1) * groups]
                 return carry
 
-            lax.fori_loop(0, (valid[c * parts + i] + chunk - 1) // chunk, body, 0)
+            lax.fori_loop(0, (valid[number] + chunk - 1) // chunk, body, 0)
 
     @pl.when(i >= parts)
     def _():
@@ -160,20 +162,22 @@
     rows, width = before.shape
     count, children, tiles = got.shape[:3]
     groups = width // LANES
-    out_steps = 4
+    steps, out_steps = count // 2, 2
 
     def block(i, *_):
-        return jnp.maximum(i - count, 0), 0
+        return jnp.maximum(i - steps, 0), 0
 
     valid = jnp.sum(place < rows, axis=2, dtype=jnp.int32)
     return pl.pallas_call(
-        functools.partial(unpack_kernel, groups, count),
+        functools.partial(unpack_kernel, groups, steps),
         out_shape=jax.ShapeDtypeStruct((rows, width), jnp.float32),
         grid_spec=pltpu.PrefetchScalarGridSpec(
             num_scalar_prefetch=2,
-            grid=(count + out_steps,),
+            grid=(steps + out_steps,),
             in_specs=[
-                pl.BlockSpec((1, children, tiles, 16, LANES), lambda i, *_: (jnp.minimum(i, count - 1), 0, 0, 0, 0)),
+                pl.BlockSpec(
+                    (count // steps, children, tiles, 16, LANES), lambda i, *_: (jnp.minimum(i, steps - 1), 0, 0, 0, 0)
+                ),
                 pl.BlockSpec((rows // out_steps, width), block),
                 pl.BlockSpec((children, rows // out_steps, LANES), lambda i, *_: (0, block(i)[0], 0)),
             ],
@@ -438,17 +442,19 @@
     digits = [d.astype(jnp.bfloat16) for d in digits] + [row_unit(schur)[..., 0]]
     digits = jnp.stack(digits + [jnp.zeros_like(digits[0])] * (NOTES - len(digits)), axis=1)
 
-    (digits,) = relay.pass_gate([digits])
-    relay.step()
     sent_lower = lower_pack(lower, picks, target * room + rank, digits, count, room)
     notes = sent_lower[:, :, cap + 3 : cap + 5, :cap].astype(jnp.int32)
     source = (notes[:, :, 0] * BASE + notes[:, :, 1]).transpose(1, 0, 2).reshape(children, -1)
+
+    sent_lower, source = relay.pass_gate([sent_lower, source])
+    relay.step()
     sent = pack(schur, 0, source[0], count, None)
+    sent_lower, sent = gate([sent_lower, sent])
+    got_lower = lax.all_to_all(sent_lower, "row", split_axis=0, concat_axis=0, tiled=True)
     while relay.k < relay.outer - 2:
         (sent,) = relay.pass_gate([sent])
         relay.step()
-    sent_lower, sent, source = relay.pass_gate([sent_lower, sent, source])
-    got_lower = lax.all_to_all(sent_lower, "row", split_axis=0, concat_axis=0, tiled=True)
+    (sent,) = relay.pass_gate([sent])
     relay.step()
     for child in range(1, children):
         sent = pack(schur, child, source[child], count, sent)

time: 268 us -> 255 us (0.951)
  waiting for transfers between devices: 137 us -> 125 us
    all_to_all x1, waiting for transfers between devices: 20.9 us -> 10.6 us  [shards(): lax.all_to_all(sent_lower, 'row', split_axis=0, concat_axis=0, tiled=True)]
    ppermute x3, waiting for transfers between devices: 44.2 us -> 41.4 us  [exchange_columns(): lax.ppermute(x, 'col', pairs)]
    unnamed x24 -> x22, local copies, waits for them, and re-layouts: 4.96 us -> 5.49 us
  transfers between devices with their start and end apart: 14 -> 14, of which waited for: 10 -> 7; matrix products, arithmetic and copies ran while one was open for 10% -> 10% of each run, Pallas kernels for 20% -> 21%
where the time goes in v5:
time: 255 us; the launch traced here: 254 us
  waiting for transfers between devices  125 us (49%)
  Pallas kernels  63.7 us (25%)
  starting transfers between devices  33.5 us (13%)
  other arithmetic  16.2 us (6%)
  local copies, waits for them, and re-layouts  15.5 us (6%)
    ppermute x9, waiting for transfers between devices, send(): lax.ppermute(x, 'row', [(z * n + i, to * n + (i + turn) % n) for z, to in...  67.8 us
    ppermute x3, waiting for transfers between devices, exchange_columns(): lax.ppermute(x, 'col', pairs)  41.4 us
    pallas_call x2, Pallas kernels, pack(): pl.pallas_call(functools.partial(pack_kernel, groups, steps), out_shape=j...  19.6 us
    ppermute x9, starting transfers between devices, send(): lax.ppermute(x, 'row', [(z * n + i, to * n + (i + turn) % n) for z, to in...  18.5 us
    pallas_call x1, Pallas kernels, product(): pl.pallas_call(functools.partial(product_kernel, children, steps, len(low...  18.3 us
    all_to_all x1, waiting for transfers between devices, shards(): lax.all_to_all(sent_lower, 'row', split_axis=0, concat_axis=0, tiled=True)  10.6 us
    pallas_call x1, Pallas kernels, unpack(): pl.pallas_call(functools.partial(unpack_kernel, groups, steps), out_shape...  10.5 us
    pallas_call x1, Pallas kernels, lower_pack(): pl.pallas_call(lower_pack_kernel, out_shape=jax.ShapeDtypeStruct((count,...  9.13 us
  transfers between devices with their start and end apart: 14, of which 7 were waited for; matrix products, arithmetic and copies ran while one was open for 10% of the time, Pallas kernels for 21%

profile of v5, /device:TPU:0, one launch (start us, length us, event | category | flops | bytes accessed | tf_op | source)
XLA Modules:
  0.0 254.0 jit_solution(9663022320763358192)
XLA Ops:
  0.0 1.3 collective-permute-start.1
  1.3 5.6 %collective-permute-start = (bf16[2,256,1024]{2,1,0:T(8,128)(2,1)}, bf16[2,256,1024]{2,1,0:T(8,128)(2,1)S(1)}, u32[]{:S(2)}, u32[]{:S(2)}) collective-permute-start(bf16[2,256,1024]{2,1,0:T(8,128)(2,1)} %refs_4_.1), channel_id=1, source_target_pairs={{0,8},{4,12},{8,16},{12,20},{16,24},{20,28},{1,9},{5,13},{9,17},{1... | collective-permute-start | bytes 3145736 | tf_op jit(solution)/shard_map/ppermute | solution.py:358
  6.9 2.0 collective-permute-start.2
  9.0 0.7 slice.44
  9.7 0.1 copy.74
  9.8 0.1 multiply_reduce_fusion
  9.9 0.1 broadcast_in_dim.38
  10.0 0.6 reshape_squeeze.3.picks
  10.6 4.1 %abs_reduce_fusion = f32[2,1024]{1,0:T(2,128)S(1)} fusion(f32[2,1024,1024]{2,1,0:T(8,128)} %x.9), kind=kLoop, calls=%fused_computation | loop fusion | flops 4192256 | bytes 8396800 | tf_op jit(solution)/shard_map/reduce_max | solution.py:49
  14.7 0.1 fusion.16
  14.8 0.7 iota_compare_fusion
  15.4 1.9 convert_reduce_fusion
  17.4 0.6 reshape.252.slot
  18.0 1.3 stack.61.digits
  19.3 9.1 %lower_pack.1.refs_3_ = bf16[8,2,208,256]{3,2,1,0:T(8,128)(2,1)} custom-call(s32[32]{0:T(128)} %reshape_squeeze.3.picks, bf16[2,1024,512]{2,1,0:T(8,128)(2,1)} %low.1, s32[2,1,1024]{2,1,0:T(1,128)} %reshape.252.slot, bf16[2,16,1024]{2,1,0:T(8,128)(2,1)} %stack.61.digits), custom_call_target="tpu_custom_call" | custom-call | flops 28000000000 | bytes 23100000 | tf_op jit(solution)/shard_map/lower_pack/pallas_call | solution.py:221
  28.5 0.9 slice_convert_fusion.2
  29.4 0.7 reshape.253.refs_4_
  30.1 0.0 collective-permute-done.1.refs_1_
  30.1 0.0 collective-permute-done.refs_0_
  30.1 1.7 collective-permute-done.2.refs_2_
  31.8 1.0 copy-done.7
  32.8 1.4 slice_reduce_fusion
  34.2 0.7 collective-permute-start.3
  35.0 1.3 collective-permute-start.4
  36.3 2.3 broadcast_select_fusion.2.refs_6_
  38.6 1.6 collective-permute-start.5
  40.2 9.8 %pack.2.refs_1_ = s16[8,2,96,16,128]{4,3,2,1,0:T(8,128)(2,1)} custom-call(s32[1536]{0:T(1024)} %get-tuple-element.43.source, f32[2,1024,1024]{2,1,0:T(8,128)} %x.9), custom_call_target="tpu_custom_call" | custom-call | flops 40000000000 | bytes 33000000 | tf_op jit(solution)/shard_map/pack/pallas_call | solution.py:98
  50.1 8.8 %all-to-all-start = ((bf16[8,2,208,256]{3,2,1,0:T(8,128)(2,1)}), bf16[8,2,208,256]{3,2,1,0:T(8,128)(2,1)S(1)}, u32[]{:S(2)}, u32[]{:S(2)}) async-start(bf16[8,2,208,256]{3,2,1,0:T(8,128)(2,1)} %get-tuple-element.30), calls=%async_computation | async-start | bytes 3407872 | tf_op jit(solution)/shard_map/all_to_all | solution.py:453
  58.8 12.1 %collective-permute-done.5.refs_2_ = bf16[2,256,1024]{2,1,0:T(8,128)(2,1)} collective-permute-done((bf16[2,256,1024]{2,1,0:T(8,128)(2,1)}, bf16[2,256,1024]{2,1,0:T(8,128)(2,1)}, u32[]{:S(2)}, u32[]{:S(2)}) %collective-permute-start.5) | collective-permute-done | bytes 1048608 | tf_op jit(solution)/shard_map/ppermute | solution.py:358
  70.9 0.0 collective-permute-done.3.refs_0_
  70.9 0.0 collective-permute-done.4.refs_1_
  70.9 1.0 copy-done.4
  71.9 1.2 copy-done.1
  73.2 3.2 %select_select_fusion = (bf16[2,256,1024]{2,1,0:T(8,128)(2,1)}, bf16[2,256,1024]{2,1,0:T(8,128)(2,1)}) fusion(bf16[2,256,1024]{2,1,0:T(8,128)(2,1)} %get-tuple-element.33, bf16[2,256,1024]{2,1,0:T(8,128)(2,1)} %get-tuple-element.34, bf16[2,256,1024]{2,1,0:T(8,128)(2,1)S(1)} %copy-done.1, pred[]{:T(512)S(6)} %eq.61, pred[]{:T(512)S(6)} %eq.60, pred[]{:T(512)S(6)} %eq.59), kind=kLoop, calls=%fused_computation.3 | loop fusion | flops 1572864 | bytes 5242883 | tf_op jit(solution)/shard_map/jit(_where)/select_n | solution.py:371
  76.3 3.0 %collective-permute-start.7 = (bf16[2,256,1024]{2,1,0:T(8,128)(2,1)}, bf16[2,256,1024]{2,1,0:T(8,128)(2,1)}, u32[]{:S(2)}, u32[]{:S(2)}) collective-permute-start(bf16[2,256,1024]{2,1,0:T(8,128)(2,1)} %get-tuple-element.49.refs_8_), channel_id=1, source_target_pairs={{0,4},{4,0},{8,12},{12,8},{16,20},{20,16},{24,28},{28,24},{1,5},{5... | collective-permute-start | bytes 3145736 | tf_op jit(solution)/shard_map/ppermute | solution.py:358
  79.3 1.3 collective-permute-start.6
  80.6 9.8 %pack.3.refs_0_ = s16[8,2,96,16,128]{4,3,2,1,0:T(8,128)(2,1)} custom-call(s32[1536]{0:T(1024)} %get-tuple-element.44.source, f32[2,1024,1024]{2,1,0:T(8,128)} %x.9, s16[8,2,96,16,128]{4,3,2,1,0:T(8,128)(2,1)} %get-tuple-element.29.refs_0_), custom_call_target="tpu_custom_call", output_to_operand_aliasing={{}: (2, {})} | custom-call | flops 40000000000 | bytes 33000000 | tf_op jit(solution)/shard_map/pack/pallas_call | solution.py:98
  90.4 10.6 %all-to-all-done.refs_1_ = bf16[8,2,208,256]{3,2,1,0:T(8,128)(2,1)S(1)} async-done(((bf16[8,2,208,256]{3,2,1,0:T(8,128)(2,1)}), bf16[8,2,208,256]{3,2,1,0:T(8,128)(2,1)S(1)}, u32[]{:S(2)}, u32[]{:S(2)}) %all-to-all-start) | async-done | bytes 1703968 | tf_op jit(solution)/shard_map/all_to_all | solution.py:453
  101.0 1.2 copy-done.2
  102.2 0.9 slice_bitcast_fusion
  103.2 4.8 %all-to-all-start.1 = ((s16[8,2,96,16,128]{4,3,2,1,0:T(8,128)(2,1)}), s16[8,2,96,16,128]{4,3,2,1,0:T(8,128)(2,1)}, u32[]{:S(2)}, u32[]{:S(2)}) async-start(s16[8,2,96,16,128]{4,3,2,1,0:T(8,128)(2,1)} %get-tuple-element.32), calls=%async_computation.1 | async-start | bytes 12582912 | tf_op jit(solution)/shard_map/all_to_all | solution.py:462
  108.0 0.7 reshape.263.unit
  108.7 0.7 reshape.261.code
  109.4 0.2 fusion
  109.6 0.7 reshape.255.place
  110.3 6.1 %lower_unpack.1 = (bf16[2,1024,512]{2,1,0:T(8,128)(2,1)}, f32[2,1024,128]{2,1,0:T(8,128)}) custom-call(bf16[8,2,208,256]{3,2,1,0:T(8,128)(2,1)} %get-tuple-element.31.got, s32[2,1,1664]{2,1,0:T(1,128)} %reshape.255.place, f32[2,1,1664]{2,1,0:T(1,128)} %reshape.261.code, f32[2,1,1664]{2,1,0:T(1,128)} %reshape.263.unit), custom_call_target="tpu_custom_call" | custom-call | flops 20000000000 | bytes 16500000 | tf_op jit(solution)/shard_map/lower_unpack/pallas_call | solution.py:274
  116.5 0.0 collective-permute-done.7.refs_1_
  116.5 1.8 collective-permute-done.6.refs_0_
  118.3 1.0 copy-done.3
  119.3 1.5 collective-permute-start.8
  120.8 0.0 collective-permute-start.9
  120.8 41.4 %collective-permute-done.8.refs_1_ = bf16[2,1024,512]{2,1,0:T(8,128)(2,1)S(1)} collective-permute-done((bf16[2,1024,512]{2,1,0:T(8,128)(2,1)}, bf16[2,1024,512]{2,1,0:T(8,128)(2,1)S(1)}, u32[]{:S(2)}, u32[]{:S(2)}) %collective-permute-start.8) | collective-permute-done | bytes 2097184 | tf_op jit(solution)/shard_map/ppermute | solution.py:419
  162.2 0.0 collective-permute-start.10
  162.2 2.1 broadcast_select_fusion.refs_10_
  164.3 1.7 collective-permute-start.11
  166.0 0.6 stack.74.starts
  166.6 0.1 sub.35
  166.7 0.1 copy.81
  166.8 0.7 reshape.254.valid
  167.5 0.6 fusion.4.row_at
  168.1 52.1 %collective-permute-done.11.refs_11_ = bf16[2,256,1024]{2,1,0:T(8,128)(2,1)} collective-permute-done((bf16[2,256,1024]{2,1,0:T(8,128)(2,1)S(1)}, bf16[2,256,1024]{2,1,0:T(8,128)(2,1)}, u32[]{:S(2)}, u32[]{:S(2)}) %collective-permute-start.11) | collective-permute-done | bytes 1048608 | tf_op jit(solution)/shard_map/ppermute | solution.py:358
  220.2 18.3 %product.1.before = f32[1024,1024]{1,0:T(8,128)} custom-call(s32[12]{0:T(128)} %stack.74.starts, f32[1024,1024]{1,0:T(8,128)} %front.1, bf16[2,1024,512]{2,1,0:T(8,128)(2,1)} %get-tuple-element.37.refs_0_, bf16[2,1024,512]{2,1,0:T(8,128)(2,1)} %copy-done.9, bf16[2,1024,512]{2,1,0:T(8,128)(2,1)} %collective-permute-done.9.refs_2_, ...), custom_call_target="tpu_custom_call" | custom-call | flops 60000002048 | bytes 49500000 | tf_op jit(solution)/shard_map/product/pallas_call | solution.py:321
  238.5 5.0 %all-to-all-done.1.got = s16[8,2,96,16,128]{4,3,2,1,0:T(8,128)(2,1)} async-done(((s16[8,2,96,16,128]{4,3,2,1,0:T(8,128)(2,1)}), s16[8,2,96,16,128]{4,3,2,1,0:T(8,128)(2,1)}, u32[]{:S(2)}, u32[]{:S(2)}) %all-to-all-start.1) | async-done | bytes 6291488 | tf_op jit(solution)/shard_map/all_to_all | solution.py:462
  243.5 10.5 %unpack.1 = f32[1024,1024]{1,0:T(8,128)} custom-call(s32[3072]{0:T(1024)} %fusion.4.row_at, s32[16]{0:T(128)} %reshape.254.valid, s16[8,2,96,16,128]{4,3,2,1,0:T(8,128)(2,1)} %all-to-all-done.1.got, f32[1024,1024]{1,0:T(8,128)} %product.1.before, f32[2,1024,128]{2,1,0:T(8,128)} %get-tuple-element.42.unit), custom_call_target="tpu_custom_call" | custom-call | flops 44000002048 | bytes 36300000 | tf_op jit(solution)/shard_map/unpack/pallas_call | solution.py:171
  (52 shorter events, 0.4 us)
Async XLA Ops:
  0.0 30.1 %collective-permute-start.1 = (bf16[2,256,1024]{2,1,0:T(8,128)(2,1)}, bf16[2,256,1024]{2,1,0:T(8,128)(2,1)S(1)}, u32[]{:S(2)}, u32[]{:S(2)}) collective-permute-start(bf16[2,256,1024]{2,1,0:T(8,128)(2,1)} %refs_4_.1), channel_id=1, source_target_pairs={{8,0},{12,4},{16,8},{20,12},{24,16},{28,20},{9,1},{13,5},{17,9},{2... | collective-permute-start | bytes 3145736 | tf_op jit(solution)/shard_map/ppermute | solution.py:358
  1.3 28.8 %collective-permute-start = (bf16[2,256,1024]{2,1,0:T(8,128)(2,1)}, bf16[2,256,1024]{2,1,0:T(8,128)(2,1)S(1)}, u32[]{:S(2)}, u32[]{:S(2)}) collective-permute-start(bf16[2,256,1024]{2,1,0:T(8,128)(2,1)} %refs_4_.1), channel_id=1, source_target_pairs={{0,8},{4,12},{8,16},{12,20},{16,24},{20,28},{1,9},{5,13},{9,17},{1... | collective-permute-start | bytes 3145736 | tf_op jit(solution)/shard_map/ppermute | solution.py:358
  6.9 24.9 %collective-permute-start.2 = (bf16[2,256,1024]{2,1,0:T(8,128)(2,1)}, bf16[2,256,1024]{2,1,0:T(8,128)(2,1)S(1)}, u32[]{:S(2)}, u32[]{:S(2)}) collective-permute-start(bf16[2,256,1024]{2,1,0:T(8,128)(2,1)} %refs_4_.1), channel_id=1, source_target_pairs={{0,4},{4,0},{8,12},{12,8},{16,20},{20,16},{24,28},{28,24},{1,5},{5... | collective-permute-start | bytes 3145736 | tf_op jit(solution)/shard_map/ppermute | solution.py:358
  10.6 4.1 %copy-start.8 = (s32[2,1024]{1,0:T(2,128)S(1)}, s32[2,1024]{1,0:T(2,128)}, u32[]{:S(2)}) copy-start(s32[2,1024]{1,0:T(2,128)} %param.10) | copy-start | bytes 24580
  30.1 1.7 copy-start
  30.1 1.7 copy-start.5
  31.8 1.0 copy-start.7
  34.2 36.7 %collective-permute-start.3 = (bf16[2,256,1024]{2,1,0:T(8,128)(2,1)}, bf16[2,256,1024]{2,1,0:T(8,128)(2,1)S(1)}, u32[]{:S(2)}, u32[]{:S(2)}) collective-permute-start(bf16[2,256,1024]{2,1,0:T(8,128)(2,1)} %get-tuple-element.25), channel_id=1, source_target_pairs={{8,16},{12,20},{16,24},{20,28},{9,17},{13,21},{17,25},{21,29},{10,... | collective-permute-start | bytes 3145736 | tf_op jit(solution)/shard_map/ppermute | solution.py:358
  35.0 35.9 %collective-permute-start.4 = (bf16[2,256,1024]{2,1,0:T(8,128)(2,1)}, bf16[2,256,1024]{2,1,0:T(8,128)(2,1)}, u32[]{:S(2)}, u32[]{:S(2)}) collective-permute-start(bf16[2,256,1024]{2,1,0:T(8,128)(2,1)} %get-tuple-element.26), channel_id=1, source_target_pairs={{8,0},{12,4},{16,8},{20,12},{9,1},{13,5},{17,9},{21,13},{10,2},{14... | collective-permute-start | bytes 3145736 | tf_op jit(solution)/shard_map/ppermute | solution.py:358
  38.6 32.3 %collective-permute-start.5 = (bf16[2,256,1024]{2,1,0:T(8,128)(2,1)}, bf16[2,256,1024]{2,1,0:T(8,128)(2,1)}, u32[]{:S(2)}, u32[]{:S(2)}) collective-permute-start(bf16[2,256,1024]{2,1,0:T(8,128)(2,1)} %broadcast_select_fusion.2.refs_6_), channel_id=1, source_target_pairs={{0,4},{4,0},{8,12},{12,8},{16,20},{20,16},{24,28},{28,24},{1,5},{5... | collective-permute-start | bytes 3145736 | tf_op jit(solution)/shard_map/ppermute | solution.py:358
  50.1 50.9 %all-to-all-start = ((bf16[8,2,208,256]{3,2,1,0:T(8,128)(2,1)}), bf16[8,2,208,256]{3,2,1,0:T(8,128)(2,1)S(1)}, u32[]{:S(2)}, u32[]{:S(2)}) async-start(bf16[8,2,208,256]{3,2,1,0:T(8,128)(2,1)} %get-tuple-element.30), calls=%async_computation | async-start | bytes 3407872 | tf_op jit(solution)/shard_map/all_to_all | solution.py:453
  70.9 1.0 copy-start.4
  71.9 1.2 copy-start.1
  76.3 40.1 %collective-permute-start.7 = (bf16[2,256,1024]{2,1,0:T(8,128)(2,1)}, bf16[2,256,1024]{2,1,0:T(8,128)(2,1)}, u32[]{:S(2)}, u32[]{:S(2)}) collective-permute-start(bf16[2,256,1024]{2,1,0:T(8,128)(2,1)} %get-tuple-element.49.refs_8_), channel_id=1, source_target_pairs={{0,4},{4,0},{8,12},{12,8},{16,20},{20,16},{24,28},{28,24},{1,5},{5... | collective-permute-start | bytes 3145736 | tf_op jit(solution)/shard_map/ppermute | solution.py:358
  79.3 39.0 %collective-permute-start.6 = (bf16[2,256,1024]{2,1,0:T(8,128)(2,1)}, bf16[2,256,1024]{2,1,0:T(8,128)(2,1)S(1)}, u32[]{:S(2)}, u32[]{:S(2)}) collective-permute-start(bf16[2,256,1024]{2,1,0:T(8,128)(2,1)} %get-tuple-element.50), channel_id=1, source_target_pairs={{8,0},{12,4},{16,24},{20,28},{9,1},{13,5},{17,25},{21,29},{10,2},{... | collective-permute-start | bytes 3145736 | tf_op jit(solution)/shard_map/ppermute | solution.py:358
  101.0 1.2 copy-start.2
  103.2 140.3 %all-to-all-start.1 = ((s16[8,2,96,16,128]{4,3,2,1,0:T(8,128)(2,1)}), s16[8,2,96,16,128]{4,3,2,1,0:T(8,128)(2,1)}, u32[]{:S(2)}, u32[]{:S(2)}) async-start(s16[8,2,96,16,128]{4,3,2,1,0:T(8,128)(2,1)} %get-tuple-element.32), calls=%async_computation.1 | async-start | bytes 12582912 | tf_op jit(solution)/shard_map/all_to_all | solution.py:462
  118.3 1.0 copy-start.3
  119.3 42.9 %collective-permute-start.8 = (bf16[2,1024,512]{2,1,0:T(8,128)(2,1)}, bf16[2,1024,512]{2,1,0:T(8,128)(2,1)S(1)}, u32[]{:S(2)}, u32[]{:S(2)}) collective-permute-start(bf16[2,1024,512]{2,1,0:T(8,128)(2,1)} %get-tuple-element.37.refs_0_), channel_id=1, source_target_pairs={{0,2},{1,3},{2,0},{3,1},{4,6},{5,7},{6,4},{7,5},{8,10},{9,11},{10,... | collective-permute-start | bytes 6291464 | tf_op jit(solution)/shard_map/ppermute | solution.py:419
  120.8 99.3 %collective-permute-start.9 = (bf16[2,1024,512]{2,1,0:T(8,128)(2,1)}, bf16[2,1024,512]{2,1,0:T(8,128)(2,1)}, u32[]{:S(2)}, u32[]{:S(2)}) collective-permute-start(bf16[2,1024,512]{2,1,0:T(8,128)(2,1)} %get-tuple-element.37.refs_0_), channel_id=1, source_target_pairs={{0,1},{1,0},{2,3},{3,2},{4,5},{5,4},{6,7},{7,6},{8,9},{9,8},{10,11... | collective-permute-start | bytes 6291464 | tf_op jit(solution)/shard_map/ppermute | solution.py:419
  162.2 58.0 %copy-start.9 = (bf16[2,1024,512]{2,1,0:T(8,128)(2,1)}, bf16[2,1024,512]{2,1,0:T(8,128)(2,1)S(1)}, u32[]{:S(2)}) copy-start(bf16[2,1024,512]{2,1,0:T(8,128)(2,1)S(1)} %collective-permute-done.8.refs_1_) | copy-start | bytes 6291460
  162.2 58.0 %collective-permute-start.10 = (bf16[2,1024,512]{2,1,0:T(8,128)(2,1)S(1)}, bf16[2,1024,512]{2,1,0:T(8,128)(2,1)}, u32[]{:S(2)}, u32[]{:S(2)}) collective-permute-start(bf16[2,1024,512]{2,1,0:T(8,128)(2,1)S(1)} %collective-permute-done.8.refs_1_), channel_id=1, source_target_pairs={{0,1},{1,0},{2,3},{3,2},{4,5},{5,4},{6,7},{7,6},{8,9},{9,8},{10,11... | collective-permute-start | bytes 6291464 | tf_op jit(solution)/shard_map/ppermute | solution.py:419
  164.3 55.9 %copy-start.6 = (bf16[2,256,1024]{2,1,0:T(8,128)(2,1)}, bf16[2,256,1024]{2,1,0:T(8,128)(2,1)S(1)}, u32[]{:S(2)}) copy-start(bf16[2,256,1024]{2,1,0:T(8,128)(2,1)S(1)} %broadcast_select_fusion.refs_10_) | copy-start | bytes 3145732
  164.3 55.9 %collective-permute-start.11 = (bf16[2,256,1024]{2,1,0:T(8,128)(2,1)S(1)}, bf16[2,256,1024]{2,1,0:T(8,128)(2,1)}, u32[]{:S(2)}, u32[]{:S(2)}) collective-permute-start(bf16[2,256,1024]{2,1,0:T(8,128)(2,1)S(1)} %broadcast_select_fusion.refs_10_), channel_id=1, source_target_pairs={{0,4},{4,0},{8,12},{12,8},{16,20},{20,16},{24,28},{28,24},{1,5},{5... | collective-permute-start | bytes 3145736 | tf_op jit(solution)/shard_map/ppermute | solution.py:358

commit v6 on v5

--- a/solution.py
+++ b/solution.py
@@ -51,7 +51,7 @@
 
 
 def pack_kernel(groups, steps, source, x, *refs):
-    out, held = refs[-2:]
+    out, held, scale = refs[-3:]
     i = pl.program_id(0)
     rows = x.shape[1]
     targets, _, tiles = out.shape[:3]
@@ -59,15 +59,16 @@
 
     @pl.when(i < steps)
     def _():
+        unit = row_unit(x[0]).astype(jnp.float32)
+        scale[...] = jnp.broadcast_to(jnp.where(unit > 0.0, 1.0 / unit, 0.0), scale.shape)
+
         def body(g, carry):
             at = pl.multiple_of(g * 8, 8)
-            v = x[0, pl.ds(at, 8), :]
-            unit = row_unit(v).astype(jnp.float32)
-            inverse = jnp.where(unit > 0.0, 1.0 / unit, 0.0)
-            q = jnp.floor(v * inverse + 0.5).astype(jnp.int32)
+            inverse = scale[pl.ds(at, 8), :]
             base = (i * rows + at) * groups
             for j in range(groups):
-                held[pl.ds(base + j, 8, stride=groups), :] = q[:, j * LANES : (j + 1) * LANES]
+                v = x[0, pl.ds(at, 8), j * LANES : (j + 1) * LANES]
+                held[pl.ds(base + j, 8, stride=groups), :] = jnp.floor(v * inverse + 0.5).astype(jnp.int32)
             return carry
 
         lax.fori_loop(0, rows // 8, body, 0, unroll=4)
@@ -107,7 +108,10 @@
                 (count // out_steps, 1, tiles, 16, LANES),
                 lambda i, s: (jnp.maximum(i - steps, 0), child, 0, 0, 0),
             ),
-            scratch_shapes=[pltpu.VMEM((rows * groups, LANES), jnp.int32)],
+            scratch_shapes=[
+                pltpu.VMEM((rows * groups, LANES), jnp.int32),
+                pltpu.VMEM((rows // steps, LANES), jnp.float32),
+            ],
         ),
         input_output_aliases={} if into is None else {2: 0},
         compiler_params=pltpu.CompilerParams(vmem_limit_bytes=VMEM_LIMIT),
@@ -162,7 +166,7 @@
     rows, width = before.shape
     count, children, tiles = got.shape[:3]
     groups = width // LANES
-    steps, out_steps = count // 2, 2
+    steps, out_steps = count // 4, 2
 
     def block(i, *_):
         return jnp.maximum(i - steps, 0), 0
@@ -401,6 +405,12 @@
         self.held.append([block] + self.exchange(block, range(self.outer)))
         return rest[len(mine) :]
 
+    def finish_along_x(self, arrays):
+        mine = self.held[-1][1:]
+        rest = gate([*mine, *arrays])
+        self.held[-1][1:] = rest[: len(mine)]
+        return rest[len(mine) :]
+
     def blocks(self):
         found = []
         for k in range(self.outer):
@@ -458,7 +468,6 @@
     relay.step()
     for child in range(1, children):
         sent = pack(schur, child, source[child], count, sent)
-    sent, got_lower = gate([sent, got_lower])
     got = lax.all_to_all(sent, "row", split_axis=0, concat_axis=0, tiled=True)
 
     notes = got_lower[:, :, cap : cap + NOTES, :cap].transpose(2, 1, 0, 3)
@@ -475,8 +484,10 @@
 
     full, units = relay.finish([full, units])
     column = lax.axis_index("col")
-    bit = lax.axis_size("col")
-    lows = [(0, full)]
+    bit = lax.axis_size("col") // 2
+    lows = exchange_columns([(0, full)], bit)
+    others = relay.finish_along_x([low for _, low in lows])
+    lows = [(far, low) for (far, _), low in zip(lows, others)]
     while bit > 1:
         bit //= 2
         lows = exchange_columns(lows, bit)

time: 255 us -> 252 us (0.988)
  Pallas kernels: 63.7 us -> 59 us
    ppermute x3, waiting for transfers between devices: 41.4 us -> 5.01 us  [exchange_columns(): lax.ppermute(x, 'col', pairs)]
    all_to_all x1, waiting for transfers between devices: 4.99 us -> 33.4 us  [shards(): got = lax.all_to_all(sent, 'row', split_axis=0, concat_axis=0, tiled=True)]
    ppermute x9, waiting for transfers between devices: 67.8 us -> 75.4 us  [send(): lax.ppermute(x, 'row', [(z * n + i, to * n + (i + turn) % n) for z, to in...]
    pallas_call x2, Pallas kernels: 19.6 us -> 15.4 us  [pack(): pl.pallas_call(functools.partial(pack_kernel, groups, steps), out_shape=j...]
    unnamed x22 -> x30, local copies, waits for them, and re-layouts: 5.49 us -> 7.47 us
  transfers between devices with their start and end apart: 14 -> 14, of which waited for: 7 -> 9; matrix products, arithmetic and copies ran while one was open for 10% -> 9% of each run, Pallas kernels for 21% -> 19%
where the time goes in v6:
time: 252 us; the launch traced here: 251 us
  waiting for transfers between devices  126 us (50%)
  Pallas kernels  59 us (23%)
  starting transfers between devices  33.1 us (13%)
  local copies, waits for them, and re-layouts  17.5 us (7%)
  other arithmetic  15.1 us (6%)
    ppermute x9, waiting for transfers between devices, send(): lax.ppermute(x, 'row', [(z * n + i, to * n + (i + turn) % n) for z, to in...  75.4 us
    all_to_all x1, waiting for transfers between devices, shards(): got = lax.all_to_all(sent, 'row', split_axis=0, concat_axis=0, tiled=True)  33.4 us
    ppermute x9, starting transfers between devices, send(): lax.ppermute(x, 'row', [(z * n + i, to * n + (i + turn) % n) for z, to in...  18.5 us
    pallas_call x1, Pallas kernels, product(): pl.pallas_call(functools.partial(product_kernel, children, steps, len(low...  18.3 us
    pallas_call x2, Pallas kernels, pack(): pl.pallas_call(functools.partial(pack_kernel, groups, steps), out_shape=j...  15.4 us
    all_to_all x1, waiting for transfers between devices, shards(): lax.all_to_all(sent_lower, 'row', split_axis=0, concat_axis=0, tiled=True)  12.7 us
    pallas_call x1, Pallas kernels, unpack(): pl.pallas_call(functools.partial(unpack_kernel, groups, steps), out_shape...  10 us
    pallas_call x1, Pallas kernels, lower_pack(): pl.pallas_call(lower_pack_kernel, out_shape=jax.ShapeDtypeStruct((count,...  9.13 us
  transfers between devices with their start and end apart: 14, of which 9 were waited for; matrix products, arithmetic and copies ran while one was open for 9% of the time, Pallas kernels for 19%

profile of v6, /device:TPU:0, one launch (start us, length us, event | category | flops | bytes accessed | tf_op | source)
XLA Modules:
  0.0 251.4 jit_solution(5850131070258693639)
XLA Ops:
  0.0 1.3 collective-permute-start.1
  1.3 5.6 %collective-permute-start = (bf16[2,256,1024]{2,1,0:T(8,128)(2,1)}, bf16[2,256,1024]{2,1,0:T(8,128)(2,1)S(1)}, u32[]{:S(2)}, u32[]{:S(2)}) collective-permute-start(bf16[2,256,1024]{2,1,0:T(8,128)(2,1)} %refs_4_.1), channel_id=1, source_target_pairs={{0,8},{4,12},{8,16},{12,20},{16,24},{20,28},{1,9},{5,13},{9,17},{1... | collective-permute-start | bytes 3145736 | tf_op jit(solution)/shard_map/ppermute | solution.py:362
  6.9 2.0 collective-permute-start.2
  9.0 0.7 slice.44
  9.7 0.1 copy.75
  9.8 0.1 multiply_reduce_fusion
  9.9 0.1 broadcast_in_dim.38
  10.0 0.6 reshape_squeeze.3.picks
  10.6 4.1 %abs_reduce_fusion = f32[2,1024]{1,0:T(2,128)S(1)} fusion(f32[2,1024,1024]{2,1,0:T(8,128)} %x.9), kind=kLoop, calls=%fused_computation | loop fusion | flops 4192256 | bytes 8396800 | tf_op jit(solution)/shard_map/reduce_max | solution.py:49
  14.7 0.1 fusion.16
  14.8 0.7 iota_compare_fusion
  15.5 1.9 convert_reduce_fusion
  17.4 0.6 reshape.252.slot
  18.1 1.3 stack.61.digits
  19.4 9.1 %lower_pack.1.refs_3_ = bf16[8,2,208,256]{3,2,1,0:T(8,128)(2,1)} custom-call(s32[32]{0:T(128)} %reshape_squeeze.3.picks, bf16[2,1024,512]{2,1,0:T(8,128)(2,1)} %low.1, s32[2,1,1024]{2,1,0:T(1,128)} %reshape.252.slot, bf16[2,16,1024]{2,1,0:T(8,128)(2,1)} %stack.61.digits), custom_call_target="tpu_custom_call" | custom-call | flops 28000000000 | bytes 23100000 | tf_op jit(solution)/shard_map/lower_pack/pallas_call | solution.py:225
  28.5 0.9 slice_convert_fusion.2
  29.4 0.7 reshape.253.refs_4_
  30.1 1.7 collective-permute-done.2.refs_2_
  31.8 1.0 copy-done.11
  32.8 1.4 slice_reduce_fusion
  34.2 0.7 collective-permute-start.3
  35.0 1.3 collective-permute-start.4
  36.3 2.3 broadcast_select_fusion.2.refs_6_
  38.6 1.6 collective-permute-start.5
  40.2 7.7 %pack.2.refs_1_ = s16[8,2,96,16,128]{4,3,2,1,0:T(8,128)(2,1)} custom-call(s32[1536]{0:T(1024)} %get-tuple-element.46.source, f32[2,1024,1024]{2,1,0:T(8,128)} %x.9), custom_call_target="tpu_custom_call" | custom-call | flops 40000000000 | bytes 33000000 | tf_op jit(solution)/shard_map/pack/pallas_call | solution.py:99
  47.9 7.8 %all-to-all-start = ((bf16[8,2,208,256]{3,2,1,0:T(8,128)(2,1)}), bf16[8,2,208,256]{3,2,1,0:T(8,128)(2,1)}, u32[]{:S(2)}, u32[]{:S(2)}) async-start(bf16[8,2,208,256]{3,2,1,0:T(8,128)(2,1)} %get-tuple-element.27), calls=%async_computation | async-start | bytes 3407872 | tf_op jit(solution)/shard_map/all_to_all | solution.py:463
  55.7 15.1 %collective-permute-done.5.refs_2_ = bf16[2,256,1024]{2,1,0:T(8,128)(2,1)S(1)} collective-permute-done((bf16[2,256,1024]{2,1,0:T(8,128)(2,1)}, bf16[2,256,1024]{2,1,0:T(8,128)(2,1)S(1)}, u32[]{:S(2)}, u32[]{:S(2)}) %collective-permute-start.5) | collective-permute-done | bytes 1048608 | tf_op jit(solution)/shard_map/ppermute | solution.py:362
  70.8 0.0 collective-permute-done.3.refs_0_
  70.8 1.7 collective-permute-done.4.refs_1_
  72.6 1.0 copy-done.4
  73.6 1.2 copy-done.1
  74.8 2.8 %select_select_fusion = (bf16[2,256,1024]{2,1,0:T(8,128)(2,1)}, bf16[2,256,1024]{2,1,0:T(8,128)(2,1)S(1)}) fusion(bf16[2,256,1024]{2,1,0:T(8,128)(2,1)} %get-tuple-element.32, bf16[2,256,1024]{2,1,0:T(8,128)(2,1)} %get-tuple-element.33, bf16[2,256,1024]{2,1,0:T(8,128)(2,1)S(1)} %copy-done.1, pred[]{:T(512)S(6)} %eq.61, pred[]{:T(512)S(6)} %eq.60, pred[]{:T(512)S(6)} %eq.59), kind=kLoop, calls=%fused_computation.3 | loop fusion | flops 1572864 | bytes 5242883 | tf_op jit(solution)/shard_map/jit(_where)/select_n | solution.py:375
  77.6 1.8 collective-permute-start.7
  79.4 1.3 collective-permute-start.6
  80.7 7.7 %pack.3 = s16[8,2,96,16,128]{4,3,2,1,0:T(8,128)(2,1)} custom-call(s32[1536]{0:T(1024)} %get-tuple-element.45.source, f32[2,1024,1024]{2,1,0:T(8,128)} %x.9, s16[8,2,96,16,128]{4,3,2,1,0:T(8,128)(2,1)} %get-tuple-element.31.refs_0_), custom_call_target="tpu_custom_call", output_to_operand_aliasing={{}: (2, {})} | custom-call | flops 40000000000 | bytes 33000000 | tf_op jit(solution)/shard_map/pack/pallas_call | solution.py:99
  88.4 12.7 %all-to-all-done.got = bf16[8,2,208,256]{3,2,1,0:T(8,128)(2,1)} async-done(((bf16[8,2,208,256]{3,2,1,0:T(8,128)(2,1)}), bf16[8,2,208,256]{3,2,1,0:T(8,128)(2,1)}, u32[]{:S(2)}, u32[]{:S(2)}) %all-to-all-start) | async-done | bytes 1703968 | tf_op jit(solution)/shard_map/all_to_all | solution.py:463
  101.1 4.7 %all-to-all-start.1 = ((s16[8,2,96,16,128]{4,3,2,1,0:T(8,128)(2,1)}), s16[8,2,96,16,128]{4,3,2,1,0:T(8,128)(2,1)}, u32[]{:S(2)}, u32[]{:S(2)}) async-start(s16[8,2,96,16,128]{4,3,2,1,0:T(8,128)(2,1)} %pack.3), calls=%async_computation.1 | async-start | bytes 12582912 | tf_op jit(solution)/shard_map/all_to_all | solution.py:471
  105.8 0.9 slice_bitcast_fusion
  106.9 0.7 reshape.263.unit
  107.6 0.7 reshape.261.code
  108.3 0.2 fusion
  108.5 0.7 reshape.255.place
  109.2 6.1 %lower_unpack.1 = (bf16[2,1024,512]{2,1,0:T(8,128)(2,1)}, f32[2,1024,128]{2,1,0:T(8,128)}) custom-call(bf16[8,2,208,256]{3,2,1,0:T(8,128)(2,1)} %all-to-all-done.got, s32[2,1,1664]{2,1,0:T(1,128)} %reshape.255.place, f32[2,1,1664]{2,1,0:T(1,128)} %reshape.261.code, f32[2,1,1664]{2,1,0:T(1,128)} %reshape.263.unit), custom_call_target="tpu_custom_call" | custom-call | flops 20000000000 | bytes 16500000 | tf_op jit(solution)/shard_map/lower_unpack/pallas_call | solution.py:278
  115.4 0.0 collective-permute-done.7.refs_1_
  115.4 5.3 %collective-permute-done.6.refs_0_ = bf16[2,256,1024]{2,1,0:T(8,128)(2,1)S(1)} collective-permute-done((bf16[2,256,1024]{2,1,0:T(8,128)(2,1)S(1)}, bf16[2,256,1024]{2,1,0:T(8,128)(2,1)S(1)}, u32[]{:S(2)}, u32[]{:S(2)}) %collective-permute-start.6) | collective-permute-done | bytes 1048608 | tf_op jit(solution)/shard_map/ppermute | solution.py:362
  120.7 1.1 copy-done.2
  121.8 1.5 collective-permute-start.9
  123.3 1.3 broadcast_select_fusion.1.refs_10_
  124.6 2.9 %collective-permute-start.8 = (bf16[2,256,1024]{2,1,0:T(8,128)(2,1)S(1)}, bf16[2,256,1024]{2,1,0:T(8,128)(2,1)S(1)}, u32[]{:S(2)}, u32[]{:S(2)}) collective-permute-start(bf16[2,256,1024]{2,1,0:T(8,128)(2,1)S(1)} %broadcast_select_fusion.1.refs_10_), channel_id=1, source_target_pairs={{0,4},{4,0},{8,12},{12,8},{16,20},{20,16},{24,28},{28,24},{1,5},{5... | collective-permute-start | bytes 3145736 | tf_op jit(solution)/shard_map/ppermute | solution.py:362
  127.5 51.6 %collective-permute-done.8.refs_0_ = bf16[2,256,1024]{2,1,0:T(8,128)(2,1)S(1)} collective-permute-done((bf16[2,256,1024]{2,1,0:T(8,128)(2,1)S(1)}, bf16[2,256,1024]{2,1,0:T(8,128)(2,1)S(1)}, u32[]{:S(2)}, u32[]{:S(2)}) %collective-permute-start.8) | collective-permute-done | bytes 1048608 | tf_op jit(solution)/shard_map/ppermute | solution.py:362
  179.1 1.0 copy-done.9
  180.1 1.3 copy-done.6
  181.4 0.5 collective-permute-start.11
  181.9 0.6 stack.74.starts
  182.5 0.1 sub.34
  182.6 0.1 copy.82
  182.7 0.6 reshape.254.valid
  183.3 0.6 fusion.4.row_at
  183.9 4.5 %collective-permute-done.10.refs_2_ = bf16[2,1024,512]{2,1,0:T(8,128)(2,1)S(1)} collective-permute-done((bf16[2,1024,512]{2,1,0:T(8,128)(2,1)}, bf16[2,1024,512]{2,1,0:T(8,128)(2,1)S(1)}, u32[]{:S(2)}, u32[]{:S(2)}) %collective-permute-start.10) | collective-permute-done | bytes 2097184 | tf_op jit(solution)/shard_map/ppermute | solution.py:429
  188.4 0.5 collective-permute-done.11.refs_3_
  188.9 0.8 copy-done.13
  189.7 18.3 %product.1.before = f32[1024,1024]{1,0:T(8,128)} custom-call(s32[12]{0:T(128)} %stack.74.starts, f32[1024,1024]{1,0:T(8,128)} %front.1, bf16[2,1024,512]{2,1,0:T(8,128)(2,1)} %get-tuple-element.38.refs_0_, bf16[2,1024,512]{2,1,0:T(8,128)(2,1)} %get-tuple-element.39.refs_1_, bf16[2,1024,512]{2,1,0:T(8,128)(2,1)} %copy-done.13, ...), custom_call_target="tpu_custom_call" | custom-call | flops 60000002048 | bytes 49500000 | tf_op jit(solution)/shard_map/product/pallas_call | solution.py:325
  208.0 33.4 %all-to-all-done.1.got = s16[8,2,96,16,128]{4,3,2,1,0:T(8,128)(2,1)} async-done(((s16[8,2,96,16,128]{4,3,2,1,0:T(8,128)(2,1)}), s16[8,2,96,16,128]{4,3,2,1,0:T(8,128)(2,1)}, u32[]{:S(2)}, u32[]{:S(2)}) %all-to-all-start.1) | async-done | bytes 6291488 | tf_op jit(solution)/shard_map/all_to_all | solution.py:471
  241.4 10.0 %unpack.1 = f32[1024,1024]{1,0:T(8,128)} custom-call(s32[3072]{0:T(1024)} %fusion.4.row_at, s32[16]{0:T(128)} %reshape.254.valid, s16[8,2,96,16,128]{4,3,2,1,0:T(8,128)(2,1)} %all-to-all-done.1.got, f32[1024,1024]{1,0:T(8,128)} %product.1.before, f32[2,1024,128]{2,1,0:T(8,128)} %get-tuple-element.44.unit), custom_call_target="tpu_custom_call" | custom-call | flops 44000002048 | bytes 36300000 | tf_op jit(solution)/shard_map/unpack/pallas_call | solution.py:175
  (60 shorter events, 0.4 us)
Async XLA Ops:
  0.0 30.1 %collective-permute-start.1 = (bf16[2,256,1024]{2,1,0:T(8,128)(2,1)}, bf16[2,256,1024]{2,1,0:T(8,128)(2,1)S(1)}, u32[]{:S(2)}, u32[]{:S(2)}) collective-permute-start(bf16[2,256,1024]{2,1,0:T(8,128)(2,1)} %refs_4_.1), channel_id=1, source_target_pairs={{8,0},{12,4},{16,8},{20,12},{24,16},{28,20},{9,1},{13,5},{17,9},{2... | collective-permute-start | bytes 3145736 | tf_op jit(solution)/shard_map/ppermute | solution.py:362
  1.3 28.8 %collective-permute-start = (bf16[2,256,1024]{2,1,0:T(8,128)(2,1)}, bf16[2,256,1024]{2,1,0:T(8,128)(2,1)S(1)}, u32[]{:S(2)}, u32[]{:S(2)}) collective-permute-start(bf16[2,256,1024]{2,1,0:T(8,128)(2,1)} %refs_4_.1), channel_id=1, source_target_pairs={{0,8},{4,12},{8,16},{12,20},{16,24},{20,28},{1,9},{5,13},{9,17},{1... | collective-permute-start | bytes 3145736 | tf_op jit(solution)/shard_map/ppermute | solution.py:362
  6.9 24.9 %collective-permute-start.2 = (bf16[2,256,1024]{2,1,0:T(8,128)(2,1)}, bf16[2,256,1024]{2,1,0:T(8,128)(2,1)S(1)}, u32[]{:S(2)}, u32[]{:S(2)}) collective-permute-start(bf16[2,256,1024]{2,1,0:T(8,128)(2,1)} %refs_4_.1), channel_id=1, source_target_pairs={{0,4},{4,0},{8,12},{12,8},{16,20},{20,16},{24,28},{28,24},{1,5},{5... | collective-permute-start | bytes 3145736 | tf_op jit(solution)/shard_map/ppermute | solution.py:362
  10.6 4.1 %copy-start.12 = (s32[2,1024]{1,0:T(2,128)S(1)}, s32[2,1024]{1,0:T(2,128)}, u32[]{:S(2)}) copy-start(s32[2,1024]{1,0:T(2,128)} %param.10) | copy-start | bytes 24580
  30.1 1.7 copy-start
  30.1 1.7 copy-start.5
  31.8 1.0 copy-start.11
  34.2 36.6 %collective-permute-start.3 = (bf16[2,256,1024]{2,1,0:T(8,128)(2,1)}, bf16[2,256,1024]{2,1,0:T(8,128)(2,1)S(1)}, u32[]{:S(2)}, u32[]{:S(2)}) collective-permute-start(bf16[2,256,1024]{2,1,0:T(8,128)(2,1)} %get-tuple-element.28), channel_id=1, source_target_pairs={{8,16},{12,20},{16,24},{20,28},{9,17},{13,21},{17,25},{21,29},{10,... | collective-permute-start | bytes 3145736 | tf_op jit(solution)/shard_map/ppermute | solution.py:362
  35.0 37.6 %collective-permute-start.4 = (bf16[2,256,1024]{2,1,0:T(8,128)(2,1)}, bf16[2,256,1024]{2,1,0:T(8,128)(2,1)S(1)}, u32[]{:S(2)}, u32[]{:S(2)}) collective-permute-start(bf16[2,256,1024]{2,1,0:T(8,128)(2,1)} %get-tuple-element.29), channel_id=1, source_target_pairs={{8,0},{12,4},{16,8},{20,12},{9,1},{13,5},{17,9},{21,13},{10,2},{14... | collective-permute-start | bytes 3145736 | tf_op jit(solution)/shard_map/ppermute | solution.py:362
  38.6 32.3 %collective-permute-start.5 = (bf16[2,256,1024]{2,1,0:T(8,128)(2,1)}, bf16[2,256,1024]{2,1,0:T(8,128)(2,1)S(1)}, u32[]{:S(2)}, u32[]{:S(2)}) collective-permute-start(bf16[2,256,1024]{2,1,0:T(8,128)(2,1)} %broadcast_select_fusion.2.refs_6_), channel_id=1, source_target_pairs={{0,4},{4,0},{8,12},{12,8},{16,20},{20,16},{24,28},{28,24},{1,5},{5... | collective-permute-start | bytes 3145736 | tf_op jit(solution)/shard_map/ppermute | solution.py:362
  47.9 53.2 %all-to-all-start = ((bf16[8,2,208,256]{3,2,1,0:T(8,128)(2,1)}), bf16[8,2,208,256]{3,2,1,0:T(8,128)(2,1)}, u32[]{:S(2)}, u32[]{:S(2)}) async-start(bf16[8,2,208,256]{3,2,1,0:T(8,128)(2,1)} %get-tuple-element.27), calls=%async_computation | async-start | bytes 3407872 | tf_op jit(solution)/shard_map/all_to_all | solution.py:463
  70.8 1.7 copy-start.8
  70.8 1.7 copy-start.3
  72.6 1.0 copy-start.4
  73.6 1.2 copy-start.1
  77.6 37.8 %collective-permute-start.7 = (bf16[2,256,1024]{2,1,0:T(8,128)(2,1)}, bf16[2,256,1024]{2,1,0:T(8,128)(2,1)S(1)}, u32[]{:S(2)}, u32[]{:S(2)}) collective-permute-start(bf16[2,256,1024]{2,1,0:T(8,128)(2,1)} %get-tuple-element.51.refs_8_), channel_id=1, source_target_pairs={{0,4},{4,0},{8,12},{12,8},{16,20},{20,16},{24,28},{28,24},{1,5},{5... | collective-permute-start | bytes 3145736 | tf_op jit(solution)/shard_map/ppermute | solution.py:362
  79.4 41.3 %collective-permute-start.6 = (bf16[2,256,1024]{2,1,0:T(8,128)(2,1)S(1)}, bf16[2,256,1024]{2,1,0:T(8,128)(2,1)S(1)}, u32[]{:S(2)}, u32[]{:S(2)}) collective-permute-start(bf16[2,256,1024]{2,1,0:T(8,128)(2,1)S(1)} %get-tuple-element.52), channel_id=1, source_target_pairs={{8,0},{12,4},{16,24},{20,28},{9,1},{13,5},{17,25},{21,29},{10,2},{... | collective-permute-start | bytes 3145736 | tf_op jit(solution)/shard_map/ppermute | solution.py:362
  101.1 140.3 %all-to-all-start.1 = ((s16[8,2,96,16,128]{4,3,2,1,0:T(8,128)(2,1)}), s16[8,2,96,16,128]{4,3,2,1,0:T(8,128)(2,1)}, u32[]{:S(2)}, u32[]{:S(2)}) async-start(s16[8,2,96,16,128]{4,3,2,1,0:T(8,128)(2,1)} %pack.3), calls=%async_computation.1 | async-start | bytes 12582912 | tf_op jit(solution)/shard_map/all_to_all | solution.py:471
  115.4 5.3 %copy-start.7 = (bf16[2,256,1024]{2,1,0:T(8,128)(2,1)}, bf16[2,256,1024]{2,1,0:T(8,128)(2,1)S(1)}, u32[]{:S(2)}) copy-start(bf16[2,256,1024]{2,1,0:T(8,128)(2,1)S(1)} %collective-permute-done.7.refs_1_) | copy-start | bytes 3145732
  120.7 1.1 copy-start.2
  121.8 57.3 %collective-permute-start.9 = (bf16[2,1024,512]{2,1,0:T(8,128)(2,1)}, bf16[2,1024,512]{2,1,0:T(8,128)(2,1)S(1)}, u32[]{:S(2)}, u32[]{:S(2)}) collective-permute-start(bf16[2,1024,512]{2,1,0:T(8,128)(2,1)} %get-tuple-element.37.refs_1_), channel_id=1, source_target_pairs={{0,2},{1,3},{2,0},{3,1},{4,6},{5,7},{6,4},{7,5},{8,10},{9,11},{10,... | collective-permute-start | bytes 6291464 | tf_op jit(solution)/shard_map/ppermute | solution.py:429
  124.6 54.5 %copy-start.10 = (bf16[2,256,1024]{2,1,0:T(8,128)(2,1)}, bf16[2,256,1024]{2,1,0:T(8,128)(2,1)S(1)}, u32[]{:S(2)}) copy-start(bf16[2,256,1024]{2,1,0:T(8,128)(2,1)S(1)} %broadcast_select_fusion.1.refs_10_) | copy-start | bytes 3145732
  124.6 54.5 %collective-permute-start.8 = (bf16[2,256,1024]{2,1,0:T(8,128)(2,1)S(1)}, bf16[2,256,1024]{2,1,0:T(8,128)(2,1)S(1)}, u32[]{:S(2)}, u32[]{:S(2)}) collective-permute-start(bf16[2,256,1024]{2,1,0:T(8,128)(2,1)S(1)} %broadcast_select_fusion.1.refs_10_), channel_id=1, source_target_pairs={{0,4},{4,0},{8,12},{12,8},{16,20},{20,16},{24,28},{28,24},{1,5},{5... | collective-permute-start | bytes 3145736 | tf_op jit(solution)/shard_map/ppermute | solution.py:362
  179.1 1.0 copy-start.9
  180.1 1.3 copy-start.6
  181.4 7.0 %collective-permute-start.10 = (bf16[2,1024,512]{2,1,0:T(8,128)(2,1)}, bf16[2,1024,512]{2,1,0:T(8,128)(2,1)S(1)}, u32[]{:S(2)}, u32[]{:S(2)}) collective-permute-start(bf16[2,1024,512]{2,1,0:T(8,128)(2,1)} %get-tuple-element.38.refs_0_), channel_id=1, source_target_pairs={{0,1},{1,0},{2,3},{3,2},{4,5},{5,4},{6,7},{7,6},{8,9},{9,8},{10,11... | collective-permute-start | bytes 6291464 | tf_op jit(solution)/shard_map/ppermute | solution.py:429
  181.4 7.5 %collective-permute-start.11 = (bf16[2,1024,512]{2,1,0:T(8,128)(2,1)}, bf16[2,1024,512]{2,1,0:T(8,128)(2,1)}, u32[]{:S(2)}, u32[]{:S(2)}) collective-permute-start(bf16[2,1024,512]{2,1,0:T(8,128)(2,1)} %get-tuple-element.39.refs_1_), channel_id=1, source_target_pairs={{0,1},{1,0},{2,3},{3,2},{4,5},{5,4},{6,7},{7,6},{8,9},{9,8},{10,11... | collective-permute-start | bytes 6291464 | tf_op jit(solution)/shard_map/ppermute | solution.py:429
  188.4 1.3 copy-start.13

commit v7 on v6

--- a/solution.py
+++ b/solution.py
@@ -109,7 +109,7 @@
                 lambda i, s: (jnp.maximum(i - steps, 0), child, 0, 0, 0),
             ),
             scratch_shapes=[
-                pltpu.VMEM((rows * groups, LANES), jnp.int32),
+                pltpu.VMEM(((rows + 8) * groups, LANES), jnp.int32),
                 pltpu.VMEM((rows // steps, LANES), jnp.float32),
             ],
         ),

time: 252 us -> 252 us (level)
  no operation moved by 1% of the time
where the time goes in v7:
time: 252 us; the launch traced here: 251 us
  waiting for transfers between devices  126 us (50%)
  Pallas kernels  59 us (23%)
  starting transfers between devices  33.1 us (13%)
  local copies, waits for them, and re-layouts  17.5 us (7%)
  other arithmetic  15.1 us (6%)
    ppermute x9, waiting for transfers between devices, send(): lax.ppermute(x, 'row', [(z * n + i, to * n + (i + turn) % n) for z, to in...  75.4 us
    all_to_all x1, waiting for transfers between devices, shards(): got = lax.all_to_all(sent, 'row', split_axis=0, concat_axis=0, tiled=True)  33.4 us
    ppermute x9, starting transfers between devices, send(): lax.ppermute(x, 'row', [(z * n + i, to * n + (i + turn) % n) for z, to in...  18.5 us
    pallas_call x1, Pallas kernels, product(): pl.pallas_call(functools.partial(product_kernel, children, steps, len(low...  18.3 us
    pallas_call x2, Pallas kernels, pack(): pl.pallas_call(functools.partial(pack_kernel, groups, steps), out_shape=j...  15.4 us
    all_to_all x1, waiting for transfers between devices, shards(): lax.all_to_all(sent_lower, 'row', split_axis=0, concat_axis=0, tiled=True)  12.7 us
    pallas_call x1, Pallas kernels, unpack(): pl.pallas_call(functools.partial(unpack_kernel, groups, steps), out_shape...  10 us
    pallas_call x1, Pallas kernels, lower_pack(): pl.pallas_call(lower_pack_kernel, out_shape=jax.ShapeDtypeStruct((count,...  9.13 us
  transfers between devices with their start and end apart: 14, of which 9 were waited for; matrix products, arithmetic and copies ran while one was open for 9% of the time, Pallas kernels for 19%

profile of v7, /device:TPU:0, one launch (start us, length us, event | category | flops | bytes accessed | tf_op | source)
XLA Modules:
  0.0 251.4 jit_solution(15078921132374184481)
XLA Ops:
  0.0 1.3 collective-permute-start.1
  1.3 5.6 %collective-permute-start = (bf16[2,256,1024]{2,1,0:T(8,128)(2,1)}, bf16[2,256,1024]{2,1,0:T(8,128)(2,1)S(1)}, u32[]{:S(2)}, u32[]{:S(2)}) collective-permute-start(bf16[2,256,1024]{2,1,0:T(8,128)(2,1)} %refs_4_.1), channel_id=1, source_target_pairs={{0,8},{4,12},{8,16},{12,20},{16,24},{20,28},{1,9},{5,13},{9,17},{1... | collective-permute-start | bytes 3145736 | tf_op jit(solution)/shard_map/ppermute | solution.py:362
  6.9 2.0 collective-permute-start.2
  9.0 0.7 slice.44
  9.7 0.1 copy.75
  9.8 0.1 multiply_reduce_fusion
  9.9 0.1 broadcast_in_dim.38
  10.0 0.6 reshape_squeeze.3.picks
  10.6 4.1 %abs_reduce_fusion = f32[2,1024]{1,0:T(2,128)S(1)} fusion(f32[2,1024,1024]{2,1,0:T(8,128)} %x.9), kind=kLoop, calls=%fused_computation | loop fusion | flops 4192256 | bytes 8396800 | tf_op jit(solution)/shard_map/reduce_max | solution.py:49
  14.7 0.1 fusion.16
  14.8 0.7 iota_compare_fusion
  15.5 1.9 convert_reduce_fusion
  17.4 0.6 reshape.252.slot
  18.1 1.3 stack.61.digits
  19.4 9.1 %lower_pack.1.refs_3_ = bf16[8,2,208,256]{3,2,1,0:T(8,128)(2,1)} custom-call(s32[32]{0:T(128)} %reshape_squeeze.3.picks, bf16[2,1024,512]{2,1,0:T(8,128)(2,1)} %low.1, s32[2,1,1024]{2,1,0:T(1,128)} %reshape.252.slot, bf16[2,16,1024]{2,1,0:T(8,128)(2,1)} %stack.61.digits), custom_call_target="tpu_custom_call" | custom-call | flops 28000000000 | bytes 23100000 | tf_op jit(solution)/shard_map/lower_pack/pallas_call | solution.py:225
  28.5 0.9 slice_convert_fusion.2
  29.4 0.7 reshape.253.refs_4_
  30.1 1.7 collective-permute-done.2.refs_2_
  31.8 1.0 copy-done.11
  32.8 1.4 slice_reduce_fusion
  34.2 0.7 collective-permute-start.3
  35.0 1.3 collective-permute-start.4
  36.3 2.3 broadcast_select_fusion.2.refs_6_
  38.6 1.6 collective-permute-start.5
  40.2 7.7 %pack.2.refs_1_ = s16[8,2,96,16,128]{4,3,2,1,0:T(8,128)(2,1)} custom-call(s32[1536]{0:T(1024)} %get-tuple-element.46.source, f32[2,1024,1024]{2,1,0:T(8,128)} %x.9), custom_call_target="tpu_custom_call" | custom-call | flops 40000000000 | bytes 33000000 | tf_op jit(solution)/shard_map/pack/pallas_call | solution.py:99
  47.9 7.8 %all-to-all-start = ((bf16[8,2,208,256]{3,2,1,0:T(8,128)(2,1)}), bf16[8,2,208,256]{3,2,1,0:T(8,128)(2,1)}, u32[]{:S(2)}, u32[]{:S(2)}) async-start(bf16[8,2,208,256]{3,2,1,0:T(8,128)(2,1)} %get-tuple-element.27), calls=%async_computation | async-start | bytes 3407872 | tf_op jit(solution)/shard_map/all_to_all | solution.py:463
  55.7 15.1 %collective-permute-done.5.refs_2_ = bf16[2,256,1024]{2,1,0:T(8,128)(2,1)S(1)} collective-permute-done((bf16[2,256,1024]{2,1,0:T(8,128)(2,1)}, bf16[2,256,1024]{2,1,0:T(8,128)(2,1)S(1)}, u32[]{:S(2)}, u32[]{:S(2)}) %collective-permute-start.5) | collective-permute-done | bytes 1048608 | tf_op jit(solution)/shard_map/ppermute | solution.py:362
  70.8 0.0 collective-permute-done.3.refs_0_
  70.8 1.7 collective-permute-done.4.refs_1_
  72.6 1.0 copy-done.4
  73.6 1.2 copy-done.1
  74.8 2.8 %select_select_fusion = (bf16[2,256,1024]{2,1,0:T(8,128)(2,1)}, bf16[2,256,1024]{2,1,0:T(8,128)(2,1)S(1)}) fusion(bf16[2,256,1024]{2,1,0:T(8,128)(2,1)} %get-tuple-element.32, bf16[2,256,1024]{2,1,0:T(8,128)(2,1)} %get-tuple-element.33, bf16[2,256,1024]{2,1,0:T(8,128)(2,1)S(1)} %copy-done.1, pred[]{:T(512)S(6)} %eq.61, pred[]{:T(512)S(6)} %eq.60, pred[]{:T(512)S(6)} %eq.59), kind=kLoop, calls=%fused_computation.3 | loop fusion | flops 1572864 | bytes 5242883 | tf_op jit(solution)/shard_map/jit(_where)/select_n | solution.py:375
  77.6 1.8 collective-permute-start.7
  79.4 1.3 collective-permute-start.6
  80.7 7.7 %pack.3 = s16[8,2,96,16,128]{4,3,2,1,0:T(8,128)(2,1)} custom-call(s32[1536]{0:T(1024)} %get-tuple-element.45.source, f32[2,1024,1024]{2,1,0:T(8,128)} %x.9, s16[8,2,96,16,128]{4,3,2,1,0:T(8,128)(2,1)} %get-tuple-element.31.refs_0_), custom_call_target="tpu_custom_call", output_to_operand_aliasing={{}: (2, {})} | custom-call | flops 40000000000 | bytes 33000000 | tf_op jit(solution)/shard_map/pack/pallas_call | solution.py:99
  88.4 12.7 %all-to-all-done.got = bf16[8,2,208,256]{3,2,1,0:T(8,128)(2,1)} async-done(((bf16[8,2,208,256]{3,2,1,0:T(8,128)(2,1)}), bf16[8,2,208,256]{3,2,1,0:T(8,128)(2,1)}, u32[]{:S(2)}, u32[]{:S(2)}) %all-to-all-start) | async-done | bytes 1703968 | tf_op jit(solution)/shard_map/all_to_all | solution.py:463
  101.1 4.7 %all-to-all-start.1 = ((s16[8,2,96,16,128]{4,3,2,1,0:T(8,128)(2,1)}), s16[8,2,96,16,128]{4,3,2,1,0:T(8,128)(2,1)}, u32[]{:S(2)}, u32[]{:S(2)}) async-start(s16[8,2,96,16,128]{4,3,2,1,0:T(8,128)(2,1)} %pack.3), calls=%async_computation.1 | async-start | bytes 12582912 | tf_op jit(solution)/shard_map/all_to_all | solution.py:471
  105.8 0.9 slice_bitcast_fusion
  106.9 0.7 reshape.263.unit
  107.6 0.7 reshape.261.code
  108.3 0.2 fusion
  108.5 0.7 reshape.255.place
  109.2 6.1 %lower_unpack.1 = (bf16[2,1024,512]{2,1,0:T(8,128)(2,1)}, f32[2,1024,128]{2,1,0:T(8,128)}) custom-call(bf16[8,2,208,256]{3,2,1,0:T(8,128)(2,1)} %all-to-all-done.got, s32[2,1,1664]{2,1,0:T(1,128)} %reshape.255.place, f32[2,1,1664]{2,1,0:T(1,128)} %reshape.261.code, f32[2,1,1664]{2,1,0:T(1,128)} %reshape.263.unit), custom_call_target="tpu_custom_call" | custom-call | flops 20000000000 | bytes 16500000 | tf_op jit(solution)/shard_map/lower_unpack/pallas_call | solution.py:278
  115.4 0.0 collective-permute-done.7.refs_1_
  115.4 5.3 %collective-permute-done.6.refs_0_ = bf16[2,256,1024]{2,1,0:T(8,128)(2,1)S(1)} collective-permute-done((bf16[2,256,1024]{2,1,0:T(8,128)(2,1)S(1)}, bf16[2,256,1024]{2,1,0:T(8,128)(2,1)S(1)}, u32[]{:S(2)}, u32[]{:S(2)}) %collective-permute-start.6) | collective-permute-done | bytes 1048608 | tf_op jit(solution)/shard_map/ppermute | solution.py:362
  120.7 1.1 copy-done.2
  121.8 1.5 collective-permute-start.9
  123.3 1.3 broadcast_select_fusion.1.refs_10_
  124.6 2.9 %collective-permute-start.8 = (bf16[2,256,1024]{2,1,0:T(8,128)(2,1)S(1)}, bf16[2,256,1024]{2,1,0:T(8,128)(2,1)S(1)}, u32[]{:S(2)}, u32[]{:S(2)}) collective-permute-start(bf16[2,256,1024]{2,1,0:T(8,128)(2,1)S(1)} %broadcast_select_fusion.1.refs_10_), channel_id=1, source_target_pairs={{0,4},{4,0},{8,12},{12,8},{16,20},{20,16},{24,28},{28,24},{1,5},{5... | collective-permute-start | bytes 3145736 | tf_op jit(solution)/shard_map/ppermute | solution.py:362
  127.5 51.6 %collective-permute-done.8.refs_0_ = bf16[2,256,1024]{2,1,0:T(8,128)(2,1)S(1)} collective-permute-done((bf16[2,256,1024]{2,1,0:T(8,128)(2,1)S(1)}, bf16[2,256,1024]{2,1,0:T(8,128)(2,1)S(1)}, u32[]{:S(2)}, u32[]{:S(2)}) %collective-permute-start.8) | collective-permute-done | bytes 1048608 | tf_op jit(solution)/shard_map/ppermute | solution.py:362
  179.1 1.0 copy-done.9
  180.1 1.3 copy-done.6
  181.4 0.5 collective-permute-start.11
  181.9 0.6 stack.74.starts
  182.5 0.1 sub.34
  182.6 0.1 copy.82
  182.7 0.6 reshape.254.valid
  183.3 0.6 fusion.4.row_at
  183.9 4.5 %collective-permute-done.10.refs_2_ = bf16[2,1024,512]{2,1,0:T(8,128)(2,1)S(1)} collective-permute-done((bf16[2,1024,512]{2,1,0:T(8,128)(2,1)}, bf16[2,1024,512]{2,1,0:T(8,128)(2,1)S(1)}, u32[]{:S(2)}, u32[]{:S(2)}) %collective-permute-start.10) | collective-permute-done | bytes 2097184 | tf_op jit(solution)/shard_map/ppermute | solution.py:429
  188.4 0.5 collective-permute-done.11.refs_3_
  188.9 0.8 copy-done.13
  189.7 18.3 %product.1.before = f32[1024,1024]{1,0:T(8,128)} custom-call(s32[12]{0:T(128)} %stack.74.starts, f32[1024,1024]{1,0:T(8,128)} %front.1, bf16[2,1024,512]{2,1,0:T(8,128)(2,1)} %get-tuple-element.38.refs_0_, bf16[2,1024,512]{2,1,0:T(8,128)(2,1)} %get-tuple-element.39.refs_1_, bf16[2,1024,512]{2,1,0:T(8,128)(2,1)} %copy-done.13, ...), custom_call_target="tpu_custom_call" | custom-call | flops 60000002048 | bytes 49500000 | tf_op jit(solution)/shard_map/product/pallas_call | solution.py:325
  208.0 33.4 %all-to-all-done.1.got = s16[8,2,96,16,128]{4,3,2,1,0:T(8,128)(2,1)} async-done(((s16[8,2,96,16,128]{4,3,2,1,0:T(8,128)(2,1)}), s16[8,2,96,16,128]{4,3,2,1,0:T(8,128)(2,1)}, u32[]{:S(2)}, u32[]{:S(2)}) %all-to-all-start.1) | async-done | bytes 6291488 | tf_op jit(solution)/shard_map/all_to_all | solution.py:471
  241.4 10.0 %unpack.1 = f32[1024,1024]{1,0:T(8,128)} custom-call(s32[3072]{0:T(1024)} %fusion.4.row_at, s32[16]{0:T(128)} %reshape.254.valid, s16[8,2,96,16,128]{4,3,2,1,0:T(8,128)(2,1)} %all-to-all-done.1.got, f32[1024,1024]{1,0:T(8,128)} %product.1.before, f32[2,1024,128]{2,1,0:T(8,128)} %get-tuple-element.44.unit), custom_call_target="tpu_custom_call" | custom-call | flops 44000002048 | bytes 36300000 | tf_op jit(solution)/shard_map/unpack/pallas_call | solution.py:175
  (60 shorter events, 0.4 us)
Async XLA Ops:
  0.0 30.1 %collective-permute-start.1 = (bf16[2,256,1024]{2,1,0:T(8,128)(2,1)}, bf16[2,256,1024]{2,1,0:T(8,128)(2,1)S(1)}, u32[]{:S(2)}, u32[]{:S(2)}) collective-permute-start(bf16[2,256,1024]{2,1,0:T(8,128)(2,1)} %refs_4_.1), channel_id=1, source_target_pairs={{8,0},{12,4},{16,8},{20,12},{24,16},{28,20},{9,1},{13,5},{17,9},{2... | collective-permute-start | bytes 3145736 | tf_op jit(solution)/shard_map/ppermute | solution.py:362
  1.3 28.8 %collective-permute-start = (bf16[2,256,1024]{2,1,0:T(8,128)(2,1)}, bf16[2,256,1024]{2,1,0:T(8,128)(2,1)S(1)}, u32[]{:S(2)}, u32[]{:S(2)}) collective-permute-start(bf16[2,256,1024]{2,1,0:T(8,128)(2,1)} %refs_4_.1), channel_id=1, source_target_pairs={{0,8},{4,12},{8,16},{12,20},{16,24},{20,28},{1,9},{5,13},{9,17},{1... | collective-permute-start | bytes 3145736 | tf_op jit(solution)/shard_map/ppermute | solution.py:362
  6.9 24.9 %collective-permute-start.2 = (bf16[2,256,1024]{2,1,0:T(8,128)(2,1)}, bf16[2,256,1024]{2,1,0:T(8,128)(2,1)S(1)}, u32[]{:S(2)}, u32[]{:S(2)}) collective-permute-start(bf16[2,256,1024]{2,1,0:T(8,128)(2,1)} %refs_4_.1), channel_id=1, source_target_pairs={{0,4},{4,0},{8,12},{12,8},{16,20},{20,16},{24,28},{28,24},{1,5},{5... | collective-permute-start | bytes 3145736 | tf_op jit(solution)/shard_map/ppermute | solution.py:362
  10.6 4.1 %copy-start.12 = (s32[2,1024]{1,0:T(2,128)S(1)}, s32[2,1024]{1,0:T(2,128)}, u32[]{:S(2)}) copy-start(s32[2,1024]{1,0:T(2,128)} %param.10) | copy-start | bytes 24580
  30.1 1.7 copy-start
  30.1 1.7 copy-start.5
  31.8 1.0 copy-start.11
  34.2 36.6 %collective-permute-start.3 = (bf16[2,256,1024]{2,1,0:T(8,128)(2,1)}, bf16[2,256,1024]{2,1,0:T(8,128)(2,1)S(1)}, u32[]{:S(2)}, u32[]{:S(2)}) collective-permute-start(bf16[2,256,1024]{2,1,0:T(8,128)(2,1)} %get-tuple-element.28), channel_id=1, source_target_pairs={{8,16},{12,20},{16,24},{20,28},{9,17},{13,21},{17,25},{21,29},{10,... | collective-permute-start | bytes 3145736 | tf_op jit(solution)/shard_map/ppermute | solution.py:362
  35.0 37.6 %collective-permute-start.4 = (bf16[2,256,1024]{2,1,0:T(8,128)(2,1)}, bf16[2,256,1024]{2,1,0:T(8,128)(2,1)S(1)}, u32[]{:S(2)}, u32[]{:S(2)}) collective-permute-start(bf16[2,256,1024]{2,1,0:T(8,128)(2,1)} %get-tuple-element.29), channel_id=1, source_target_pairs={{8,0},{12,4},{16,8},{20,12},{9,1},{13,5},{17,9},{21,13},{10,2},{14... | collective-permute-start | bytes 3145736 | tf_op jit(solution)/shard_map/ppermute | solution.py:362
  38.6 32.3 %collective-permute-start.5 = (bf16[2,256,1024]{2,1,0:T(8,128)(2,1)}, bf16[2,256,1024]{2,1,0:T(8,128)(2,1)S(1)}, u32[]{:S(2)}, u32[]{:S(2)}) collective-permute-start(bf16[2,256,1024]{2,1,0:T(8,128)(2,1)} %broadcast_select_fusion.2.refs_6_), channel_id=1, source_target_pairs={{0,4},{4,0},{8,12},{12,8},{16,20},{20,16},{24,28},{28,24},{1,5},{5... | collective-permute-start | bytes 3145736 | tf_op jit(solution)/shard_map/ppermute | solution.py:362
  47.9 53.2 %all-to-all-start = ((bf16[8,2,208,256]{3,2,1,0:T(8,128)(2,1)}), bf16[8,2,208,256]{3,2,1,0:T(8,128)(2,1)}, u32[]{:S(2)}, u32[]{:S(2)}) async-start(bf16[8,2,208,256]{3,2,1,0:T(8,128)(2,1)} %get-tuple-element.27), calls=%async_computation | async-start | bytes 3407872 | tf_op jit(solution)/shard_map/all_to_all | solution.py:463
  70.8 1.7 copy-start.8
  70.8 1.7 copy-start.3
  72.6 1.0 copy-start.4
  73.6 1.2 copy-start.1
  77.6 37.8 %collective-permute-start.7 = (bf16[2,256,1024]{2,1,0:T(8,128)(2,1)}, bf16[2,256,1024]{2,1,0:T(8,128)(2,1)S(1)}, u32[]{:S(2)}, u32[]{:S(2)}) collective-permute-start(bf16[2,256,1024]{2,1,0:T(8,128)(2,1)} %get-tuple-element.51.refs_8_), channel_id=1, source_target_pairs={{0,4},{4,0},{8,12},{12,8},{16,20},{20,16},{24,28},{28,24},{1,5},{5... | collective-permute-start | bytes 3145736 | tf_op jit(solution)/shard_map/ppermute | solution.py:362
  79.4 41.3 %collective-permute-start.6 = (bf16[2,256,1024]{2,1,0:T(8,128)(2,1)S(1)}, bf16[2,256,1024]{2,1,0:T(8,128)(2,1)S(1)}, u32[]{:S(2)}, u32[]{:S(2)}) collective-permute-start(bf16[2,256,1024]{2,1,0:T(8,128)(2,1)S(1)} %get-tuple-element.52), channel_id=1, source_target_pairs={{8,0},{12,4},{16,24},{20,28},{9,1},{13,5},{17,25},{21,29},{10,2},{... | collective-permute-start | bytes 3145736 | tf_op jit(solution)/shard_map/ppermute | solution.py:362
  101.1 140.3 %all-to-all-start.1 = ((s16[8,2,96,16,128]{4,3,2,1,0:T(8,128)(2,1)}), s16[8,2,96,16,128]{4,3,2,1,0:T(8,128)(2,1)}, u32[]{:S(2)}, u32[]{:S(2)}) async-start(s16[8,2,96,16,128]{4,3,2,1,0:T(8,128)(2,1)} %pack.3), calls=%async_computation.1 | async-start | bytes 12582912 | tf_op jit(solution)/shard_map/all_to_all | solution.py:471
  115.4 5.3 %copy-start.7 = (bf16[2,256,1024]{2,1,0:T(8,128)(2,1)}, bf16[2,256,1024]{2,1,0:T(8,128)(2,1)S(1)}, u32[]{:S(2)}) copy-start(bf16[2,256,1024]{2,1,0:T(8,128)(2,1)S(1)} %collective-permute-done.7.refs_1_) | copy-start | bytes 3145732
  120.7 1.1 copy-start.2
  121.8 57.3 %collective-permute-start.9 = (bf16[2,1024,512]{2,1,0:T(8,128)(2,1)}, bf16[2,1024,512]{2,1,0:T(8,128)(2,1)S(1)}, u32[]{:S(2)}, u32[]{:S(2)}) collective-permute-start(bf16[2,1024,512]{2,1,0:T(8,128)(2,1)} %get-tuple-element.37.refs_1_), channel_id=1, source_target_pairs={{0,2},{1,3},{2,0},{3,1},{4,6},{5,7},{6,4},{7,5},{8,10},{9,11},{10,... | collective-permute-start | bytes 6291464 | tf_op jit(solution)/shard_map/ppermute | solution.py:429
  124.6 54.5 %copy-start.10 = (bf16[2,256,1024]{2,1,0:T(8,128)(2,1)}, bf16[2,256,1024]{2,1,0:T(8,128)(2,1)S(1)}, u32[]{:S(2)}) copy-start(bf16[2,256,1024]{2,1,0:T(8,128)(2,1)S(1)} %broadcast_select_fusion.1.refs_10_) | copy-start | bytes 3145732
  124.6 54.5 %collective-permute-start.8 = (bf16[2,256,1024]{2,1,0:T(8,128)(2,1)S(1)}, bf16[2,256,1024]{2,1,0:T(8,128)(2,1)S(1)}, u32[]{:S(2)}, u32[]{:S(2)}) collective-permute-start(bf16[2,256,1024]{2,1,0:T(8,128)(2,1)S(1)} %broadcast_select_fusion.1.refs_10_), channel_id=1, source_target_pairs={{0,4},{4,0},{8,12},{12,8},{16,20},{20,16},{24,28},{28,24},{1,5},{5... | collective-permute-start | bytes 3145736 | tf_op jit(solution)/shard_map/ppermute | solution.py:362
  179.1 1.0 copy-start.9
  180.1 1.3 copy-start.6
  181.4 7.0 %collective-permute-start.10 = (bf16[2,1024,512]{2,1,0:T(8,128)(2,1)}, bf16[2,1024,512]{2,1,0:T(8,128)(2,1)S(1)}, u32[]{:S(2)}, u32[]{:S(2)}) collective-permute-start(bf16[2,1024,512]{2,1,0:T(8,128)(2,1)} %get-tuple-element.38.refs_0_), channel_id=1, source_target_pairs={{0,1},{1,0},{2,3},{3,2},{4,5},{5,4},{6,7},{7,6},{8,9},{9,8},{10,11... | collective-permute-start | bytes 6291464 | tf_op jit(solution)/shard_map/ppermute | solution.py:429
  181.4 7.5 %collective-permute-start.11 = (bf16[2,1024,512]{2,1,0:T(8,128)(2,1)}, bf16[2,1024,512]{2,1,0:T(8,128)(2,1)}, u32[]{:S(2)}, u32[]{:S(2)}) collective-permute-start(bf16[2,1024,512]{2,1,0:T(8,128)(2,1)} %get-tuple-element.39.refs_1_), channel_id=1, source_target_pairs={{0,1},{1,0},{2,3},{3,2},{4,5},{5,4},{6,7},{7,6},{8,9},{9,8},{10,11... | collective-permute-start | bytes 6291464 | tf_op jit(solution)/shard_map/ppermute | solution.py:429
  188.4 1.3 copy-start.13

commit v8 on v7

--- a/solution.py
+++ b/solution.py
@@ -120,73 +120,89 @@
     )(source, x, *first)
 
 
-def unpack_kernel(groups, parts, row_at, valid, got, before, unit, out, held):
+def unpack_kernel(groups, pieces, row_at, valid, got, before, unit, out, held, total, units, sems):
     i = pl.program_id(0)
+    steps = pl.num_programs(0)
     children = unit.shape[0]
     per = 16 // groups
     chunk = 16
     tiles = got.shape[2]
-
-    @pl.when(i < parts)
+    inward = [
+        pltpu.make_async_copy(before, total, sems.at[pieces]),
+        pltpu.make_async_copy(unit, units, sems.at[pieces + 1]),
+    ]
+
+    @pl.when(i == 0)
     def _():
-        for c, s in [(c, s) for s in range(got.shape[0]) for c in range(children)]:
-            device = i * got.shape[0] + s
-            number = c * parts * got.shape[0] + device
-            base = number * tiles * per
-
-            def body(k, carry):
-                for t in range(chunk // per):
-                    v = got[s, c, k * (chunk // per) + t].astype(jnp.int32).astype(jnp.float32)
-                    for a in range(per):
-                        row = pl.multiple_of(row_at[base + k * chunk + t * per + a], groups)
-                        held[c, pl.ds(row, groups), :] = v[a * groups : (a + 1) * groups]
+        for copy in inward:
+            copy.start()
+
+    for c, s in [(c, s) for s in range(got.shape[0]) for c in range(children)]:
+        device = i * got.shape[0] + s
+        number = c * steps * got.shape[0] + device
+        base = number * tiles * per
+
+        def body(k, carry):
+            for t in range(chunk // per):
+                v = got[s, c, k * (chunk // per) + t].astype(jnp.int32).astype(jnp.float32)
+                for a in range(per):
+                    row = pl.multiple_of(row_at[base + k * chunk + t * per + a], groups)
+                    held[c, pl.ds(row, groups), :] = v[a * groups : (a + 1) * groups]
+            return carry
+
+        lax.fori_loop(0, (valid[number] + chunk - 1) // chunk, body, 0)
+
+    @pl.when(i == steps - 1)
+    def _():
+        for copy in inward:
+            copy.wait()
+        rows = total.shape[0] // pieces
+        outward = []
+        for piece in range(pieces):
+
+            def body(g, carry):
+                at = pl.multiple_of(piece * rows + g * 8, 8)
+                base = at * groups
+                for j in range(groups):
+                    cols = pl.ds(j * LANES, LANES)
+                    value = total[pl.ds(at, 8), cols]
+                    for c in range(children):
+                        value += held[c, pl.ds(base + j, 8, stride=groups), :] * units[c, pl.ds(at, 8), :]
+                    total[pl.ds(at, 8), cols] = value
                 return carry
 
-            lax.fori_loop(0, (valid[number] + chunk - 1) // chunk, body, 0)
-
-    @pl.when(i >= parts)
-    def _():
-        rows = out.shape[0]
-
-        def body(g, carry):
-            at = pl.multiple_of(g * 8, 8)
-            base = ((i - parts) * rows + at) * groups
-            for j in range(groups):
-                cols = pl.ds(j * LANES, LANES)
-                total = before[pl.ds(at, 8), cols]
-                for c in range(children):
-                    total += held[c, pl.ds(base + j, 8, stride=groups), :] * unit[c, pl.ds(at, 8), :]
-                out[pl.ds(at, 8), cols] = total
-            return carry
-
-        lax.fori_loop(0, rows // 8, body, 0, unroll=2)
+            lax.fori_loop(0, rows // 8, body, 0, unroll=2)
+            here = pl.ds(piece * rows, rows)
+            outward.append(pltpu.make_async_copy(total.at[here], out.at[here], sems.at[piece]))
+            outward[-1].start()
+        for copy in outward:
+            copy.wait()
 
 
 def unpack(got, place, unit, before):
     rows, width = before.shape
     count, children, tiles = got.shape[:3]
     groups = width // LANES
-    steps, out_steps = count // 4, 2
-
-    def block(i, *_):
-        return jnp.maximum(i - steps, 0), 0
-
+    steps, pieces = count // 2, 8
     valid = jnp.sum(place < rows, axis=2, dtype=jnp.int32)
     return pl.pallas_call(
-        functools.partial(unpack_kernel, groups, steps),
+        functools.partial(unpack_kernel, groups, pieces),
         out_shape=jax.ShapeDtypeStruct((rows, width), jnp.float32),
         grid_spec=pltpu.PrefetchScalarGridSpec(
             num_scalar_prefetch=2,
-            grid=(steps + out_steps,),
+            grid=(steps,),
             in_specs=[
-                pl.BlockSpec(
-                    (count // steps, children, tiles, 16, LANES), lambda i, *_: (jnp.minimum(i, steps - 1), 0, 0, 0, 0)
-                ),
-                pl.BlockSpec((rows // out_steps, width), block),
-                pl.BlockSpec((children, rows // out_steps, LANES), lambda i, *_: (0, block(i)[0], 0)),
+                pl.BlockSpec((count // steps, children, tiles, 16, LANES), lambda i, *_: (i, 0, 0, 0, 0)),
+                ANY,
+                ANY,
             ],
-            out_specs=pl.BlockSpec((rows // out_steps, width), block),
-            scratch_shapes=[pltpu.VMEM((children, (rows + 8) * groups, LANES), jnp.float32)],
+            out_specs=ANY,
+            scratch_shapes=[
+                pltpu.VMEM((children, (rows + 8) * groups, LANES), jnp.float32),
+                pltpu.VMEM((rows, width), jnp.float32),
+                pltpu.VMEM(unit.shape, jnp.float32),
+                pltpu.SemaphoreType.DMA((pieces + 2,)),
+            ],
         ),
         compiler_params=pltpu.CompilerParams(vmem_limit_bytes=VMEM_LIMIT),
         cost_estimate=takes(11),

time: 252 us -> 252 us (level)
  transfers between devices with their start and end apart: 14 -> 14, of which waited for: 9 -> 9; matrix products, arithmetic and copies ran while one was open for 9% -> 9% of each run, Pallas kernels for 19% -> 20%
where the time goes in v8:
time: 252 us; the launch traced here: 251 us
  waiting for transfers between devices  126 us (50%)
  Pallas kernels  58.3 us (23%)
  starting transfers between devices  33.1 us (13%)
  local copies, waits for them, and re-layouts  17.5 us (7%)
  other arithmetic  15.1 us (6%)
    ppermute x9, waiting for transfers between devices, send(): lax.ppermute(x, 'row', [(z * n + i, to * n + (i + turn) % n) for z, to in...  75.4 us
    all_to_all x1, waiting for transfers between devices, shards(): got = lax.all_to_all(sent, 'row', split_axis=0, concat_axis=0, tiled=True)  33.4 us
    ppermute x9, starting transfers between devices, send(): lax.ppermute(x, 'row', [(z * n + i, to * n + (i + turn) % n) for z, to in...  18.5 us
    pallas_call x1, Pallas kernels, product(): pl.pallas_call(functools.partial(product_kernel, children, steps, len(low...  18.3 us
    pallas_call x2, Pallas kernels, pack(): pl.pallas_call(functools.partial(pack_kernel, groups, steps), out_shape=j...  15.4 us
    all_to_all x1, waiting for transfers between devices, shards(): lax.all_to_all(sent_lower, 'row', split_axis=0, concat_axis=0, tiled=True)  12.7 us
    pallas_call x1, Pallas kernels, unpack(): pl.pallas_call(functools.partial(unpack_kernel, groups, pieces), out_shap...  9.38 us
    pallas_call x1, Pallas kernels, lower_pack(): pl.pallas_call(lower_pack_kernel, out_shape=jax.ShapeDtypeStruct((count,...  9.13 us
  transfers between devices with their start and end apart: 14, of which 9 were waited for; matrix products, arithmetic and copies ran while one was open for 9% of the time, Pallas kernels for 20%

profile of v8, /device:TPU:0, one launch (start us, length us, event | category | flops | bytes accessed | tf_op | source)
XLA Modules:
  0.0 250.8 jit_solution(11241794553765781774)
XLA Ops:
  0.0 1.3 collective-permute-start.1
  1.3 5.6 %collective-permute-start = (bf16[2,256,1024]{2,1,0:T(8,128)(2,1)}, bf16[2,256,1024]{2,1,0:T(8,128)(2,1)S(1)}, u32[]{:S(2)}, u32[]{:S(2)}) collective-permute-start(bf16[2,256,1024]{2,1,0:T(8,128)(2,1)} %refs_4_.1), channel_id=1, source_target_pairs={{0,8},{4,12},{8,16},{12,20},{16,24},{20,28},{1,9},{5,13},{9,17},{1... | collective-permute-start | bytes 3145736 | tf_op jit(solution)/shard_map/ppermute | solution.py:378
  6.9 2.0 collective-permute-start.2
  9.0 0.7 slice.44
  9.7 0.1 copy.75
  9.8 0.1 multiply_reduce_fusion
  9.9 0.1 broadcast_in_dim.38
  10.0 0.6 reshape_squeeze.3.picks
  10.6 4.1 %abs_reduce_fusion = f32[2,1024]{1,0:T(2,128)S(1)} fusion(f32[2,1024,1024]{2,1,0:T(8,128)} %x.9), kind=kLoop, calls=%fused_computation | loop fusion | flops 4192256 | bytes 8396800 | tf_op jit(solution)/shard_map/reduce_max | solution.py:49
  14.7 0.1 fusion.16
  14.8 0.7 iota_compare_fusion
  15.5 1.9 convert_reduce_fusion
  17.4 0.6 reshape.252.slot
  18.1 1.3 stack.61.digits
  19.4 9.1 %lower_pack.1.refs_3_ = bf16[8,2,208,256]{3,2,1,0:T(8,128)(2,1)} custom-call(s32[32]{0:T(128)} %reshape_squeeze.3.picks, bf16[2,1024,512]{2,1,0:T(8,128)(2,1)} %low.1, s32[2,1,1024]{2,1,0:T(1,128)} %reshape.252.slot, bf16[2,16,1024]{2,1,0:T(8,128)(2,1)} %stack.61.digits), custom_call_target="tpu_custom_call" | custom-call | flops 28000000000 | bytes 23100000 | tf_op jit(solution)/shard_map/lower_pack/pallas_call | solution.py:241
  28.5 0.9 slice_convert_fusion.2
  29.4 0.7 reshape.253.refs_4_
  30.1 1.7 collective-permute-done.2.refs_2_
  31.8 1.0 copy-done.11
  32.8 1.4 slice_reduce_fusion
  34.2 0.7 collective-permute-start.3
  35.0 1.3 collective-permute-start.4
  36.3 2.3 broadcast_select_fusion.2.refs_6_
  38.6 1.6 collective-permute-start.5
  40.2 7.7 %pack.2.refs_1_ = s16[8,2,96,16,128]{4,3,2,1,0:T(8,128)(2,1)} custom-call(s32[1536]{0:T(1024)} %get-tuple-element.46.source, f32[2,1024,1024]{2,1,0:T(8,128)} %x.9), custom_call_target="tpu_custom_call" | custom-call | flops 40000000000 | bytes 33000000 | tf_op jit(solution)/shard_map/pack/pallas_call | solution.py:99
  47.9 7.8 %all-to-all-start = ((bf16[8,2,208,256]{3,2,1,0:T(8,128)(2,1)}), bf16[8,2,208,256]{3,2,1,0:T(8,128)(2,1)}, u32[]{:S(2)}, u32[]{:S(2)}) async-start(bf16[8,2,208,256]{3,2,1,0:T(8,128)(2,1)} %get-tuple-element.27), calls=%async_computation | async-start | bytes 3407872 | tf_op jit(solution)/shard_map/all_to_all | solution.py:479
  55.7 15.1 %collective-permute-done.5.refs_2_ = bf16[2,256,1024]{2,1,0:T(8,128)(2,1)S(1)} collective-permute-done((bf16[2,256,1024]{2,1,0:T(8,128)(2,1)}, bf16[2,256,1024]{2,1,0:T(8,128)(2,1)S(1)}, u32[]{:S(2)}, u32[]{:S(2)}) %collective-permute-start.5) | collective-permute-done | bytes 1048608 | tf_op jit(solution)/shard_map/ppermute | solution.py:378
  70.8 0.0 collective-permute-done.3.refs_0_
  70.8 1.7 collective-permute-done.4.refs_1_
  72.6 1.0 copy-done.4
  73.6 1.2 copy-done.1
  74.8 2.8 %select_select_fusion = (bf16[2,256,1024]{2,1,0:T(8,128)(2,1)}, bf16[2,256,1024]{2,1,0:T(8,128)(2,1)S(1)}) fusion(bf16[2,256,1024]{2,1,0:T(8,128)(2,1)} %get-tuple-element.32, bf16[2,256,1024]{2,1,0:T(8,128)(2,1)} %get-tuple-element.33, bf16[2,256,1024]{2,1,0:T(8,128)(2,1)S(1)} %copy-done.1, pred[]{:T(512)S(6)} %eq.61, pred[]{:T(512)S(6)} %eq.60, pred[]{:T(512)S(6)} %eq.59), kind=kLoop, calls=%fused_computation.3 | loop fusion | flops 1572864 | bytes 5242883 | tf_op jit(solution)/shard_map/jit(_where)/select_n | solution.py:391
  77.6 1.8 collective-permute-start.7
  79.4 1.3 collective-permute-start.6
  80.7 7.7 %pack.3 = s16[8,2,96,16,128]{4,3,2,1,0:T(8,128)(2,1)} custom-call(s32[1536]{0:T(1024)} %get-tuple-element.45.source, f32[2,1024,1024]{2,1,0:T(8,128)} %x.9, s16[8,2,96,16,128]{4,3,2,1,0:T(8,128)(2,1)} %get-tuple-element.31.refs_0_), custom_call_target="tpu_custom_call", output_to_operand_aliasing={{}: (2, {})} | custom-call | flops 40000000000 | bytes 33000000 | tf_op jit(solution)/shard_map/pack/pallas_call | solution.py:99
  88.4 12.7 %all-to-all-done.got = bf16[8,2,208,256]{3,2,1,0:T(8,128)(2,1)} async-done(((bf16[8,2,208,256]{3,2,1,0:T(8,128)(2,1)}), bf16[8,2,208,256]{3,2,1,0:T(8,128)(2,1)}, u32[]{:S(2)}, u32[]{:S(2)}) %all-to-all-start) | async-done | bytes 1703968 | tf_op jit(solution)/shard_map/all_to_all | solution.py:479
  101.1 4.7 %all-to-all-start.1 = ((s16[8,2,96,16,128]{4,3,2,1,0:T(8,128)(2,1)}), s16[8,2,96,16,128]{4,3,2,1,0:T(8,128)(2,1)}, u32[]{:S(2)}, u32[]{:S(2)}) async-start(s16[8,2,96,16,128]{4,3,2,1,0:T(8,128)(2,1)} %pack.3), calls=%async_computation.1 | async-start | bytes 12582912 | tf_op jit(solution)/shard_map/all_to_all | solution.py:487
  105.8 0.9 slice_bitcast_fusion
  106.9 0.7 reshape.263.unit
  107.6 0.7 reshape.261.code
  108.3 0.2 fusion
  108.5 0.7 reshape.255.place
  109.2 6.1 %lower_unpack.1 = (bf16[2,1024,512]{2,1,0:T(8,128)(2,1)}, f32[2,1024,128]{2,1,0:T(8,128)}) custom-call(bf16[8,2,208,256]{3,2,1,0:T(8,128)(2,1)} %all-to-all-done.got, s32[2,1,1664]{2,1,0:T(1,128)} %reshape.255.place, f32[2,1,1664]{2,1,0:T(1,128)} %reshape.261.code, f32[2,1,1664]{2,1,0:T(1,128)} %reshape.263.unit), custom_call_target="tpu_custom_call" | custom-call | flops 20000000000 | bytes 16500000 | tf_op jit(solution)/shard_map/lower_unpack/pallas_call | solution.py:294
  115.4 0.0 collective-permute-done.7.refs_1_
  115.4 5.3 %collective-permute-done.6.refs_0_ = bf16[2,256,1024]{2,1,0:T(8,128)(2,1)S(1)} collective-permute-done((bf16[2,256,1024]{2,1,0:T(8,128)(2,1)S(1)}, bf16[2,256,1024]{2,1,0:T(8,128)(2,1)S(1)}, u32[]{:S(2)}, u32[]{:S(2)}) %collective-permute-start.6) | collective-permute-done | bytes 1048608 | tf_op jit(solution)/shard_map/ppermute | solution.py:378
  120.7 1.1 copy-done.2
  121.8 1.5 collective-permute-start.9
  123.3 1.3 broadcast_select_fusion.1.refs_10_
  124.6 2.9 %collective-permute-start.8 = (bf16[2,256,1024]{2,1,0:T(8,128)(2,1)S(1)}, bf16[2,256,1024]{2,1,0:T(8,128)(2,1)S(1)}, u32[]{:S(2)}, u32[]{:S(2)}) collective-permute-start(bf16[2,256,1024]{2,1,0:T(8,128)(2,1)S(1)} %broadcast_select_fusion.1.refs_10_), channel_id=1, source_target_pairs={{0,4},{4,0},{8,12},{12,8},{16,20},{20,16},{24,28},{28,24},{1,5},{5... | collective-permute-start | bytes 3145736 | tf_op jit(solution)/shard_map/ppermute | solution.py:378
  127.5 51.6 %collective-permute-done.8.refs_0_ = bf16[2,256,1024]{2,1,0:T(8,128)(2,1)S(1)} collective-permute-done((bf16[2,256,1024]{2,1,0:T(8,128)(2,1)S(1)}, bf16[2,256,1024]{2,1,0:T(8,128)(2,1)S(1)}, u32[]{:S(2)}, u32[]{:S(2)}) %collective-permute-start.8) | collective-permute-done | bytes 1048608 | tf_op jit(solution)/shard_map/ppermute | solution.py:378
  179.1 1.0 copy-done.9
  180.1 1.3 copy-done.6
  181.4 0.5 collective-permute-start.11
  181.9 0.6 stack.74.starts
  182.5 0.1 sub.34
  182.6 0.1 copy.82
  182.7 0.6 reshape.254.valid
  183.3 0.6 fusion.4.row_at
  183.9 4.5 %collective-permute-done.10.refs_2_ = bf16[2,1024,512]{2,1,0:T(8,128)(2,1)S(1)} collective-permute-done((bf16[2,1024,512]{2,1,0:T(8,128)(2,1)}, bf16[2,1024,512]{2,1,0:T(8,128)(2,1)S(1)}, u32[]{:S(2)}, u32[]{:S(2)}) %collective-permute-start.10) | collective-permute-done | bytes 2097184 | tf_op jit(solution)/shard_map/ppermute | solution.py:445
  188.4 0.5 collective-permute-done.11.refs_3_
  188.9 0.8 copy-done.13
  189.7 18.3 %product.1.before = f32[1024,1024]{1,0:T(8,128)} custom-call(s32[12]{0:T(128)} %stack.74.starts, f32[1024,1024]{1,0:T(8,128)} %front.1, bf16[2,1024,512]{2,1,0:T(8,128)(2,1)} %get-tuple-element.38.refs_0_, bf16[2,1024,512]{2,1,0:T(8,128)(2,1)} %get-tuple-element.39.refs_1_, bf16[2,1024,512]{2,1,0:T(8,128)(2,1)} %copy-done.13, ...), custom_call_target="tpu_custom_call" | custom-call | flops 60000002048 | bytes 49500000 | tf_op jit(solution)/shard_map/product/pallas_call | solution.py:341
  208.0 33.4 %all-to-all-done.1.got = s16[8,2,96,16,128]{4,3,2,1,0:T(8,128)(2,1)} async-done(((s16[8,2,96,16,128]{4,3,2,1,0:T(8,128)(2,1)}), s16[8,2,96,16,128]{4,3,2,1,0:T(8,128)(2,1)}, u32[]{:S(2)}, u32[]{:S(2)}) %all-to-all-start.1) | async-done | bytes 6291488 | tf_op jit(solution)/shard_map/all_to_all | solution.py:487
  241.4 9.4 %unpack.1 = f32[1024,1024]{1,0:T(8,128)} custom-call(s32[3072]{0:T(1024)} %fusion.4.row_at, s32[16]{0:T(128)} %reshape.254.valid, s16[8,2,96,16,128]{4,3,2,1,0:T(8,128)(2,1)} %all-to-all-done.1.got, f32[1024,1024]{1,0:T(8,128)} %product.1.before, f32[2,1024,128]{2,1,0:T(8,128)} %get-tuple-element.44.unit), custom_call_target="tpu_custom_call" | custom-call | flops 44000002048 | bytes 36300000 | tf_op jit(solution)/shard_map/unpack/pallas_call | solution.py:188
  (60 shorter events, 0.4 us)
Async XLA Ops:
  0.0 30.1 %collective-permute-start.1 = (bf16[2,256,1024]{2,1,0:T(8,128)(2,1)}, bf16[2,256,1024]{2,1,0:T(8,128)(2,1)S(1)}, u32[]{:S(2)}, u32[]{:S(2)}) collective-permute-start(bf16[2,256,1024]{2,1,0:T(8,128)(2,1)} %refs_4_.1), channel_id=1, source_target_pairs={{8,0},{12,4},{16,8},{20,12},{24,16},{28,20},{9,1},{13,5},{17,9},{2... | collective-permute-start | bytes 3145736 | tf_op jit(solution)/shard_map/ppermute | solution.py:378
  1.3 28.8 %collective-permute-start = (bf16[2,256,1024]{2,1,0:T(8,128)(2,1)}, bf16[2,256,1024]{2,1,0:T(8,128)(2,1)S(1)}, u32[]{:S(2)}, u32[]{:S(2)}) collective-permute-start(bf16[2,256,1024]{2,1,0:T(8,128)(2,1)} %refs_4_.1), channel_id=1, source_target_pairs={{0,8},{4,12},{8,16},{12,20},{16,24},{20,28},{1,9},{5,13},{9,17},{1... | collective-permute-start | bytes 3145736 | tf_op jit(solution)/shard_map/ppermute | solution.py:378
  6.9 24.9 %collective-permute-start.2 = (bf16[2,256,1024]{2,1,0:T(8,128)(2,1)}, bf16[2,256,1024]{2,1,0:T(8,128)(2,1)S(1)}, u32[]{:S(2)}, u32[]{:S(2)}) collective-permute-start(bf16[2,256,1024]{2,1,0:T(8,128)(2,1)} %refs_4_.1), channel_id=1, source_target_pairs={{0,4},{4,0},{8,12},{12,8},{16,20},{20,16},{24,28},{28,24},{1,5},{5... | collective-permute-start | bytes 3145736 | tf_op jit(solution)/shard_map/ppermute | solution.py:378
  10.6 4.1 %copy-start.12 = (s32[2,1024]{1,0:T(2,128)S(1)}, s32[2,1024]{1,0:T(2,128)}, u32[]{:S(2)}) copy-start(s32[2,1024]{1,0:T(2,128)} %param.10) | copy-start | bytes 24580
  30.1 1.7 copy-start
  30.1 1.7 copy-start.5
  31.8 1.0 copy-start.11
  34.2 36.6 %collective-permute-start.3 = (bf16[2,256,1024]{2,1,0:T(8,128)(2,1)}, bf16[2,256,1024]{2,1,0:T(8,128)(2,1)S(1)}, u32[]{:S(2)}, u32[]{:S(2)}) collective-permute-start(bf16[2,256,1024]{2,1,0:T(8,128)(2,1)} %get-tuple-element.28), channel_id=1, source_target_pairs={{8,16},{12,20},{16,24},{20,28},{9,17},{13,21},{17,25},{21,29},{10,... | collective-permute-start | bytes 3145736 | tf_op jit(solution)/shard_map/ppermute | solution.py:378
  35.0 37.6 %collective-permute-start.4 = (bf16[2,256,1024]{2,1,0:T(8,128)(2,1)}, bf16[2,256,1024]{2,1,0:T(8,128)(2,1)S(1)}, u32[]{:S(2)}, u32[]{:S(2)}) collective-permute-start(bf16[2,256,1024]{2,1,0:T(8,128)(2,1)} %get-tuple-element.29), channel_id=1, source_target_pairs={{8,0},{12,4},{16,8},{20,12},{9,1},{13,5},{17,9},{21,13},{10,2},{14... | collective-permute-start | bytes 3145736 | tf_op jit(solution)/shard_map/ppermute | solution.py:378
  38.6 32.3 %collective-permute-start.5 = (bf16[2,256,1024]{2,1,0:T(8,128)(2,1)}, bf16[2,256,1024]{2,1,0:T(8,128)(2,1)S(1)}, u32[]{:S(2)}, u32[]{:S(2)}) collective-permute-start(bf16[2,256,1024]{2,1,0:T(8,128)(2,1)} %broadcast_select_fusion.2.refs_6_), channel_id=1, source_target_pairs={{0,4},{4,0},{8,12},{12,8},{16,20},{20,16},{24,28},{28,24},{1,5},{5... | collective-permute-start | bytes 3145736 | tf_op jit(solution)/shard_map/ppermute | solution.py:378
  47.9 53.2 %all-to-all-start = ((bf16[8,2,208,256]{3,2,1,0:T(8,128)(2,1)}), bf16[8,2,208,256]{3,2,1,0:T(8,128)(2,1)}, u32[]{:S(2)}, u32[]{:S(2)}) async-start(bf16[8,2,208,256]{3,2,1,0:T(8,128)(2,1)} %get-tuple-element.27), calls=%async_computation | async-start | bytes 3407872 | tf_op jit(solution)/shard_map/all_to_all | solution.py:479
  70.8 1.7 copy-start.8
  70.8 1.7 copy-start.3
  72.6 1.0 copy-start.4
  73.6 1.2 copy-start.1
  77.6 37.8 %collective-permute-start.7 = (bf16[2,256,1024]{2,1,0:T(8,128)(2,1)}, bf16[2,256,1024]{2,1,0:T(8,128)(2,1)S(1)}, u32[]{:S(2)}, u32[]{:S(2)}) collective-permute-start(bf16[2,256,1024]{2,1,0:T(8,128)(2,1)} %get-tuple-element.51.refs_8_), channel_id=1, source_target_pairs={{0,4},{4,0},{8,12},{12,8},{16,20},{20,16},{24,28},{28,24},{1,5},{5... | collective-permute-start | bytes 3145736 | tf_op jit(solution)/shard_map/ppermute | solution.py:378
  79.4 41.3 %collective-permute-start.6 = (bf16[2,256,1024]{2,1,0:T(8,128)(2,1)S(1)}, bf16[2,256,1024]{2,1,0:T(8,128)(2,1)S(1)}, u32[]{:S(2)}, u32[]{:S(2)}) collective-permute-start(bf16[2,256,1024]{2,1,0:T(8,128)(2,1)S(1)} %get-tuple-element.52), channel_id=1, source_target_pairs={{8,0},{12,4},{16,24},{20,28},{9,1},{13,5},{17,25},{21,29},{10,2},{... | collective-permute-start | bytes 3145736 | tf_op jit(solution)/shard_map/ppermute | solution.py:378
  101.1 140.3 %all-to-all-start.1 = ((s16[8,2,96,16,128]{4,3,2,1,0:T(8,128)(2,1)}), s16[8,2,96,16,128]{4,3,2,1,0:T(8,128)(2,1)}, u32[]{:S(2)}, u32[]{:S(2)}) async-start(s16[8,2,96,16,128]{4,3,2,1,0:T(8,128)(2,1)} %pack.3), calls=%async_computation.1 | async-start | bytes 12582912 | tf_op jit(solution)/shard_map/all_to_all | solution.py:487
  115.4 5.3 %copy-start.7 = (bf16[2,256,1024]{2,1,0:T(8,128)(2,1)}, bf16[2,256,1024]{2,1,0:T(8,128)(2,1)S(1)}, u32[]{:S(2)}) copy-start(bf16[2,256,1024]{2,1,0:T(8,128)(2,1)S(1)} %collective-permute-done.7.refs_1_) | copy-start | bytes 3145732
  120.7 1.1 copy-start.2
  121.8 57.3 %collective-permute-start.9 = (bf16[2,1024,512]{2,1,0:T(8,128)(2,1)}, bf16[2,1024,512]{2,1,0:T(8,128)(2,1)S(1)}, u32[]{:S(2)}, u32[]{:S(2)}) collective-permute-start(bf16[2,1024,512]{2,1,0:T(8,128)(2,1)} %get-tuple-element.37.refs_1_), channel_id=1, source_target_pairs={{0,2},{1,3},{2,0},{3,1},{4,6},{5,7},{6,4},{7,5},{8,10},{9,11},{10,... | collective-permute-start | bytes 6291464 | tf_op jit(solution)/shard_map/ppermute | solution.py:445
  124.6 54.5 %copy-start.10 = (bf16[2,256,1024]{2,1,0:T(8,128)(2,1)}, bf16[2,256,1024]{2,1,0:T(8,128)(2,1)S(1)}, u32[]{:S(2)}) copy-start(bf16[2,256,1024]{2,1,0:T(8,128)(2,1)S(1)} %broadcast_select_fusion.1.refs_10_) | copy-start | bytes 3145732
  124.6 54.5 %collective-permute-start.8 = (bf16[2,256,1024]{2,1,0:T(8,128)(2,1)S(1)}, bf16[2,256,1024]{2,1,0:T(8,128)(2,1)S(1)}, u32[]{:S(2)}, u32[]{:S(2)}) collective-permute-start(bf16[2,256,1024]{2,1,0:T(8,128)(2,1)S(1)} %broadcast_select_fusion.1.refs_10_), channel_id=1, source_target_pairs={{0,4},{4,0},{8,12},{12,8},{16,20},{20,16},{24,28},{28,24},{1,5},{5... | collective-permute-start | bytes 3145736 | tf_op jit(solution)/shard_map/ppermute | solution.py:378
  179.1 1.0 copy-start.9
  180.1 1.3 copy-start.6
  181.4 7.0 %collective-permute-start.10 = (bf16[2,1024,512]{2,1,0:T(8,128)(2,1)}, bf16[2,1024,512]{2,1,0:T(8,128)(2,1)S(1)}, u32[]{:S(2)}, u32[]{:S(2)}) collective-permute-start(bf16[2,1024,512]{2,1,0:T(8,128)(2,1)} %get-tuple-element.38.refs_0_), channel_id=1, source_target_pairs={{0,1},{1,0},{2,3},{3,2},{4,5},{5,4},{6,7},{7,6},{8,9},{9,8},{10,11... | collective-permute-start | bytes 6291464 | tf_op jit(solution)/shard_map/ppermute | solution.py:445
  181.4 7.5 %collective-permute-start.11 = (bf16[2,1024,512]{2,1,0:T(8,128)(2,1)}, bf16[2,1024,512]{2,1,0:T(8,128)(2,1)}, u32[]{:S(2)}, u32[]{:S(2)}) collective-permute-start(bf16[2,1024,512]{2,1,0:T(8,128)(2,1)} %get-tuple-element.39.refs_1_), channel_id=1, source_target_pairs={{0,1},{1,0},{2,3},{3,2},{4,5},{5,4},{6,7},{7,6},{8,9},{9,8},{10,11... | collective-permute-start | bytes 6291464 | tf_op jit(solution)/shard_map/ppermute | solution.py:445
  188.4 1.3 copy-start.13
